TPU v7x, 128 devices: a whole 4x4x4 slice. The times are simulated.
128 devices in a mesh: dp: 32 (over x_lo, z, y), tensor: 4 (over x_hi, core).
Axes of the slice: x: 4 (x_hi: 2, x_lo: 2; x = x_hi * 2 + x_lo), y: 4, z: 4, core: 2. Of those that a mesh axis runs over, the one named last changes fastest.
Arguments:
- token_ids: int32 [4, 256], replicated, may hold values from 0 to 75967
- embed_table: bfloat16 [75968, 4096], P('dp', 'tensor'), may hold values from -6 to 6
- norm_gain: float32 [4096], replicated, may hold values from 0.25 to 1.75
- query_gain: float32 [128], replicated, may hold values from 0.25 to 1.75
- key_gain: float32 [128], replicated, may hold values from 0.25 to 1.75
- base_query_weight: bfloat16 [4096, 4096], P(None, 'tensor'), may hold values from -0.09375 to 0.09375
- pair_weight: bfloat16 [2, 4096, 256], replicated, may hold values from -0.09375 to 0.09375
- past_pairs: bfloat16 [256, 512, 2, 256], P('dp'), may hold values from -96 to 96
- down_factor: float32 [64, 4096], P('dp'), may hold values from -6 to 6
- up_factor: float32 [64, 4096], P('dp', 'tensor'), may hold values from -6 to 6
- grad_down: bfloat16 [32, 64, 4096], P('dp'), may hold values from -200 to 200
- grad_up: bfloat16 [32, 64, 4096], P('dp', None, 'tensor'), may hold values from -200 to 200
- group_scale: float32 [32], replicated, may hold values from 0.25 to 4
- learner_group: int32 [32], replicated, may hold values from 0 to 31, each once
Outputs:
- attended: bfloat16 [4, 256, 4096], P(None, 'dp', 'tensor')
- new_down: float32 [64, 4096], P('dp')
- new_up: float32 [64, 4096], P('dp', 'tensor')
Inputs may be any that keep to these rules, and one draw needn't show every extreme that they name: `learner_group`: each learner processed exactly one rollout group, each group exactly once.
All inputs are finite; a program needn't handle non-finite values.
Results may differ from a plain program's by a relative error of at most 0.012.
The roundings to bfloat16 on the way count: a program that leaves them out, or rounds other values in their place, can miss the bound.
Values may be sent and summed in bfloat16 or wider, within the bound.
No kernel may reach another device: no remote copies, remote signals or barrier semaphores. Data moves between devices by JAX's collectives and lax.ppermute only.
A program may use at most 128 MiB of HBM per device.

v0:
```python
import math

import jax
import jax.numpy as jnp
from jax import lax
from jax.sharding import PartitionSpec as P

D = 4096
HEAD = 128
HEADS = 32
KVH = 2
R = 64
STEPS = 4
HD = 4096


EPSILON = 1e-06
STEP_RATIO = 0.3
ADAPTER_SCALING = 1.0 / 1024.0


def normalize(values, gain):
    return values * lax.rsqrt(jnp.mean(values * values, axis=-1, keepdims=True) + EPSILON) * gain


def lookup(id_block, embed_table):
    vocab_rows = embed_table.shape[0]
    start = lax.axis_index("dp") * vocab_rows
    one_hot = (id_block[..., None] == start + jnp.arange(vocab_rows, dtype=jnp.int32)).astype(
        jnp.bfloat16
    )
    partial_rows = jnp.einsum(
        "kgv,vd->kgd", one_hot, embed_table, preferred_element_type=jnp.float32
    )
    own_rows = lax.psum_scatter(
        partial_rows.astype(jnp.bfloat16), "dp", scatter_dimension=1, tiled=True
    )
    return lax.all_gather(own_rows, "tensor", axis=2, tiled=True)


def clip_factor(sum_down, up_factor_sum):
    down_width = sum_down.shape[1] // lax.axis_size("tensor")
    own_cols = lax.dynamic_slice_in_dim(
        sum_down, lax.axis_index("tensor") * down_width, down_width, 1
    )
    own_square = jnp.sum(own_cols * own_cols) + jnp.sum(up_factor_sum * up_factor_sum)
    overall = lax.psum(own_square, ("dp", "tensor"))
    return 1.0 / jnp.maximum(jnp.sqrt(overall), 1.0)


def body(
    token_ids,
    embed_table,
    norm_gain,
    query_gain,
    key_gain,
    base_query_weight,
    pair_weight,
    past_pairs,
    down_factor,
    up_factor,
    grad_down,
    grad_up,
    group_scale,
    learner_group,
):
    highest = lax.Precision.HIGHEST
    learners = lax.axis_size("dp")
    decode_position = jnp.arange(learners, dtype=jnp.int32)
    chosen = jnp.sum(jnp.where(decode_position == lax.axis_index("dp"), learner_group, 0))
    weight = jnp.sum(jnp.where(decode_position == chosen, group_scale, 0.0))
    term_down = grad_down[0].astype(jnp.float32) * weight
    term_up = grad_up[0].astype(jnp.float32) * weight
    sum_down, up_factor_sum = (
        lax.psum_scatter(term_down, "dp", scatter_dimension=0, tiled=True),
        lax.psum_scatter(term_up, "dp", scatter_dimension=0, tiled=True),
    )
    rate = STEP_RATIO * math.sqrt(R * (D + HD))
    clip_coef = clip_factor(sum_down, up_factor_sum)
    new_down = down_factor - rate * clip_coef * sum_down
    new_up = up_factor - rate * clip_coef * up_factor_sum
    full_down, full_up = (
        lax.all_gather(new_down, "dp", axis=0, tiled=True),
        lax.all_gather(new_up, "dp", axis=0, tiled=True),
    )
    weight_change = lax.dot_general(
        full_down,
        full_up,
        (((0,), (0,)), ((), ())),
        precision=highest,
        preferred_element_type=jnp.float32,
    )
    merged_weight = (
        base_query_weight.astype(jnp.float32) + ADAPTER_SCALING * weight_change
    ).astype(jnp.bfloat16)
    head_count = merged_weight.shape[1] // HEAD
    pair_index = lax.axis_index("tensor") * head_count // (HEADS // KVH)
    own_weight = lax.dynamic_index_in_dim(pair_weight, pair_index, 0, keepdims=False)
    own_cache = lax.dynamic_index_in_dim(past_pairs, pair_index, 2, keepdims=False)
    cached_keys = own_cache[..., :HEAD]
    cached_values = own_cache[..., HEAD:]
    row_count = own_cache.shape[0]
    inverse = 1.0 / math.sqrt(HEAD)
    fresh_keys = []
    fresh_values = []
    outputs = []
    for decode_step in range(STEPS):
        embedded = lookup(token_ids[decode_step : decode_step + 1], embed_table)[0]
        normed = normalize(embedded.astype(jnp.float32), norm_gain).astype(jnp.bfloat16)
        query = jnp.dot(normed, merged_weight, preferred_element_type=jnp.float32).reshape(
            row_count, head_count, HEAD
        )
        query_normed = normalize(query, query_gain).astype(jnp.bfloat16)
        pairs = jnp.dot(normed, own_weight, preferred_element_type=jnp.float32)
        fresh_keys.append(normalize(pairs[:, :HEAD], key_gain).astype(jnp.bfloat16))
        fresh_values.append(pairs[:, HEAD:].astype(jnp.bfloat16))
        new_keys = jnp.stack(fresh_keys, axis=1)
        new_values = jnp.stack(fresh_values, axis=1)
        scores_old = (
            jnp.einsum(
                "rhd,rcd->rhc", query_normed, cached_keys, preferred_element_type=jnp.float32
            )
            * inverse
        )
        scores_new = (
            jnp.einsum("rhd,rcd->rhc", query_normed, new_keys, preferred_element_type=jnp.float32)
            * inverse
        )
        scores = jnp.concatenate([scores_old, scores_new], axis=-1)
        top = jnp.max(scores, axis=-1, keepdims=True)
        expo = jnp.exp(scores - top)
        probs = (expo / jnp.sum(expo, axis=-1, keepdims=True)).astype(jnp.bfloat16)
        ctx_len = cached_keys.shape[1]
        result = jnp.einsum(
            "rhc,rcd->rhd", probs[..., :ctx_len], cached_values, preferred_element_type=jnp.float32
        )
        result = result + jnp.einsum(
            "rhc,rcd->rhd", probs[..., ctx_len:], new_values, preferred_element_type=jnp.float32
        )
        outputs.append(result.astype(jnp.bfloat16).reshape(row_count, head_count * HEAD))
    return (jnp.stack(outputs), new_down, new_up)


def solution(mesh):
    in_specs = (
        P(),
        P("dp", "tensor"),
        P(),
        P(),
        P(),
        P(None, "tensor"),
        P(),
        P("dp", None, None, None),
        P("dp", None),
        P("dp", "tensor"),
        P("dp", None, None),
        P("dp", None, "tensor"),
        P(),
        P(),
    )
    out_specs = (P(None, "dp", "tensor"), P("dp", None), P("dp", "tensor"))
    return jax.shard_map(body, mesh=mesh, in_specs=in_specs, out_specs=out_specs, check_vma=False)
```

profile of v0, /device:TPU:1, one launch (start us, length us, event | category | flops | bytes accessed | tf_op | source)
XLA Modules:
  0.0 1200.0 jit_solution(16868277369607578267)
XLA Ops:
  7.2 0.8 fusion.147
  8.1 4.8 fusion.40
  12.9 4.8 fusion.43
  17.7 4.8 fusion.46
  22.7 4.9 fusion.49
  27.6 0.6 fusion.139
  28.2 1.2 fusion.140
  29.5 1.4 multiply_bitcast_fusion.1
  30.9 1.7 multiply_bitcast_fusion
  32.8 0.6 dynamic-slice
  34.1 11.3 copy.60
  45.4 8.8 constant_dynamic-slice_fusion
  54.2 2.6 copy.142
  56.8 94.0 %reduce-scatter.11.cloned.1.call-done = bf16[1,8,1024]{2,1,0:T(8,128)(2,1)} async-done(((bf16[1,256,1024]{2,1,0:T(8,128)(2,1)}), bf16[1,8,1024]{2,1,0:T(8,128)(2,1)}) %reduce-scatter.11.cloned.1.call-update) | async-done | bytes 16400 | tf_op jit(solution)/shard_map/reduce_scatter | solution.py:35
  150.8 33.0 %all_gather.23 = bf16[1,8,4096]{2,1,0:T(8,128)(2,1)S(1)} all-gather(bf16[1,8,1024]{2,1,0:T(8,128)(2,1)} %reduce-scatter.11.cloned.1.call-done), channel_id=1, replica_groups=mesh['dp'=32,'tensor'=4] {'tensor'}, dimensions={2}, use_global_device_ids=true | all-gather | bytes 81920 | tf_op jit(solution)/shard_map/all_gather | solution.py:38
  184.0 126.0 %reduce-scatter.9.cloned.1.call-done = bf16[1,8,1024]{2,1,0:T(8,128)(2,1)} async-done(((bf16[1,256,1024]{2,1,0:T(8,128)(2,1)}), bf16[1,8,1024]{2,1,0:T(8,128)(2,1)}) %reduce-scatter.9.cloned.1.call-update) | async-done | bytes 16400 | tf_op jit(solution)/shard_map/reduce_scatter | solution.py:35
  309.9 32.9 %all_gather.22 = bf16[1,8,4096]{2,1,0:T(8,128)(2,1)S(1)} all-gather(bf16[1,8,1024]{2,1,0:T(8,128)(2,1)} %reduce-scatter.9.cloned.1.call-done), channel_id=1, replica_groups=mesh['dp'=32,'tensor'=4] {'tensor'}, dimensions={2}, use_global_device_ids=true | all-gather | bytes 81920 | tf_op jit(solution)/shard_map/all_gather | solution.py:38
  343.0 125.7 %reduce-scatter.7.cloned.1.call-done = bf16[1,8,1024]{2,1,0:T(8,128)(2,1)} async-done(((bf16[1,256,1024]{2,1,0:T(8,128)(2,1)}), bf16[1,8,1024]{2,1,0:T(8,128)(2,1)}) %reduce-scatter.7.cloned.1.call-update) | async-done | bytes 16400 | tf_op jit(solution)/shard_map/reduce_scatter | solution.py:35
  468.7 33.0 %all_gather.21 = bf16[1,8,4096]{2,1,0:T(8,128)(2,1)S(1)} all-gather(bf16[1,8,1024]{2,1,0:T(8,128)(2,1)} %reduce-scatter.7.cloned.1.call-done), channel_id=1, replica_groups=mesh['dp'=32,'tensor'=4] {'tensor'}, dimensions={2}, use_global_device_ids=true | all-gather | bytes 81920 | tf_op jit(solution)/shard_map/all_gather | solution.py:38
  501.8 125.6 %reduce-scatter.5.cloned.1.call-done = bf16[1,8,1024]{2,1,0:T(8,128)(2,1)} async-done(((bf16[1,256,1024]{2,1,0:T(8,128)(2,1)}), bf16[1,8,1024]{2,1,0:T(8,128)(2,1)}) %reduce-scatter.5.cloned.1.call-update) | async-done | bytes 16400 | tf_op jit(solution)/shard_map/reduce_scatter | solution.py:35
  627.5 33.1 %all_gather.18 = bf16[1,8,4096]{2,1,0:T(8,128)(2,1)S(1)} all-gather(bf16[1,8,1024]{2,1,0:T(8,128)(2,1)} %reduce-scatter.5.cloned.1.call-done), channel_id=1, replica_groups=mesh['dp'=32,'tensor'=4] {'tensor'}, dimensions={2}, use_global_device_ids=true | all-gather | bytes 81920 | tf_op jit(solution)/shard_map/all_gather | solution.py:38
  660.8 2.0 fusion.14
  663.0 2.0 fusion.8
  666.3 274.0 %all-reduce.5.cloned.1.call-done = (f32[64,4096]{1,0:T(8,128)}, f32[64,1024]{1,0:T(8,128)}) async-done(((f32[64,4096]{1,0:T(8,128)}, f32[64,1024]{1,0:T(8,128)}), (f32[64,4096]{1,0:T(8,128)}, f32[64,1024]{1,0:T(8,128)})) %all-reduce.5.cloned.1.call-update) | async-done | bytes 1310736
  940.3 1.6 multiply_reduce_fusion.4
  943.2 86.6 %psum.7 = f32[]{:T(128)} all-reduce(f32[]{:T(128)S(6)} %add.158), channel_id=1, replica_groups=mesh['dp'=32,'tensor'=4] {'dp','tensor'}, use_global_device_ids=true, to_apply=%region_8.9 | all-reduce | flops 1 | bytes 8 | tf_op jit(solution)/shard_map/psum | solution.py:47
  1030.5 1.5 fusion.103
  1032.1 0.7 fusion.146
  1032.8 0.6 pad_maximum_fusion.5
  1033.4 0.6 fusion.137
  1034.0 0.6 pad_maximum_fusion.6
  1034.6 0.6 pad_maximum_fusion.3
  1035.2 0.6 pad_maximum_fusion.4
  1035.8 0.6 pad_maximum_fusion.1
  1036.4 0.6 pad_maximum_fusion.2
  1037.0 0.8 multiply_subtract_fusion
  1037.8 0.6 copy-done.11
  1038.3 67.1 %all-gather.1 = f32[32,2,1024]{2,1,0:T(2,128)S(1)} all-gather(f32[1,2,1024]{2,1,0:T(2,128)S(1)} %bitcast.111), channel_id=1, replica_groups=mesh['dp'=32,'tensor'=4] {'dp'}, dimensions={0}, use_global_device_ids=true | all-gather | bytes 270336 | tf_op jit(solution)/shard_map/all_gather | solution.py:84
  1105.6 53.6 %all-gather.4.cloned.1.call-done = f32[32,2,4096]{2,1,0:T(2,128)} async-done(((f32[1,2,4096]{2,1,0:T(2,128)}), f32[32,2,4096]{2,1,0:T(2,128)}) %all-gather.4.cloned.1.call-update) | async-done | bytes 1048592 | tf_op jit(solution)/shard_map/all_gather | solution.py:83
  1159.2 1.9 reshape.373
  1161.1 16.1 %add_convert_fusion = bf16[4096,1024]{0,1:T(8,128)(2,1)S(1)} fusion(bf16[4096,1024]{0,1:T(8,128)(2,1)} %copy.60, f32[64,4096]{1,0:T(8,128)S(1)} %reshape.373, f32[64,1024]{1,0:T(8,128)S(1)} %reshape.375), kind=kOutput, calls=%fused_computation | convolution fusion | flops 3238002688 | bytes 18087936 | tf_op jit(solution)/shard_map/dot_general | solution.py:86
  1177.2 2.3 multiply_reduce_fusion
  1179.6 2.3 multiply_reduce_fusion.1
  1182.0 2.3 multiply_reduce_fusion.2
  1184.4 2.3 multiply_reduce_fusion.3
  1187.1 0.5 fusion.154
  1188.4 0.5 fusion.152
  1192.5 0.6 pad_maximum_fusion
  (134 shorter events, 7.5 us)
Async XLA Ops:
  7.2 143.6 %reduce-scatter.11.cloned.1.call-start = ((), (), s32[]{:S(2)}) async-start(), calls=%async_computation.7 | async-start | bytes 540672 | tf_op jit(solution)/shard_map/reduce_scatter | solution.py:35
  12.9 297.1 %reduce-scatter.9.cloned.1.call-start = ((), (), s32[]{:S(2)}) async-start(), calls=%async_computation.6 | async-start | bytes 540672 | tf_op jit(solution)/shard_map/reduce_scatter | solution.py:35
  17.7 451.0 %reduce-scatter.7.cloned.1.call-start = ((), (), s32[]{:S(2)}) async-start(), calls=%async_computation.5 | async-start | bytes 540672 | tf_op jit(solution)/shard_map/reduce_scatter | solution.py:35
  22.6 604.9 %reduce-scatter.5.cloned.1.call-start = ((), (), s32[]{:S(2)}) async-start(), calls=%async_computation.4 | async-start | bytes 540672 | tf_op jit(solution)/shard_map/reduce_scatter | solution.py:35
  22.6 5.0 copy-start.29
  22.6 5.6 copy-start.30
  22.6 6.9 copy-start.7
  22.6 8.2 copy-start.6
  22.7 10.2 copy-start.31
  27.5 912.8 %all-reduce.5.cloned.1.call-start = ((), (), s32[]{:S(2)}) async-start(), calls=%async_computation.9 | async-start | bytes 2621440
  32.6 1126.6 %all-gather.4.cloned.1.call-start = ((), (), s32[]{:S(2)}) async-start(), calls=%async_computation.8 | async-start | bytes 1081344 | tf_op jit(solution)/shard_map/all_gather | solution.py:83
  54.2 606.6 %copy-start.1 = (f32[4096]{0:T(1024)S(1)}, f32[4096]{0:T(1024)}, u32[]{:S(2)}) copy-start(f32[4096]{0:T(1024)} %param.16) | copy-start | bytes 49156
  183.9 481.0 %copy-start.19 = (f32[8]{0:T(128)}, f32[8]{0:T(128)S(1)}, u32[]{:S(2)}) copy-start(f32[8]{0:T(128)S(1)} %add_rsqrt_fusion.5) | copy-start | bytes 100
  342.9 322.7 %copy-start.21 = (f32[8]{0:T(128)}, f32[8]{0:T(128)S(1)}, u32[]{:S(2)}) copy-start(f32[8]{0:T(128)S(1)} %add_rsqrt_fusion.7) | copy-start | bytes 100
  501.7 164.4 %copy-start.2 = (bf16[1,8,4096]{2,1,0:T(8,128)(2,1)}, bf16[1,8,4096]{2,1,0:T(8,128)(2,1)S(1)}, u32[]{:S(2)}) copy-start(bf16[1,8,4096]{2,1,0:T(8,128)(2,1)S(1)} %all_gather.21) | copy-start | bytes 196612
  627.5 37.6 %copy-start = (bf16[2,4096,256]{2,1,0:T(8,128)(2,1)S(1)}, bf16[2,4096,256]{2,1,0:T(8,128)(2,1)}, u32[]{:S(2)}) copy-start(bf16[2,4096,256]{2,1,0:T(8,128)(2,1)} %param.20) | copy-start | bytes 12582916
  660.6 5.5 copy-start.4
  660.8 4.2 copy-start.23
  660.8 369.7 %copy-start.10 = (f32[2,4096]{1,0:T(2,128)S(1)}, f32[2,4096]{1,0:T(2,128)}, u32[]{:S(2)}) copy-start(f32[2,4096]{1,0:T(2,128)} %param.22) | copy-start | bytes 98308
  660.8 371.3 %copy-start.27 = (f32[128]{0:T(128)S(1)}, f32[128]{0:T(128)}, u32[]{:S(2)}) copy-start(f32[128]{0:T(128)} %param.18) | copy-start | bytes 1540
  660.8 376.2 %copy-start.16 = (f32[2,1024]{1,0:T(2,128)S(1)}, f32[2,1024]{1,0:T(2,128)}, u32[]{:S(2)}) copy-start(f32[2,1024]{1,0:T(2,128)} %param.23) | copy-start | bytes 24580
  665.7 372.1 %copy-start.25 = (f32[8]{0:T(128)}, f32[8]{0:T(128)S(1)}, u32[]{:S(2)}) copy-start(f32[8]{0:T(128)S(1)} %add_rsqrt_fusion.9) | copy-start | bytes 100
  1037.7 0.6 copy-start.11
  1161.1 16.1 %copy-start.20 = (f32[8]{0:T(128)S(1)}, f32[8]{0:T(128)}, u32[]{:S(2)}) copy-start(f32[8]{0:T(128)} %copy-done.19) | copy-start | bytes 100
  1177.2 2.3 copy-start.22
  1179.6 2.4 copy-start.3
  1179.6 2.4 copy-start.26
  1182.0 2.4 copy-start.5
  1182.0 2.4 copy-start.24
  1184.4 2.5 copy-start.28
  1184.4 2.6 copy-start.18
  1184.4 3.7 copy-start.17
  1186.7 2.1 copy-start.14
  1186.7 2.8 copy-start.15
  1186.8 3.4 copy-start.9
  1187.1 3.9 copy-start.8
  1188.0 3.6 copy-start.13
  1188.4 4.0 copy-start.12
Sparse Core Ops, SparseCore 0:
  13.0 137.7 reduce-scatter.10
  153.2 156.6 reduce-scatter.8
  312.3 156.3 reduce-scatter.6
  471.0 156.4 reduce-scatter.4
  629.9 310.3 all-reduce.4
  1032.2 126.9 all-gather.3
where the time goes:
time: 1220 us; the launch traced here: 1200 us
  waiting for transfers between devices  799 us (65%)
  blocking collectives  286 us (23%)
  matrix products  53.4 us (4%)
  local copies, waits for them, and re-layouts  27.2 us (2%)
  between operations  17.4 us (1%)
  other arithmetic  16.8 us (1%)
    reduce_scatter x4, waiting for transfers between devices, lookup(): lax.psum_scatter(partial_rows.astype(jnp.bfloat16), 'dp', scatter_dimensi...  471 us
    unnamed x7, waiting for transfers between devices  274 us
    all_gather x4, blocking collectives, lookup(): return lax.all_gather(own_rows, 'tensor', axis=2, tiled=True)  132 us
    psum x1, blocking collectives, clip_factor(): overall = lax.psum(own_square, ('dp', 'tensor'))  86.6 us
    all_gather x1, blocking collectives, body(): lax.all_gather(new_up, 'dp', axis=0, tiled=True)  67.1 us
    all_gather x1, waiting for transfers between devices, body(): lax.all_gather(new_down, 'dp', axis=0, tiled=True)  53.6 us
  transfers between devices with their start and end apart: 6, of which 6 were waited for; matrix products, arithmetic and copies ran while one was open for 5% of the time, Pallas kernels for 0%

commit v1 on v0

v1 whole, which is shorter than its diff:
```python
import functools
import math

import jax
import jax.numpy as jnp
from jax import lax
from jax.experimental import pallas as pl
from jax.experimental.pallas import tpu as pltpu
from jax.sharding import PartitionSpec as P

D = 4096
HEAD = 128
HEADS = 32
KVH = 2
R = 64
STEPS = 4
HD = 4096
CAP = 8

EPSILON = 1e-06
STEP_RATIO = 0.3
ADAPTER_SCALING = 1.0 / 1024.0
RATE = STEP_RATIO * math.sqrt(R * (D + HD))
VMEM_LIMIT = 48 * 1024 * 1024


def split(values):
    high = values.astype(jnp.bfloat16)
    return high, (values - high.astype(jnp.float32)).astype(jnp.bfloat16)


def dot_nt(a, b):
    return lax.dot_general(a, b, (((1,), (1,)), ((), ())), preferred_element_type=jnp.float32)


def dot_nn(a, b):
    return lax.dot_general(a, b, (((1,), (0,)), ((), ())), preferred_element_type=jnp.float32)


def plan_tokens(token_ids, groups, vocab_rows):
    steps, rows = token_ids.shape
    ids = token_ids.reshape(steps, groups, rows // groups).transpose(1, 0, 2)
    ids = ids.reshape(groups, steps * (rows // groups))
    count = ids.shape[1]
    earlier = jnp.arange(count)[None, :] < jnp.arange(count)[:, None]
    one, other = ids[:, :, None], ids[:, None, :]
    repeated = jnp.any((one == other) & earlier[None], axis=2)
    low = ids // vocab_rows * vocab_rows
    before = (other >= low[:, :, None]) & (other < one) & ~repeated[:, None, :]
    slot = jnp.sum(before.astype(jnp.int32), axis=2)
    return ids, slot


def own_rows(ids, slot, first_slot, embed_table):
    vocab_rows = embed_table.shape[0]
    local = ids - lax.axis_index("dp") * vocab_rows
    mine = (local >= 0) & (local < vocab_rows)
    wanted = slot[:, None, :] == first_slot + jnp.arange(CAP)[None, :, None]
    chosen = jnp.max(jnp.where(wanted & mine[:, None, :], local[:, None, :], -1), axis=2)
    one_hot = (chosen.reshape(-1, 1) == jnp.arange(vocab_rows)[None, :]).astype(jnp.bfloat16)
    found = dot_nn(one_hot, embed_table).astype(jnp.bfloat16)
    return found.reshape(ids.shape[0], CAP, -1)


def pick_rows(ids, slot, first_slot, vocab_rows, received):
    me = lax.axis_index("dp")
    own_ids = lax.dynamic_index_in_dim(ids, me, 0, keepdims=False)
    own_slot = lax.dynamic_index_in_dim(slot, me, 0, keepdims=False) - first_slot
    place = own_ids // vocab_rows * CAP + own_slot
    place = jnp.where((own_slot >= 0) & (own_slot < CAP), place, -1)
    columns = received.shape[0] * CAP
    one_hot = (place[:, None] == jnp.arange(columns)[None, :]).astype(jnp.bfloat16)
    return dot_nn(one_hot, received.reshape(columns, -1)).astype(jnp.bfloat16)


def project_kernel(place, e0, e1, e2, e3, gain, factors, normed, partial):
    t = place[0]
    blocks = [e[...].astype(jnp.float32) for e in (e0, e1, e2, e3)]
    square = sum(jnp.sum(b * b, axis=1, keepdims=True) for b in blocks)
    scale = lax.rsqrt(square / D + EPSILON)
    width = blocks[0].shape[1]
    own = None
    for k, block in enumerate(blocks):
        columns = pl.ds(pl.multiple_of((t ^ k) * width, width), width)
        value = (block * scale * gain[:, columns]).astype(jnp.bfloat16)
        normed[:, columns] = value
        own = value if k == 0 else own
    rows = factors[...].reshape(-1, width)
    high, low = split(rows)
    rows_at = lax.broadcasted_iota(jnp.int32, rows.shape, 0) % 8
    total = jnp.sum(jnp.where(rows_at < 4, rows * rows, 0.0))
    count = own.shape[0]
    partial[:count, :] = dot_nt(own, high) + dot_nt(own, low)
    partial[count:, :] = jnp.full((8, rows.shape[0]), total, jnp.float32)


def base_kernel(place, normed, base, pair, gain, query, key_new, value_new, pairs):
    step = pl.program_id(0)

    @pl.when(step == 0)
    def _():
        query[...] = jnp.zeros_like(query)
        pairs[...] = jnp.zeros_like(pairs)

    query[...] += dot_nn(normed[...], base[...])
    pairs[...] += dot_nn(normed[...], pair[0])

    @pl.when(step == pl.num_programs(0) - 1)
    def _():
        keys = pairs[:, :HEAD]
        scale = lax.rsqrt(jnp.mean(keys * keys, axis=1, keepdims=True) + EPSILON)
        key_new[...] = (keys * scale * gain[...]).astype(jnp.bfloat16)
        value_new[...] = pairs[:, HEAD:].astype(jnp.bfloat16)


def attend_kernel(
    place, base_query, products, factors, gain, key_new, value_new, cache, out, queries, results
):
    row = pl.program_id(0)
    row_count = pl.num_programs(0)
    pair_index = place[1]
    count, width = base_query.shape
    heads = width // HEAD
    per_row = count // 8 * heads

    @pl.when(row == 0)
    def _():
        sums = products[:count, :]
        overall = products[count : count + 1, :]
        clip = RATE / jnp.maximum(jnp.sqrt(overall), 1.0)
        lane = lax.broadcasted_iota(jnp.int32, sums.shape, 1) % 8
        updated = sums - clip * pltpu.roll(sums, 4, 1)
        updated = jnp.where((lane == 4) | (lane == 5), updated, 0.0)
        lanes = updated.shape[1]
        spread = pltpu.roll(updated, 2, 1) - clip * pltpu.roll(updated, lanes - 2, 1)
        rows = factors[...].reshape(-1, width)
        high, low = split(rows)
        left_high, left_low = split(spread)
        change = dot_nn(left_high, high) + dot_nn(left_low, high) + dot_nn(left_high, low)
        query = base_query[...] + ADAPTER_SCALING * change
        for h in range(heads):
            part = query[:, h * HEAD : (h + 1) * HEAD]
            scale = lax.rsqrt(jnp.mean(part * part, axis=1, keepdims=True) + EPSILON)
            part = (part * scale * gain[...]).astype(jnp.bfloat16).astype(jnp.float32)
            for s in range(count // 8):
                queries[pl.ds(s * heads + h, 8, stride=per_row), :] = part[s * 8 : s * 8 + 8]

    own = pl.ds(pl.multiple_of(row * per_row, per_row), per_row)
    query = queries[own, :].astype(jnp.bfloat16)
    inverse = 1.0 / math.sqrt(HEAD)
    pairs = cache[0]
    old = dot_nt(query, pairs) * inverse
    lane = lax.broadcasted_iota(jnp.int32, old.shape, 1) % 4
    old = jnp.where(lane == pair_index, old, -jnp.inf)
    new = dot_nt(query, key_new[...]) * inverse
    new_lane = lax.broadcasted_iota(jnp.int32, new.shape, 1)
    step = lax.broadcasted_iota(jnp.int32, new.shape, 0) // heads
    new = jnp.where((new_lane % 8 == row) & (new_lane // 8 <= step), new, -jnp.inf)
    top = jnp.maximum(jnp.max(old, axis=1, keepdims=True), jnp.max(new, axis=1, keepdims=True))
    old, new = jnp.exp(old - top), jnp.exp(new - top)
    total = jnp.sum(old, axis=1, keepdims=True) + jnp.sum(new, axis=1, keepdims=True)
    old = pltpu.roll(old / total, 2, 1).astype(jnp.bfloat16)
    new = (new / total).astype(jnp.bfloat16)
    results[own, :] = dot_nn(old, pairs) + dot_nn(new, value_new[...])

    @pl.when(row == row_count - 1)
    def _():
        for h in range(heads):
            parts = [
                results[pl.ds(s * heads + h, 8, stride=per_row), :] for s in range(count // 8)
            ]
            out[:, h * HEAD : (h + 1) * HEAD] = jnp.concatenate(parts, 0).astype(jnp.bfloat16)


def vmem():
    return pl.BlockSpec(memory_space=pltpu.VMEM)


def smem():
    return pl.BlockSpec(memory_space=pltpu.SMEM)


def project(place, blocks, gain, factors):
    count, width = blocks[0].shape
    return pl.pallas_call(
        project_kernel,
        out_shape=(
            jax.ShapeDtypeStruct((count, 4 * width), jnp.bfloat16),
            jax.ShapeDtypeStruct((count + 8, factors.shape[0] * factors.shape[1]), jnp.float32),
        ),
        in_specs=[smem()] + [vmem()] * 6,
        out_specs=(vmem(), vmem()),
        compiler_params=pltpu.CompilerParams(vmem_limit_bytes=VMEM_LIMIT),
        name="project",
    )(place, *blocks, gain.reshape(1, -1), factors)


def base_products(place, normed, base, pair, gain):
    count, depth = normed.shape
    width = base.shape[1]
    tile = 512
    spec = pltpu.PrefetchScalarGridSpec(
        num_scalar_prefetch=1,
        grid=(depth // tile,),
        in_specs=[
            pl.BlockSpec((count, tile), lambda i, place: (0, i)),
            pl.BlockSpec((tile, width), lambda i, place: (i, 0)),
            pl.BlockSpec((1, tile, 2 * HEAD), lambda i, place: (place[1], i, 0)),
            pl.BlockSpec((1, HEAD), lambda i, place: (0, 0)),
        ],
        out_specs=(
            pl.BlockSpec((count, width), lambda i, place: (0, 0)),
            pl.BlockSpec((count, HEAD), lambda i, place: (0, 0)),
            pl.BlockSpec((count, HEAD), lambda i, place: (0, 0)),
        ),
        scratch_shapes=[pltpu.VMEM((count, 2 * HEAD), jnp.float32)],
    )
    return pl.pallas_call(
        base_kernel,
        out_shape=(
            jax.ShapeDtypeStruct((count, width), jnp.float32),
            jax.ShapeDtypeStruct((count, HEAD), jnp.bfloat16),
            jax.ShapeDtypeStruct((count, HEAD), jnp.bfloat16),
        ),
        grid_spec=spec,
        compiler_params=pltpu.CompilerParams(vmem_limit_bytes=VMEM_LIMIT),
        cost_estimate=pl.CostEstimate(
            flops=2 * count * depth * width, bytes_accessed=2 * depth * width, transcendentals=0
        ),
        name="base_products",
    )(place, normed, base, pair, gain.reshape(1, -1))


def attend(place, base_query, products, factors, gain, key_new, value_new, cache):
    count, width = base_query.shape
    rows, entries, _ = cache.shape

    def whole(x):
        return pl.BlockSpec(x.shape, lambda i, place: (0,) * x.ndim)

    gain = gain.reshape(1, -1)
    spec = pltpu.PrefetchScalarGridSpec(
        num_scalar_prefetch=1,
        grid=(rows,),
        in_specs=[
            whole(base_query),
            whole(products),
            whole(factors),
            whole(gain),
            whole(key_new),
            whole(value_new),
            pl.BlockSpec((1, entries, HEAD), lambda i, place: (i, 0, 0)),
        ],
        out_specs=pl.BlockSpec((count, width), lambda i, place: (0, 0)),
        scratch_shapes=[
            pltpu.VMEM((count * width // HEAD, HEAD), jnp.float32),
            pltpu.VMEM((count * width // HEAD, HEAD), jnp.float32),
        ],
    )
    return pl.pallas_call(
        attend_kernel,
        out_shape=jax.ShapeDtypeStruct((count, width), jnp.bfloat16),
        grid_spec=spec,
        compiler_params=pltpu.CompilerParams(vmem_limit_bytes=VMEM_LIMIT),
        name="attend",
    )(place, base_query, products, factors, gain, key_new, value_new, cache)


def tensor_swap(values, bit):
    size = lax.axis_size("tensor")
    return lax.ppermute(values, "tensor", [(i, i ^ bit) for i in range(size)])


def body(
    token_ids,
    embed_table,
    norm_gain,
    query_gain,
    key_gain,
    base_query_weight,
    pair_weight,
    past_pairs,
    down_factor,
    up_factor,
    grad_down,
    grad_up,
    group_scale,
    learner_group,
):
    groups = lax.axis_size("dp")
    t = lax.axis_index("tensor")
    vocab_rows, width = embed_table.shape
    own_rank = down_factor.shape[0]
    pair_index = t * (width // HEAD) // (HEADS // KVH)
    place = jnp.stack([t, pair_index]).astype(jnp.int32)

    ids, slot = plan_tokens(token_ids, groups, vocab_rows)
    rounds = jnp.max(slot) // CAP + 1
    found = own_rows(ids, slot, 0, embed_table)

    own_down = lax.dynamic_slice_in_dim(grad_down[0], t * width, width, 1)
    half = width // 2

    def fold(rows):
        return rows.reshape(groups, own_rank * 2, half)

    sent = jnp.concatenate(
        [found, jnp.concatenate([fold(own_down), fold(grad_up[0])], axis=1)], axis=2
    )
    got = lax.all_to_all(sent, "dp", 0, 0, tiled=True)

    embedded = pick_rows(ids, slot, 0, vocab_rows, got[:, :, :width])

    def later_round(state):
        r, rows = state
        again = own_rows(ids, slot, r * CAP, embed_table)
        again = lax.all_to_all(again, "dp", 0, 0, tiled=True)
        return r + 1, rows + pick_rows(ids, slot, r * CAP, vocab_rows, again)

    _, embedded = lax.while_loop(lambda s: s[0] < rounds, later_round, (1, embedded))

    position = jnp.arange(groups, dtype=jnp.int32)
    chosen = learner_group[:, None] == position[None, :]
    weight = jnp.sum(jnp.where(chosen, group_scale[None, :], 0.0), axis=1)
    sums = jnp.sum(got[:, :, width:].astype(jnp.float32) * weight[:, None, None], axis=0)
    sums = sums.reshape(2 * own_rank, width)
    sum_down, sum_up = sums[:own_rank], sums[own_rank:]

    blocks = [embedded] + [tensor_swap(embedded, bit) for bit in (1, 2, 3)]
    own_factor = lax.dynamic_slice_in_dim(down_factor, t * width, width, 1)
    rows = jnp.concatenate([sums, own_factor, up_factor], axis=0)
    factors = lax.all_to_all(
        jnp.broadcast_to(rows[None], (groups,) + rows.shape), "dp", 0, 0, tiled=True
    )

    normed, products = project(place, blocks, norm_gain, factors)
    lanes = products.shape[1]
    count = products.shape[0]
    own_sum = sum_down.reshape(-1, lanes)
    other = tensor_swap(jnp.concatenate([products, own_sum], axis=0), 1)
    both = products + other[:count]
    other_sum = other[count:]
    is_odd = (t % 2) == 1
    pair_sum = jnp.stack(
        [jnp.where(is_odd, other_sum, own_sum), jnp.where(is_odd, own_sum, other_sum)]
    )
    far = tensor_swap(jnp.concatenate([both, pair_sum.reshape(-1, lanes)], axis=0), 2)
    products = both + far[:count]
    far_sum = far[count:].reshape(pair_sum.shape)
    is_high = t >= 2
    all_sum = jnp.concatenate(
        [jnp.where(is_high, far_sum, pair_sum), jnp.where(is_high, pair_sum, far_sum)]
    )
    full_down = all_sum.reshape(4, own_rank, width).transpose(1, 0, 2).reshape(own_rank, -1)

    query, key_new, value_new = base_products(
        place, normed, base_query_weight, pair_weight, key_gain
    )
    rows_here, context = past_pairs.shape[:2]
    cache = past_pairs.reshape(rows_here, context, KVH, 2, HEAD).transpose(0, 1, 3, 2, 4)
    cache = cache.reshape(rows_here, context * KVH * 2, HEAD)
    attended = attend(place, query, products, factors, query_gain, key_new, value_new, cache)

    clip_coef = 1.0 / jnp.maximum(jnp.sqrt(products[count - 8, 0]), 1.0)
    new_down = down_factor - RATE * clip_coef * full_down
    new_up = up_factor - RATE * clip_coef * sum_up
    return attended.reshape(STEPS, rows_here, width), new_down, new_up


def solution(mesh):
    in_specs = (
        P(),
        P("dp", "tensor"),
        P(),
        P(),
        P(),
        P(None, "tensor"),
        P(),
        P("dp", None, None, None),
        P("dp", None),
        P("dp", "tensor"),
        P("dp", None, None),
        P("dp", None, "tensor"),
        P(),
        P(),
    )
    out_specs = (P(None, "dp", "tensor"), P("dp", None), P("dp", "tensor"))
    return jax.shard_map(body, mesh=mesh, in_specs=in_specs, out_specs=out_specs, check_vma=False)
```

time: 1220 us -> 88 us (0.07); the launches traced: 1200 us -> 87.3 us
  waiting for transfers between devices: 799 us -> 23.9 us
  blocking collectives: 286 us -> 0 us
  matrix products: 53.4 us -> 4.2 us
  starting transfers between devices: 0.43 us -> 23.6 us
  local copies, waits for them, and re-layouts: 27.2 us -> 8.52 us
  Pallas kernels: 0 us -> 16.6 us
  between operations: 17.4 us -> 4.33 us
    reduce_scatter x4 -> x0, waiting for transfers between devices: 471 us -> none  [lookup(): lax.psum_scatter(partial_rows.astype(jnp.bfloat16), 'dp', scatter_dimensi...]
    unnamed x7 -> x0, waiting for transfers between devices: 274 us -> none
    all_gather x5 -> x0, blocking collectives: 199 us -> none  [the longest x4 132 us: lookup(): return lax.all_gather(own_rows, 'tensor', axis=2, tiled=True)]
    psum x1 -> x0, blocking collectives: 86.6 us -> none  [clip_factor(): overall = lax.psum(own_square, ('dp', 'tensor'))]
    all_gather x1 -> x0, waiting for transfers between devices: 53.6 us -> none  [body(): lax.all_gather(new_down, 'dp', axis=0, tiled=True)]
    dot_general x28 -> x2, matrix products: 53.4 us -> 4.2 us  [dot_nn(): lax.dot_general(a, b, (((1,), (0,)), ((), ())), preferred_element_type=jn...]
    pallas_call x0 -> x3, Pallas kernels: none -> 16.6 us  [the longest x1 7.91 us: attend(): pl.pallas_call(attend_kernel, out_shape=jax.ShapeDtypeStruct((count, widt...]
    all_to_all x0 -> x2, starting transfers between devices: none -> 15.8 us  [the longest x1 9.81 us: body(): got = lax.all_to_all(sent, 'dp', 0, 0, tiled=True)]
  transfers between devices with their start and end apart: 6 -> 7, of which waited for: 6 -> 4; matrix products, arithmetic and copies ran while one was open for 5% -> 2% of each run, Pallas kernels for 0% -> 9%
where the time goes in v1:
time: 88 us; the launch traced here: 87.3 us
  waiting for transfers between devices  23.9 us (27%)
  starting transfers between devices  23.6 us (27%)
  Pallas kernels  16.6 us (19%)
  local copies, waits for them, and re-layouts  8.52 us (10%)
  other arithmetic  6.16 us (7%)
  between operations  4.33 us (5%)
  matrix products  4.2 us (5%)
    ppermute x5, waiting for transfers between devices, tensor_swap(): return lax.ppermute(values, 'tensor', [(i, i ^ bit) for i in range(size)])  15.6 us
    all_to_all x1, starting transfers between devices, body(): got = lax.all_to_all(sent, 'dp', 0, 0, tiled=True)  9.81 us
    all_to_all x1, waiting for transfers between devices, body(): got = lax.all_to_all(sent, 'dp', 0, 0, tiled=True)  8.3 us
    pallas_call x1, Pallas kernels, attend(): pl.pallas_call(attend_kernel, out_shape=jax.ShapeDtypeStruct((count, widt...  7.91 us
    ppermute x5, starting transfers between devices, tensor_swap(): return lax.ppermute(values, 'tensor', [(i, i ^ bit) for i in range(size)])  7.78 us
    pallas_call x1, Pallas kernels, base_products(): pl.pallas_call(base_kernel, out_shape=(jax.ShapeDtypeStruct((count, width...  7.54 us
    all_to_all x1, starting transfers between devices, body(): lax.all_to_all(jnp.broadcast_to(rows[None], (groups,) + rows.shape), 'dp'...  6 us
    unnamed x21, local copies, waits for them, and re-layouts  4.43 us
  transfers between devices with their start and end apart: 7, of which 4 were waited for; matrix products, arithmetic and copies ran while one was open for 2% of the time, Pallas kernels for 9%

profile of v1, /device:TPU:1, one launch (start us, length us, event | category | flops | bytes accessed | tf_op | source)
XLA Modules:
  0.0 87.3 jit_solution(17134975945593066978)
XLA Ops:
  0.6 0.0 copy-start
  0.7 0.8 reshape.259
  1.5 0.1 copy.38
  1.6 0.1 copy.39
  1.7 0.8 and_reduce_fusion
  2.5 0.1 copy.40
  2.6 0.1 copy.43
  2.6 0.1 copy.42
  2.7 0.9 %convert_reduce_fusion = s32[32,32]{1,0:T(8,128)S(1)} fusion(s32[32,32]{1,0:T(8,128)S(1)} %copy.39, s32[32,32]{1,0:T(8,128)S(1)} %copy.40, pred[32,32]{1,0:T(8,128)(4,1)S(1)} %not.8), kind=kLoop, calls=%fused_computation.26 | loop fusion | flops 195584 | bytes 13312 | tf_op jit(solution)/shard_map/reduce_sum | solution.py:50
  3.7 0.6 select_reduce_fusion.1
  4.3 0.1 eq.140
  4.4 0.1 reshape.261
  4.5 1.0 %reshape_squeeze.3 = bf16[32,4,512]{2,1,0:T(4,128)(2,1)S(1)} reshape(bf16[1,64,1024]{2,1,0:T(8,128)(2,1)} %param.27) | data formatting | bytes 262144 | tf_op jit(solution)/shard_map/reshape;squeeze | solution.py:305
  5.5 0.0 copy-start.6
  5.5 0.0 copy-start.8
  5.5 0.0 copy-start.9
  5.5 0.0 copy-start.7
  5.5 4.0 %fusion.10 = bf16[32,8,1024]{2,1,0:T(8,128)(2,1)S(1)} fusion(bf16[2374,1024]{1,0:T(8,128)(2,1)} %param.17, s32[256]{0:T(256)S(1)} %eq.140), kind=kOutput, calls=%fused_computation.21 | convolution fusion | flops 1245529600 | bytes 5387264 | tf_op jit(solution)/shard_map/dot_general | solution.py:37
  9.5 1.0 %maximum_maximum_fusion = bf16[32,8,1536]{2,1,0:T(8,128)(2,1)} fusion(bf16[32,4,512]{2,1,0:T(4,128)(2,1)S(1)} %reshape_squeeze.3, bf16[32,4,512]{2,1,0:T(4,128)(2,1)S(1)} %reshape.261, bf16[32,8,1024]{2,1,0:T(8,128)(2,1)S(1)} %fusion.10), kind=kLoop, calls=%fused_computation.23 | loop fusion | flops 2359296 | bytes 1572864 | tf_op jit(solution)/shard_map/concatenate | solution.py:307
  10.6 9.8 %all-to-all-start.1 = ((bf16[32,8,1536]{2,1,0:T(8,128)(2,1)}), bf16[32,8,1536]{2,1,0:T(8,128)(2,1)S(1)}, u32[]{:S(2)}, u32[]{:S(2)}) async-start(bf16[32,8,1536]{2,1,0:T(8,128)(2,1)} %maximum_maximum_fusion), calls=%async_computation.1 | async-start | bytes 1572864 | tf_op jit(solution)/shard_map/all_to_all | solution.py:310
  20.4 0.6 reduce_max.31
  23.6 0.2 fusion.16
  23.8 0.2 divide_reduce_fusion
  24.1 0.2 select_reduce_fusion.2
  24.3 8.3 %all-to-all-done.1 = bf16[32,8,1536]{2,1,0:T(8,128)(2,1)S(1)} async-done(((bf16[32,8,1536]{2,1,0:T(8,128)(2,1)}), bf16[32,8,1536]{2,1,0:T(8,128)(2,1)S(1)}, u32[]{:S(2)}, u32[]{:S(2)}) %all-to-all-start.1) | async-done | bytes 786464 | tf_op jit(solution)/shard_map/all_to_all | solution.py:310
  32.6 0.1 multiply_reduce_fusion
  32.7 0.2 convolution_convert_fusion.1
  33.0 0.0 copy-start.4
  33.0 1.1 %broadcast_in_dim.60 = f32[32,8,1024]{2,1,0:T(8,128)} broadcast(f32[8,1024]{1,0:T(8,128)S(1)} %pad_maximum_fusion.2), dimensions={1,2} | broadcast | bytes 1081344 | tf_op jit(solution)/shard_map/broadcast_in_dim | solution.py:333
  34.1 6.0 %all-to-all-start.2 = ((f32[32,8,1024]{2,1,0:T(8,128)}), f32[32,8,1024]{2,1,0:T(8,128)S(1)}, u32[]{:S(2)}, u32[]{:S(2)}) async-start(f32[32,8,1024]{2,1,0:T(8,128)} %broadcast_in_dim.60), calls=%async_computation.2 | async-start | bytes 2097152 | tf_op jit(solution)/shard_map/all_to_all | solution.py:332
  40.1 1.3 %collective-permute-start = (bf16[32,1024]{1,0:T(8,128)(2,1)S(1)}, bf16[32,1024]{1,0:T(8,128)(2,1)S(1)}, u32[]{:S(2)}, u32[]{:S(2)}) collective-permute-start(bf16[32,1024]{1,0:T(8,128)(2,1)S(1)} %get-tuple-element.89.e0), channel_id=1, source_target_pairs={{0,1},{1,0},{2,3},{3,2},{4,5},{5,4},{6,7},{7,6},{8,9},{9,8},{10,11... | collective-permute-start | bytes 196616 | tf_op jit(solution)/shard_map/ppermute | solution.py:271
  41.4 2.5 %collective-permute-start.1 = (bf16[32,1024]{1,0:T(8,128)(2,1)S(1)}, bf16[32,1024]{1,0:T(8,128)(2,1)S(1)}, u32[]{:S(2)}, u32[]{:S(2)}) collective-permute-start(bf16[32,1024]{1,0:T(8,128)(2,1)S(1)} %get-tuple-element.89.e0), channel_id=1, source_target_pairs={{0,2},{1,3},{2,0},{3,1},{4,6},{5,7},{6,4},{7,5},{8,10},{9,11},{10,... | collective-permute-start | bytes 196616 | tf_op jit(solution)/shard_map/ppermute | solution.py:271
  43.9 0.8 collective-permute-start.2
  44.6 0.1 pad_add_fusion.place
  44.7 10.2 %collective-permute-done.1.e2 = bf16[32,1024]{1,0:T(8,128)(2,1)S(1)} collective-permute-done((bf16[32,1024]{1,0:T(8,128)(2,1)S(1)}, bf16[32,1024]{1,0:T(8,128)(2,1)S(1)}, u32[]{:S(2)}, u32[]{:S(2)}) %collective-permute-start.1) | collective-permute-done | bytes 65568 | tf_op jit(solution)/shard_map/ppermute | solution.py:271
  54.9 2.9 %collective-permute-done.2.e3 = bf16[32,1024]{1,0:T(8,128)(2,1)S(1)} collective-permute-done((bf16[32,1024]{1,0:T(8,128)(2,1)S(1)}, bf16[32,1024]{1,0:T(8,128)(2,1)S(1)}, u32[]{:S(2)}, u32[]{:S(2)}) %collective-permute-start.2) | collective-permute-done | bytes 65568 | tf_op jit(solution)/shard_map/ppermute | solution.py:271
  57.8 0.0 all-to-all-done.2.factors
  57.8 1.2 %project.1 = (bf16[32,4096]{1,0:T(8,128)(2,1)S(1)}, f32[40,256]{1,0:T(8,128)S(1)}) custom-call(s32[2]{0:T(128)S(1)} %pad_add_fusion.place, bf16[32,1024]{1,0:T(8,128)(2,1)S(1)} %get-tuple-element.89.e0, bf16[32,1024]{1,0:T(8,128)(2,1)S(1)} %collective-permute-done.e1, bf16[32,1024]{1,0:T(8,128)(2,1)S(1)} %collective-permute-done.1.e2, ...), custom_call_target="tpu_custom_call" | custom-call | tf_op jit(solution)/shard_map/project/pallas_call | solution.py:185
  59.0 0.7 collective-permute-start.3
  59.7 2.2 %copy-done.1 = bf16[2,4096,256]{2,1,0:T(8,128)(2,1)S(1)} copy-done((bf16[2,4096,256]{2,1,0:T(8,128)(2,1)S(1)}, bf16[2,4096,256]{2,1,0:T(8,128)(2,1)}, u32[]{:S(2)}) %copy-start.1) | copy-done | bytes 4194328
  61.9 7.5 %base_products.1 = (f32[32,1024]{1,0:T(8,128)S(1)}, bf16[32,128]{1,0:T(8,128)(2,1)S(1)}, bf16[32,128]{1,0:T(8,128)(2,1)S(1)}) custom-call(s32[2]{0:T(128)S(1)} %pad_add_fusion.place, bf16[32,4096]{1,0:T(8,128)(2,1)S(1)} %get-tuple-element.90.normed, bf16[4096,1024]{1,0:T(8,128)(2,1)} %base.1, bf16[2,4096,256]{2,1,0:T(8,128)(2,1)S(1)} %copy-done.1, ...), custom_call_target="tpu_custom_call" | custom-call | flops 268435456 | bytes 8388608 | tf_op jit(solution)/shard_map/base_products/pallas_call | solution.py:218
  69.6 2.5 %collective-permute-start.4 = (f32[56,256]{1,0:T(8,128)S(1)}, f32[56,256]{1,0:T(8,128)S(1)}, u32[]{:S(2)}, u32[]{:S(2)}) collective-permute-start(f32[56,256]{1,0:T(8,128)S(1)} %pad_maximum_fusion), channel_id=1, source_target_pairs={{0,2},{1,3},{2,0},{3,1},{4,6},{5,7},{6,4},{7,5},{8,10},{9,11},{10,... | collective-permute-start | bytes 172040 | tf_op jit(solution)/shard_map/ppermute | solution.py:271
  72.1 2.5 %collective-permute-done.4 = f32[56,256]{1,0:T(8,128)S(1)} collective-permute-done((f32[56,256]{1,0:T(8,128)S(1)}, f32[56,256]{1,0:T(8,128)S(1)}, u32[]{:S(2)}, u32[]{:S(2)}) %collective-permute-start.4) | collective-permute-done | bytes 57376 | tf_op jit(solution)/shard_map/ppermute | solution.py:271
  74.7 0.5 slice.44
  75.9 0.6 sub.86
  76.6 0.6 sub.85
  77.3 2.2 %copy-done.2 = bf16[8,512,2,256]{3,2,1,0:T(2,128)(2,1)S(1)} copy-done((bf16[8,512,2,256]{3,2,1,0:T(2,128)(2,1)S(1)}, bf16[8,512,2,256]{3,2,1,0:T(2,128)(2,1)}, u32[]{:S(2)}) %copy-start.2) | copy-done | bytes 4194328
  79.4 7.9 %attend.1 = bf16[32,1024]{1,0:T(8,128)(2,1)} custom-call(s32[2]{0:T(128)S(1)} %pad_add_fusion.place, f32[32,1024]{1,0:T(8,128)S(1)} %get-tuple-element.91.base_query, f32[40,256]{1,0:T(8,128)S(1)} %slice_add_fusion.products, f32[32,8,1024]{2,1,0:T(8,128)S(1)} %all-to-all-done.2.factors, f32[1,128]{1,0:T(1,128)S(1)} %bitcast.68, ...), custom_call_target="tpu_custom_call" | custom-call | tf_op jit(solution)/shard_map/attend/pallas_call | solution.py:260
  (42 shorter events, 0.3 us)
Async XLA Ops:
  0.6 3.7 %copy-start = (bf16[1,64,4096]{2,1,0:T(8,128)(2,1)S(1)}, bf16[1,64,4096]{2,1,0:T(8,128)(2,1)}, u32[]{:S(2)}) copy-start(bf16[1,64,4096]{2,1,0:T(8,128)(2,1)} %param.26) | copy-start | bytes 1572868
  5.5 18.5 %copy-start.6 = (f32[2,4096]{1,0:T(2,128)S(1)}, f32[2,4096]{1,0:T(2,128)}, u32[]{:S(2)}) copy-start(f32[2,4096]{1,0:T(2,128)} %param.24) | copy-start | bytes 98308
  5.5 18.5 %copy-start.8 = (f32[32]{0:T(128)S(1)}, f32[32]{0:T(128)}, u32[]{:S(2)}) copy-start(f32[32]{0:T(128)} %param.28) | copy-start | bytes 388
  5.5 18.5 %copy-start.9 = (s32[32]{0:T(128)S(1)}, s32[32]{0:T(128)}, u32[]{:S(2)}) copy-start(s32[32]{0:T(128)} %param.29) | copy-start | bytes 388
  5.5 27.2 %copy-start.7 = (f32[2,1024]{1,0:T(2,128)S(1)}, f32[2,1024]{1,0:T(2,128)}, u32[]{:S(2)}) copy-start(f32[2,1024]{1,0:T(2,128)} %param.25) | copy-start | bytes 24580
  10.6 22.0 %all-to-all-start.1 = ((bf16[32,8,1536]{2,1,0:T(8,128)(2,1)}), bf16[32,8,1536]{2,1,0:T(8,128)(2,1)S(1)}, u32[]{:S(2)}, u32[]{:S(2)}) async-start(bf16[32,8,1536]{2,1,0:T(8,128)(2,1)} %maximum_maximum_fusion), calls=%async_computation.1 | async-start | bytes 1572864 | tf_op jit(solution)/shard_map/all_to_all | solution.py:310
  33.0 24.9 %copy-start.3 = (f32[4096]{0:T(1024)S(1)}, f32[4096]{0:T(1024)}, u32[]{:S(2)}) copy-start(f32[4096]{0:T(1024)} %param.18) | copy-start | bytes 49156
  33.0 26.7 %copy-start.4 = (f32[128]{0:T(128)S(1)}, f32[128]{0:T(128)}, u32[]{:S(2)}) copy-start(f32[128]{0:T(128)} %param.20) | copy-start | bytes 1540
  34.1 23.7 %all-to-all-start.2 = ((f32[32,8,1024]{2,1,0:T(8,128)}), f32[32,8,1024]{2,1,0:T(8,128)S(1)}, u32[]{:S(2)}, u32[]{:S(2)}) async-start(f32[32,8,1024]{2,1,0:T(8,128)} %broadcast_in_dim.60), calls=%async_computation.2 | async-start | bytes 2097152 | tf_op jit(solution)/shard_map/all_to_all | solution.py:332
  40.1 4.6 %collective-permute-start = (bf16[32,1024]{1,0:T(8,128)(2,1)S(1)}, bf16[32,1024]{1,0:T(8,128)(2,1)S(1)}, u32[]{:S(2)}, u32[]{:S(2)}) collective-permute-start(bf16[32,1024]{1,0:T(8,128)(2,1)S(1)} %get-tuple-element.89.e0), channel_id=1, source_target_pairs={{0,1},{1,0},{2,3},{3,2},{4,5},{5,4},{6,7},{7,6},{8,9},{9,8},{10,11... | collective-permute-start | bytes 196616 | tf_op jit(solution)/shard_map/ppermute | solution.py:271
  41.4 13.5 %collective-permute-start.1 = (bf16[32,1024]{1,0:T(8,128)(2,1)S(1)}, bf16[32,1024]{1,0:T(8,128)(2,1)S(1)}, u32[]{:S(2)}, u32[]{:S(2)}) collective-permute-start(bf16[32,1024]{1,0:T(8,128)(2,1)S(1)} %get-tuple-element.89.e0), channel_id=1, source_target_pairs={{0,2},{1,3},{2,0},{3,1},{4,6},{5,7},{6,4},{7,5},{8,10},{9,11},{10,... | collective-permute-start | bytes 196616 | tf_op jit(solution)/shard_map/ppermute | solution.py:271
  43.9 13.9 %collective-permute-start.2 = (bf16[32,1024]{1,0:T(8,128)(2,1)S(1)}, bf16[32,1024]{1,0:T(8,128)(2,1)S(1)}, u32[]{:S(2)}, u32[]{:S(2)}) collective-permute-start(bf16[32,1024]{1,0:T(8,128)(2,1)S(1)} %get-tuple-element.89.e0), channel_id=1, source_target_pairs={{0,3},{1,2},{2,1},{3,0},{4,7},{5,6},{6,5},{7,4},{8,11},{9,10},{10,... | collective-permute-start | bytes 196616 | tf_op jit(solution)/shard_map/ppermute | solution.py:271
  59.0 10.4 %collective-permute-start.3 = (f32[48,256]{1,0:T(8,128)S(1)}, f32[48,256]{1,0:T(8,128)S(1)}, u32[]{:S(2)}, u32[]{:S(2)}) collective-permute-start(f32[48,256]{1,0:T(8,128)S(1)} %pad_maximum_fusion.1), channel_id=1, source_target_pairs={{0,1},{1,0},{2,3},{3,2},{4,5},{5,4},{6,7},{7,6},{8,9},{9,8},{10,11... | collective-permute-start | bytes 147464 | tf_op jit(solution)/shard_map/ppermute | solution.py:271
  59.7 2.2 %copy-start.1 = (bf16[2,4096,256]{2,1,0:T(8,128)(2,1)S(1)}, bf16[2,4096,256]{2,1,0:T(8,128)(2,1)}, u32[]{:S(2)}) copy-start(bf16[2,4096,256]{2,1,0:T(8,128)(2,1)} %pair.1) | copy-start | bytes 12582916
  61.9 15.3 %copy-start.5 = (f32[128]{0:T(128)S(1)}, f32[128]{0:T(128)}, u32[]{:S(2)}) copy-start(f32[128]{0:T(128)} %param.19) | copy-start | bytes 1540
  69.6 5.1 %collective-permute-start.4 = (f32[56,256]{1,0:T(8,128)S(1)}, f32[56,256]{1,0:T(8,128)S(1)}, u32[]{:S(2)}, u32[]{:S(2)}) collective-permute-start(f32[56,256]{1,0:T(8,128)S(1)} %pad_maximum_fusion), channel_id=1, source_target_pairs={{0,2},{1,3},{2,0},{3,1},{4,6},{5,7},{6,4},{7,5},{8,10},{9,11},{10,... | collective-permute-start | bytes 172040 | tf_op jit(solution)/shard_map/ppermute | solution.py:271
  77.3 2.2 %copy-start.2 = (bf16[8,512,2,256]{3,2,1,0:T(2,128)(2,1)S(1)}, bf16[8,512,2,256]{3,2,1,0:T(2,128)(2,1)}, u32[]{:S(2)}) copy-start(bf16[8,512,2,256]{3,2,1,0:T(2,128)(2,1)} %param.23) | copy-start | bytes 12582916

commit v2 on v0

v2 whole, which is shorter than its diff:
```python
import math

import jax
import jax.numpy as jnp
from jax import lax
from jax.experimental import pallas as pl
from jax.experimental.pallas import tpu as pltpu
from jax.sharding import PartitionSpec as P

D = 4096
HEAD = 128
HEADS = 32
KVH = 2
R = 64
STEPS = 4
HD = 4096
CAP = 8

TABLE_PARTS = 2

EPSILON = 1e-06
STEP_RATIO = 0.3
ADAPTER_SCALING = 1.0 / 1024.0
RATE = STEP_RATIO * math.sqrt(R * (D + HD))
MIB = 1024 * 1024


def split(values):
    high = values.astype(jnp.bfloat16)
    return high, (values - high.astype(jnp.float32)).astype(jnp.bfloat16)


def dot_nt(a, b):
    return lax.dot_general(a, b, (((1,), (1,)), ((), ())), preferred_element_type=jnp.float32)


def dot_nn(a, b):
    return lax.dot_general(a, b, (((1,), (0,)), ((), ())), preferred_element_type=jnp.float32)


def vmem():
    return pl.BlockSpec(memory_space=pltpu.VMEM)


def smem():
    return pl.BlockSpec(memory_space=pltpu.SMEM)


def whole(x):
    return pl.BlockSpec(x.shape, lambda *_: (0,) * len(x.shape))


def params(mib):
    return pltpu.CompilerParams(vmem_limit_bytes=mib * MIB)


def fold(down, up):
    half = down.shape[1] // 2
    rows = [x[i : i + 1, h * half : (h + 1) * half] for x in (down, up) for i in (0, 1) for h in (0, 1)]
    return jnp.concatenate(rows, axis=0)


def arrange_ids(tokens, groups):
    steps, rows = tokens.shape
    here = rows // groups
    row = lax.broadcasted_iota(jnp.int32, (groups, rows), 0)
    lane = lax.broadcasted_iota(jnp.int32, (groups, rows), 1)
    parts = []
    for s in range(steps):
        own = jnp.where(lane // here == row, jnp.broadcast_to(tokens[s : s + 1], lane.shape), 0)
        parts.append(own)
    wide = jnp.concatenate(parts, axis=1)
    pieces = jnp.concatenate([wide & 255, (wide >> 8) & 255, wide >> 16], axis=0)
    pieces = pieces.astype(jnp.float32).astype(jnp.bfloat16)
    source = lax.broadcasted_iota(jnp.int32, (steps * rows, 128), 0)
    target = lax.broadcasted_iota(jnp.int32, (steps * rows, 128), 1) % (steps * here)
    same = (source % here == target % here) & (source // rows == target // here)
    ids = dot_nn(pieces, jnp.where(same, 1.0, 0.0).astype(jnp.bfloat16)).astype(jnp.int32)
    return ids[:groups] + (ids[groups : 2 * groups] << 8) + (ids[2 * groups :] << 16)


def find_rows(place, first, ids, table, period, pick, places):
    groups, lanes = ids.shape
    vocab_rows = table.shape[0]
    lane = lax.broadcasted_iota(jnp.int32, ids.shape, 1) % period
    owner = ((ids.astype(jnp.float32) + 0.5) * (1.0 / vocab_rows)).astype(jnp.int32)
    lowest = owner * vocab_rows
    repeated = jnp.zeros(ids.shape, jnp.int32)
    for k in range(1, period):
        repeated = jnp.where((pltpu.roll(ids, k, 1) == ids) & (lane >= k), 1, repeated)
    distinct = jnp.where(repeated == 0, ids, -1)
    slot = jnp.zeros(ids.shape, jnp.int32)
    for k in range(1, period):
        other = pltpu.roll(distinct, k, 1)
        slot += jnp.where((other >= lowest) & (other < ids), 1, 0)
    rounds = jnp.max(slot) // CAP + 1
    slot -= first
    places[...] = jnp.where((slot >= 0) & (slot < CAP), owner * CAP + slot, -1)

    me = place[2]
    own = places[pl.ds(me, 1), :]
    rows = groups * CAP
    at = lax.broadcasted_iota(jnp.int32, (rows, lanes), 0)
    pick[...] = jnp.where(at == own, 1.0, 0.0).astype(jnp.bfloat16)[:, :period]

    local = jnp.where(owner == me, ids - lowest, -1)
    spread = (groups, CAP, lanes)
    local = jnp.broadcast_to(local[:, None, :], spread).reshape(rows, lanes)
    slot = jnp.broadcast_to(slot[:, None, :], spread).reshape(rows, lanes)
    wanted = lax.broadcasted_iota(jnp.int32, (rows, lanes), 0) % CAP
    chosen = jnp.max(jnp.where(slot == wanted, local, -1), axis=1, keepdims=True)
    return chosen, rounds


def one_hot(chosen, vocab_rows):
    at = lax.broadcasted_iota(jnp.int32, (chosen.shape[0], vocab_rows), 1)
    return jnp.where(at == chosen, 1.0, 0.0).astype(jnp.bfloat16)


def read_rows(hot, table):
    main = hot.shape[1] // 256 * 256
    found = dot_nn(hot[:, :main], table[:main, :])
    if main < hot.shape[1]:
        found += dot_nn(hot[:, main:], table[main:, :])
    return found.astype(jnp.bfloat16)


def send_kernel(
    place, tokens_at, table_at, grad_down_at, grad_up_at, down_at, up_at, sent, pick, rounds,
    tokens, table, grad_down, grad_up, down, up, places, sems,
):
    groups = sent.shape[0] // CAP
    vocab_rows, width = table.shape
    half = width // 2
    ranks = grad_up.shape[1]
    columns = pl.ds(pl.multiple_of(place[0] * width, width), width)
    copies = [
        pltpu.make_async_copy(source, target, sems.at[i])
        for i, (source, target) in enumerate(
            (
                (tokens_at, tokens),
                (grad_down_at.at[:, :, columns], grad_down),
                (grad_up_at, grad_up),
                (down_at, down),
                (up_at, up),
            )
        )
    ]
    span = width // TABLE_PARTS
    spans = [slice(i * span, (i + 1) * span) for i in range(TABLE_PARTS)]
    copies += [
        pltpu.make_async_copy(table_at.at[:, at], table.at[:, at], sems.at[5 + i])
        for i, at in enumerate(spans)
    ]
    for copy in copies:
        copy.start()
    copies[0].wait()
    ids = arrange_ids(tokens[...], groups)
    chosen, count = find_rows(place, 0, ids, table, pick.shape[1], pick, places)
    rounds[0] = count
    for copy in copies[1:5]:
        copy.wait()

    grads = jnp.concatenate([grad_down[0], grad_up[0]], axis=0)
    row = lax.broadcasted_iota(jnp.int32, (groups * 8, 2 * ranks), 0)
    source = lax.broadcasted_iota(jnp.int32, (groups * 8, 2 * ranks), 1)
    wanted = row // 4 % 2 * ranks + row // 8 * 2 + row // 2 % 2
    moved = jnp.zeros((groups * 8, half), jnp.float32)
    for h in (0, 1):
        taken = jnp.where((source == wanted) & (row % 2 == h), 1.0, 0.0).astype(jnp.bfloat16)
        moved += dot_nn(taken, grads[:, h * half : (h + 1) * half])
    sent[:, width : width + half] = moved.astype(jnp.bfloat16)
    for i, part in enumerate(split(fold(down[:, columns], up[...]))):
        part = jnp.broadcast_to(part[None], (groups, 8, half)).reshape(groups * 8, half)
        sent[:, width + (1 + i) * half : width + (2 + i) * half] = part

    hot = one_hot(chosen, vocab_rows)
    for i, at in enumerate(spans):
        copies[5 + i].wait()
        sent[:, at] = read_rows(hot, table.at[:, at])


def send(place, tokens, table, grad_down, grad_up, down, up, groups):
    width = table.shape[1]
    count = tokens.size // groups
    anywhere = pl.BlockSpec(memory_space=pl.ANY)
    return pl.pallas_call(
        send_kernel,
        out_shape=(
            jax.ShapeDtypeStruct((groups * CAP, width * 5 // 2), jnp.bfloat16),
            jax.ShapeDtypeStruct((groups * CAP, count), jnp.bfloat16),
            jax.ShapeDtypeStruct((1,), jnp.int32),
        ),
        in_specs=[smem()] + [anywhere] * 6,
        out_specs=(vmem(), vmem(), smem()),
        scratch_shapes=[
            pltpu.VMEM(tokens.shape, jnp.int32),
            pltpu.VMEM(table.shape, jnp.bfloat16),
            pltpu.VMEM(grad_up.shape, jnp.bfloat16),
            pltpu.VMEM(grad_up.shape, jnp.bfloat16),
            pltpu.VMEM(down.shape, jnp.float32),
            pltpu.VMEM(up.shape, jnp.float32),
            pltpu.VMEM((groups, 128), jnp.int32),
            pltpu.SemaphoreType.DMA((5 + TABLE_PARTS,)),
        ],
        compiler_params=params(56),
        name="send",
    )(place, tokens, table, grad_down, grad_up, down, up)


def again_kernel(place, first, tokens, table, sent, pick, places):
    groups = sent.shape[0] // CAP
    ids = arrange_ids(tokens[...], groups)
    chosen, _ = find_rows(place, first[0], ids, table, pick.shape[1], pick, places)
    sent[...] = read_rows(one_hot(chosen, table.shape[0]), table)


def again(place, first, tokens, table, groups):
    return pl.pallas_call(
        again_kernel,
        out_shape=(
            jax.ShapeDtypeStruct((groups * CAP, table.shape[1]), jnp.bfloat16),
            jax.ShapeDtypeStruct((groups * CAP, tokens.size // groups), jnp.bfloat16),
        ),
        in_specs=[smem(), smem(), vmem(), vmem()],
        out_specs=(vmem(), vmem()),
        scratch_shapes=[pltpu.VMEM((groups, 128), jnp.int32)],
        compiler_params=params(20),
        name="again",
    )(place, first, tokens, table)


def gather_kernel(scale, learner, got, pick, extra, block, own_sum, sent):
    groups = got.shape[0]
    count, width = extra.shape
    half = width // 2
    total = jnp.zeros((8, half), jnp.float32)
    for learn in range(groups):
        weight = scale[learner[learn]]
        total += got[learn, :, width : width + half].astype(jnp.float32) * weight
    own_sum[...] = total
    sent[...] = jnp.broadcast_to(total[None], sent.shape)
    rows = got[:, :, :width].reshape(groups * CAP, width)
    found = lax.dot_general(
        pick[...], rows, (((0,), (0,)), ((), ())), preferred_element_type=jnp.float32
    )
    block[:count, :] = found.astype(jnp.bfloat16) + extra[...]
    down = jnp.concatenate(
        [jnp.concatenate([total[2 * i : 2 * i + 1], total[2 * i + 1 : 2 * i + 2]], 1) for i in (0, 1)], 0
    )
    first, _ = split(down)
    second, third = split(down - first.astype(jnp.float32))
    rows = [first, second, third, jnp.zeros((10, width), jnp.bfloat16)]
    block[count:, :] = jnp.concatenate([r.astype(jnp.float32) for r in rows], 0).astype(jnp.bfloat16)


def gather(scale, learner, got, pick, extra):
    groups = got.shape[0]
    count, width = extra.shape
    return pl.pallas_call(
        gather_kernel,
        out_shape=(
            jax.ShapeDtypeStruct((count + 16, width), jnp.bfloat16),
            jax.ShapeDtypeStruct((8, width // 2), jnp.float32),
            jax.ShapeDtypeStruct((groups, 8, width // 2), jnp.float32),
        ),
        in_specs=[smem(), smem(), vmem(), vmem(), vmem()],
        out_specs=(vmem(), vmem(), vmem()),
        compiler_params=params(8),
        name="gather",
    )(scale, learner, got, pick, extra)


def stage_kernel(place, cache_at, keys_at, values_at, cache, keys, values, wide, sems):
    rows, _, count = keys.shape
    copies = [pltpu.make_async_copy(cache_at.at[i], cache.at[i], sems.at[i]) for i in range(rows)]
    for copy in copies:
        copy.start()
    back = []
    for i in range(rows):
        copies[i].wait()
        wide[...] = cache[i].astype(jnp.float32)
        keys[i] = wide[pl.ds(place[1], count, stride=4), :].T.astype(jnp.bfloat16)
        values[i] = wide[pl.ds(place[1] + 2, count, stride=4), :].astype(jnp.bfloat16)
        back.append(pltpu.make_async_copy(keys.at[i], keys_at.at[i], sems.at[rows + 2 * i]))
        back.append(pltpu.make_async_copy(values.at[i], values_at.at[i], sems.at[rows + 2 * i + 1]))
        back[-2].start()
        back[-1].start()
    for copy in back:
        copy.wait()


def stage(place, cache, after):
    rows, entries, _ = cache.shape
    place, _ = lax.optimization_barrier((place, after))
    anywhere = pl.BlockSpec(memory_space=pl.ANY)
    keys = jax.ShapeDtypeStruct((rows, HEAD, entries // 4), jnp.bfloat16)
    values = jax.ShapeDtypeStruct((rows, entries // 4, HEAD), jnp.bfloat16)
    return pl.pallas_call(
        stage_kernel,
        out_shape=[keys, values],
        in_specs=[smem(), anywhere],
        out_specs=[anywhere] * 2,
        scratch_shapes=[
            pltpu.VMEM(cache.shape, jnp.bfloat16),
            pltpu.VMEM(keys.shape, jnp.bfloat16),
            pltpu.VMEM(values.shape, jnp.bfloat16),
            pltpu.VMEM((entries, HEAD), jnp.float32),
            pltpu.SemaphoreType.DMA((3 * rows,)),
        ],
        compiler_params=params(58),
        cost_estimate=pl.CostEstimate(flops=0, bytes_accessed=2**23, transcendentals=0),
        name="stage",
    )(place, cache)


def pair_kernel(place, normed, gain, pair_at, key_new, value_new, pair, sem):
    copy = pltpu.make_async_copy(pair_at.at[place[1]], pair, sem)
    copy.start()
    copy.wait()
    pairs = dot_nn(normed[...], pair[...])
    keys = pairs[:, :HEAD]
    scale = lax.rsqrt(jnp.mean(keys * keys, axis=1, keepdims=True) + EPSILON)
    key_new[...] = (keys * scale * gain[...]).astype(jnp.bfloat16)
    value_new[...] = pairs[:, HEAD:].astype(jnp.bfloat16)


def pair_products(place, normed, gain, pair):
    fresh = jax.ShapeDtypeStruct((normed.shape[0], HEAD), jnp.bfloat16)
    return pl.pallas_call(
        pair_kernel,
        out_shape=(fresh, fresh),
        in_specs=[smem(), vmem(), vmem(), pl.BlockSpec(memory_space=pl.ANY)],
        out_specs=(vmem(), vmem()),
        scratch_shapes=[
            pltpu.VMEM(pair.shape[1:], jnp.bfloat16),
            pltpu.SemaphoreType.DMA(()),
        ],
        compiler_params=params(58),
        cost_estimate=pl.CostEstimate(flops=0, bytes_accessed=2**23, transcendentals=0),
        name="pair_products",
    )(place, normed, gain.reshape(1, -1), pair)


def fetch_kernel(place, keys_at, values_at, keys, values, sems):
    copies = [
        pltpu.make_async_copy(keys_at, keys, sems.at[0]),
        pltpu.make_async_copy(values_at, values, sems.at[1]),
    ]
    for copy in copies:
        copy.start()
    for copy in copies:
        copy.wait()


def fetch(place, keys, values, after):
    place, _ = lax.optimization_barrier((place, after))
    return pl.pallas_call(
        fetch_kernel,
        out_shape=[jax.ShapeDtypeStruct(x.shape, x.dtype) for x in (keys, values)],
        in_specs=[smem()] + [pl.BlockSpec(memory_space=pl.ANY)] * 2,
        out_specs=[vmem(), vmem()],
        scratch_shapes=[pltpu.SemaphoreType.DMA((2,))],
        compiler_params=params(1),
        cost_estimate=pl.CostEstimate(flops=0, bytes_accessed=2**22, transcendentals=0),
        name="fetch",
    )(place, keys, values)


def norm_kernel(place, e0, e1, e2, e3, gain, normed, own):
    t = place[0]
    count, width = own.shape
    blocks = [e[:count, :].astype(jnp.float32) for e in (e0, e1, e2, e3)]
    square = sum(jnp.sum(b * b, axis=1, keepdims=True) for b in blocks)
    scale = lax.rsqrt(square / D + EPSILON)
    for k, block in enumerate(blocks):
        columns = pl.ds(pl.multiple_of((t ^ k) * width, width), width)
        value = (block * scale * gain[:, columns]).astype(jnp.bfloat16)
        normed[:, columns] = value
        if k == 0:
            own[...] = value


def norm(place, blocks, gain, count):
    width = blocks[0].shape[1]
    return pl.pallas_call(
        norm_kernel,
        out_shape=(
            jax.ShapeDtypeStruct((count, 4 * width), jnp.bfloat16),
            jax.ShapeDtypeStruct((count, width), jnp.bfloat16),
        ),
        in_specs=[smem()] + [vmem()] * 5,
        out_specs=(vmem(), vmem()),
        compiler_params=params(8),
        name="norm",
    )(place, *blocks, gain.reshape(1, -1))


def old_factors(got, half):
    return got[:, :, 3 * half : 4 * half], got[:, :, 4 * half :]


def products_kernel(own, sums, got, out):
    count = own.shape[0]
    half = sums.shape[2]

    def combine(parts):
        left = sum(dot_nt(own[:, :half], p) for p in parts)
        right = sum(dot_nt(own[:, half:], p) for p in parts)
        lane = lax.broadcasted_iota(jnp.int32, left.shape, 1)
        mixed = jnp.where(lane % 2 == 0, left, right)
        mixed = mixed + pltpu.roll(mixed, mixed.shape[1] - 1, 1)
        return jnp.where((lane % 8 == 0) | (lane % 8 == 2), mixed, 0.0)

    rows = sums[...].reshape(-1, half)
    high, low = old_factors(got, half)
    old = combine([high.reshape(-1, half), low.reshape(-1, half)])
    new = combine(split(rows))
    out[:count, :] = new + pltpu.roll(old, 1, 1)
    out[count:, :] = jnp.full((8, rows.shape[0]), jnp.sum(rows * rows), jnp.float32)


def products(own, sums, got):
    count = own.shape[0]
    return pl.pallas_call(
        products_kernel,
        out_shape=jax.ShapeDtypeStruct((count + 8, sums.shape[0] * 8), jnp.float32),
        in_specs=[vmem()] * 3,
        out_specs=vmem(),
        compiler_params=params(8),
        name="products",
    )(own, sums, got)


def attend_kernel(
    place, base_query, p0, p1, p2, p3, sums, got, gain, key_new, value_new, s0, s1, s2,
    s3, own_sum, old_down, old_up, keys, values, out, new_down, new_up, queries, results,
):
    t = place[0]
    rows_here = keys.shape[0]
    count, width = base_query.shape
    heads = width // HEAD
    steps = count // rows_here
    per_row = steps * heads
    half = width // 2

    both = (p0[...] + p1[...]) + (p2[...] + p3[...])
    product = both[:count, :]
    overall = both[count : count + 1, :]
    clip = RATE * (1.0 / jnp.maximum(jnp.sqrt(overall), 1.0))
    lanes = product.shape[1]
    lane = lax.broadcasted_iota(jnp.int32, product.shape, 1) % 8
    updated = pltpu.roll(product, lanes - 1, 1) - clip * product
    updated = jnp.where((lane == 0) | (lane == 2), updated, 0.0)
    clip = clip[:, :1]
    high, low = old_factors(got, half)
    old = high.astype(jnp.float32) + low.astype(jnp.float32)
    rows = (old - clip[None] * sums[...]).reshape(-1, half)
    row_high, row_low = split(rows)
    for h in (0, 1):
        left_high, left_low = split(pltpu.roll(updated, 4 + h, 1))
        change = dot_nn(left_high, row_high) + dot_nn(left_low, row_high)
        change += dot_nn(left_high, row_low)
        query = base_query[:, h * half : (h + 1) * half] + ADAPTER_SCALING * change
        for j in range(heads // 2):
            part = query[:, j * HEAD : (j + 1) * HEAD]
            scale = lax.rsqrt(jnp.mean(part * part, axis=1, keepdims=True) + EPSILON)
            part = (part * scale * gain[...]).astype(jnp.bfloat16).astype(jnp.float32)
            for s in range(steps):
                at = s * heads + h * (heads // 2) + j
                queries[pl.ds(at, rows_here, stride=per_row), :] = part[
                    s * rows_here : (s + 1) * rows_here
                ]

    inverse = 1.0 / math.sqrt(HEAD)
    new_lane = lax.broadcasted_iota(jnp.int32, (per_row, count), 1)
    step = lax.broadcasted_iota(jnp.int32, (per_row, count), 0) // heads
    seen = new_lane // rows_here <= step
    query = queries[...].astype(jnp.bfloat16)
    own = [slice(row * per_row, (row + 1) * per_row) for row in range(rows_here)]
    fresh = dot_nt(query, key_new[...]) * inverse
    old, new = [], []
    for row in range(rows_here):
        old.append(dot_nn(query[own[row]], keys[row]) * inverse)
        new.append(jnp.where((new_lane % rows_here == row) & seen, fresh[own[row]], -jnp.inf))
    for row in range(rows_here):
        top = jnp.maximum(
            jnp.max(old[row], axis=1, keepdims=True), jnp.max(new[row], axis=1, keepdims=True)
        )
        old[row], new[row] = jnp.exp(old[row] - top), jnp.exp(new[row] - top)
    for row in range(rows_here):
        total = jnp.sum(old[row], axis=1, keepdims=True) + jnp.sum(new[row], axis=1, keepdims=True)
        share = 1.0 / total
        old[row] = (old[row] * share).astype(jnp.bfloat16)
        new[row] = (new[row] * share).astype(jnp.bfloat16)
    for row in range(rows_here):
        results[own[row], :] = dot_nn(old[row], values[row]) + dot_nn(new[row], value_new[...])

    for h in range(heads):
        parts = [results[pl.ds(s * heads + h, rows_here, stride=per_row), :] for s in range(steps)]
        out[:, h * HEAD : (h + 1) * HEAD] = jnp.concatenate(parts, 0).astype(jnp.bfloat16)

    for k, block in enumerate((s0, s1, s2, s3)):
        columns = pl.ds(pl.multiple_of((t ^ k) * width, width), width)
        part = block[count : count + 16, :].astype(jnp.float32)
        summed = (part[0:2] + part[2:4]) + part[4:6]
        new_down[:, columns] = old_down[:, columns] - clip * summed
    up = own_sum[...]
    for i in (0, 1):
        for h in (0, 1):
            columns = slice(h * half, (h + 1) * half)
            value = up[4 + 2 * i + h : 5 + 2 * i + h, :]
            new_up[i : i + 1, columns] = old_up[i : i + 1, columns] - clip * value


def attend(place, *arrays):
    base_query = arrays[0]
    count, width = base_query.shape
    old_down, old_up = arrays[-4:-2]
    return pl.pallas_call(
        attend_kernel,
        out_shape=(
            jax.ShapeDtypeStruct((count, width), jnp.bfloat16),
            jax.ShapeDtypeStruct(old_down.shape, jnp.float32),
            jax.ShapeDtypeStruct(old_up.shape, jnp.float32),
        ),
        in_specs=[smem()] + [vmem()] * len(arrays),
        out_specs=(vmem(), vmem(), vmem()),
        scratch_shapes=[
            pltpu.VMEM((count * width // HEAD, HEAD), jnp.float32),
            pltpu.VMEM((count * width // HEAD, HEAD), jnp.float32),
        ],
        compiler_params=params(16),
        name="attend",
    )(place, *arrays)


def tensor_swap(values, bit):
    size = lax.axis_size("tensor")
    return lax.ppermute(values, "tensor", [(i, i ^ bit) for i in range(size)])


def body(
    token_ids,
    embed_table,
    norm_gain,
    query_gain,
    key_gain,
    base_query_weight,
    pair_weight,
    past_pairs,
    down_factor,
    up_factor,
    grad_down,
    grad_up,
    group_scale,
    learner_group,
):
    groups = lax.axis_size("dp")
    t = lax.axis_index("tensor")
    me = lax.axis_index("dp")
    width = embed_table.shape[1]
    half = width // 2
    pair_index = t * (width // HEAD) // (HEADS // KVH)
    place = jnp.stack([t, pair_index, me]).astype(jnp.int32)
    rows_here, context = past_pairs.shape[:2]
    steps = token_ids.shape[0]
    count = steps * rows_here

    sent, pick, rounds = send(
        place, token_ids, embed_table, grad_down, grad_up, down_factor, up_factor, groups
    )
    got = lax.all_to_all(sent.reshape(groups, CAP, -1), "dp", 0, 0, tiled=True)

    def later_round(state):
        r, rows = state
        sent, pick = again(place, (r * CAP).reshape(1), token_ids, embed_table, groups)
        back = lax.all_to_all(sent.reshape(groups, CAP, -1), "dp", 0, 0, tiled=True)
        found = lax.dot_general(
            pick,
            back.reshape(groups * CAP, width),
            (((0,), (0,)), ((), ())),
            preferred_element_type=jnp.float32,
        )
        return r + 1, rows + found.astype(jnp.bfloat16)

    _, extra = lax.while_loop(
        lambda s: s[0] < rounds[0],
        later_round,
        (jnp.int32(1), jnp.zeros((count, width), jnp.bfloat16)),
    )
    cache = past_pairs.reshape(rows_here, context, KVH, 2, HEAD).transpose(0, 1, 3, 2, 4)
    cache = cache.reshape(rows_here, context * KVH * 2, HEAD)
    keys, values = stage(place, cache, pick)
    pick, keys, values = lax.optimization_barrier((pick, keys, values))
    block, own_sum, sums = gather(group_scale, learner_group, got, pick, extra)
    sums = lax.all_to_all(sums, "dp", 0, 0, tiled=True)

    blocks = [block] + [tensor_swap(block, bit) for bit in (1, 2, 3)]
    normed, own = norm(place, blocks, norm_gain, count)

    key_new, value_new = pair_products(place, normed, key_gain, pair_weight)
    query = jnp.dot(normed, base_query_weight, preferred_element_type=jnp.float32)
    own, query, key_new = lax.optimization_barrier((own, query, key_new))

    part = products(own, sums, got)
    keys, values = fetch(place, keys, values, part)
    parts = [part] + [tensor_swap(part, bit) for bit in (1, 2, 3)]
    attended, new_down, new_up = attend(
        place, query, *parts, sums, got, query_gain.reshape(1, -1), key_new, value_new,
        *blocks, own_sum, down_factor, up_factor, keys, values,
    )
    return attended.reshape(steps, rows_here, width), new_down, new_up


def solution(mesh):
    in_specs = (
        P(),
        P("dp", "tensor"),
        P(),
        P(),
        P(),
        P(None, "tensor"),
        P(),
        P("dp", None, None, None),
        P("dp", None),
        P("dp", "tensor"),
        P("dp", None, None),
        P("dp", None, "tensor"),
        P(),
        P(),
    )
    out_specs = (P(None, "dp", "tensor"), P("dp", None), P("dp", "tensor"))
    return jax.shard_map(body, mesh=mesh, in_specs=in_specs, out_specs=out_specs, check_vma=False)
```

time: 1220 us -> 69.6 us (0.06); the launches traced: 1200 us -> 69.2 us
  waiting for transfers between devices: 799 us -> 15.6 us
  blocking collectives: 286 us -> 0 us
  matrix products: 53.4 us -> 5.09 us
  local copies, waits for them, and re-layouts: 27.2 us -> 1.99 us
  starting transfers between devices: 0.43 us -> 25.3 us
  Pallas kernels: 0 us -> 19.5 us
  other arithmetic: 16.8 us -> 0.08 us
  between operations: 17.4 us -> 0.92 us
    reduce_scatter x4 -> x0, waiting for transfers between devices: 471 us -> none  [lookup(): lax.psum_scatter(partial_rows.astype(jnp.bfloat16), 'dp', scatter_dimensi...]
    unnamed x7 -> x0, waiting for transfers between devices: 274 us -> none
    all_gather x5 -> x0, blocking collectives: 199 us -> none  [the longest x4 132 us: lookup(): return lax.all_gather(own_rows, 'tensor', axis=2, tiled=True)]
    psum x1 -> x0, blocking collectives: 86.6 us -> none  [clip_factor(): overall = lax.psum(own_square, ('dp', 'tensor'))]
    all_gather x1 -> x0, waiting for transfers between devices: 53.6 us -> none  [body(): lax.all_gather(new_down, 'dp', axis=0, tiled=True)]
    dot_general x28 -> x1, matrix products: 53.4 us -> 5.09 us  [body(): jnp.dot(normed, base_query_weight, preferred_element_type=jnp.float32)]
    pallas_call x0 -> x8, Pallas kernels: none -> 19.5 us  [the longest x1 5.48 us: send(): pl.pallas_call(send_kernel, out_shape=(jax.ShapeDtypeStruct((groups * CAP...]
    unnamed x69 -> x30, local copies, waits for them, and re-layouts: 17.4 us -> 1.99 us
  transfers between devices with their start and end apart: 6 -> 8, of which waited for: 6 -> 3; matrix products, arithmetic and copies ran while one was open for 5% -> 7% of each run, Pallas kernels for 0% -> 13%
where the time goes in v2:
time: 69.6 us; the launch traced here: 69.2 us
  starting transfers between devices  25.3 us (36%)
  Pallas kernels  19.5 us (28%)
  waiting for transfers between devices  15.6 us (22%)
  matrix products  5.09 us (7%)
  local copies, waits for them, and re-layouts  1.99 us (3%)
  between operations  0.92 us (1%)
    all_to_all x1, waiting for transfers between devices, body(): got = lax.all_to_all(sent.reshape(groups, CAP, -1), 'dp', 0, 0, tiled=True)  13.5 us
    ppermute x6, starting transfers between devices, tensor_swap(): return lax.ppermute(values, 'tensor', [(i, i ^ bit) for i in range(size)])  10.7 us
    all_to_all x1, starting transfers between devices, body(): got = lax.all_to_all(sent.reshape(groups, CAP, -1), 'dp', 0, 0, tiled=True)  9.96 us
    pallas_call x1, Pallas kernels, send(): pl.pallas_call(send_kernel, out_shape=(jax.ShapeDtypeStruct((groups * CAP...  5.48 us
    dot_general x1, matrix products, body(): jnp.dot(normed, base_query_weight, preferred_element_type=jnp.float32)  5.09 us
    all_to_all x1, starting transfers between devices, body(): sums = lax.all_to_all(sums, 'dp', 0, 0, tiled=True)  4.71 us
    pallas_call x1, Pallas kernels, stage(): pl.pallas_call(stage_kernel, out_shape=[keys, values], in_specs=[smem(),...  3.9 us
    pallas_call x1, Pallas kernels, pair_products(): pl.pallas_call(pair_kernel, out_shape=(fresh, fresh), in_specs=[smem(), v...  3.72 us
  transfers between devices with their start and end apart: 8, of which 3 were waited for; matrix products, arithmetic and copies ran while one was open for 7% of the time, Pallas kernels for 13%

profile of v2, /device:TPU:1, one launch (start us, length us, event | category | flops | bytes accessed | tf_op | source)
XLA Modules:
  0.0 69.2 jit_solution(3915975609194542004)
XLA Ops:
  0.6 0.0 copy-start.12
  0.7 0.1 pad_add_fusion.place
  0.7 5.5 %send.1 = (bf16[256,2560]{1,0:T(8,128)(2,1)}, bf16[256,32]{1,0:T(8,128)(2,1)}, s32[1]{0:T(128)}) custom-call(s32[3]{0:T(128)S(1)} %pad_add_fusion.place, s32[4,256]{1,0:T(4,128)} %tokens_at.1, bf16[2374,1024]{1,0:T(8,128)(2,1)} %table_at.1, bf16[1,64,4096]{2,1,0:T(8,128)(2,1)} %grad_down_at.1, bf16[1,64,1024]{2,1,0:T(8,128)(2,1)} %grad_up_at.1, ...), custom_call_target="tpu_custom_call" | custom-call | tf_op jit(solution)/shard_map/send/pallas_call | solution.py:187
  6.2 0.0 copy-done.12
  6.2 0.7 while.10
  6.9 0.0 copy-start.13
  6.9 0.0 copy-start.4
  6.9 0.0 copy-start.9
  6.9 0.0 copy-start.10
  7.0 0.0 copy-start.6
  7.0 10.0 %all-to-all-start.1 = ((bf16[32,8,2560]{2,1,0:T(8,128)(2,1)}), bf16[32,8,2560]{2,1,0:T(8,128)(2,1)S(1)}, u32[]{:S(2)}, u32[]{:S(2)}) async-start(bf16[32,8,2560]{2,1,0:T(8,128)(2,1)} %bitcast.34), calls=%async_computation.1 | async-start | bytes 2621440 | tf_op jit(solution)/shard_map/all_to_all | solution.py:573
  16.9 3.9 %stage.1 = (bf16[8,128,512]{2,1,0:T(8,128)(2,1)}, bf16[8,512,128]{2,1,0:T(8,128)(2,1)}) custom-call(s32[3]{0:T(128)S(1)} %get-tuple-element.184, bf16[8,2048,128]{2,1,0:T(8,128)(2,1)} %bitcast.33), custom_call_target="tpu_custom_call" | custom-call | bytes 8388608 | tf_op jit(solution)/shard_map/stage/pallas_call | solution.py:299
  20.8 13.5 %all-to-all-done.1.got = bf16[32,8,2560]{2,1,0:T(8,128)(2,1)S(1)} async-done(((bf16[32,8,2560]{2,1,0:T(8,128)(2,1)}), bf16[32,8,2560]{2,1,0:T(8,128)(2,1)S(1)}, u32[]{:S(2)}, u32[]{:S(2)}) %all-to-all-start.1) | async-done | bytes 1310752 | tf_op jit(solution)/shard_map/all_to_all | solution.py:573
  34.4 0.0 copy-done.4
  34.4 0.0 copy-done.9
  34.4 0.0 copy-done.10
  34.4 1.5 %gather.1 = (bf16[48,1024]{1,0:T(8,128)(2,1)S(1)}, f32[8,512]{1,0:T(8,128)S(1)}, f32[32,8,512]{2,1,0:T(8,128)}) custom-call(f32[32]{0:T(128)S(1)} %copy-done.9, s32[32]{0:T(128)S(1)} %copy-done.10, bf16[32,8,2560]{2,1,0:T(8,128)(2,1)S(1)} %all-to-all-done.1.got, bf16[256,32]{1,0:T(8,128)(2,1)S(1)} %copy-done.4, bf16[32,1024]{1,0:T(8,128)(2,1)S(1)} %get-tuple-element.70.extra), custom_call_target="tpu_custom_call" | custom-call | tf_op jit(solution)/shard_map/gather/pallas_call | solution.py:260
  35.9 5.3 %collective-permute-start.2 = (bf16[48,1024]{1,0:T(8,128)(2,1)S(1)}, bf16[48,1024]{1,0:T(8,128)(2,1)S(1)}, u32[]{:S(2)}, u32[]{:S(2)}) collective-permute-start(bf16[48,1024]{1,0:T(8,128)(2,1)S(1)} %get-tuple-element.71.e0.s0), channel_id=1, source_target_pairs={{0,3},{1,2},{2,1},{3,0},{4,7},{5,6},{6,5},{7,4},{8,11},{9,10},{10,... | collective-permute-start | bytes 294920 | tf_op jit(solution)/shard_map/ppermute | solution.py:540
  41.2 0.5 collective-permute-start.1
  41.7 0.0 collective-permute-start
  41.7 4.7 %all-to-all-start.2 = ((f32[32,8,512]{2,1,0:T(8,128)}), f32[32,8,512]{2,1,0:T(8,128)S(1)}, u32[]{:S(2)}, u32[]{:S(2)}) async-start(f32[32,8,512]{2,1,0:T(8,128)} %get-tuple-element.77), calls=%async_computation.2 | async-start | bytes 1048576 | tf_op jit(solution)/shard_map/all_to_all | solution.py:597
  46.4 0.0 collective-permute-done.2.e3.s3
  46.4 0.2 collective-permute-done.1.e2.s2
  46.6 0.0 collective-permute-done.e1.s1
  46.6 0.0 copy-done.6
  46.7 0.7 %norm.1 = (bf16[32,4096]{1,0:T(8,128)(2,1)S(1)}, bf16[32,1024]{1,0:T(8,128)(2,1)S(1)}) custom-call(s32[3]{0:T(128)S(1)} %get-tuple-element.184, bf16[48,1024]{1,0:T(8,128)(2,1)S(1)} %get-tuple-element.71.e0.s0, bf16[48,1024]{1,0:T(8,128)(2,1)S(1)} %collective-permute-done.e1.s1, bf16[48,1024]{1,0:T(8,128)(2,1)S(1)} %collective-permute-done.1.e2.s2, ...), custom_call_target="tpu_custom_call" | custom-call | tf_op jit(solution)/shard_map/norm/pallas_call | solution.py:386
  47.4 0.7 copy-done
  48.1 3.7 %pair_products.1 = (bf16[32,128]{1,0:T(8,128)(2,1)}, bf16[32,128]{1,0:T(8,128)(2,1)}) custom-call(s32[3]{0:T(128)S(1)} %get-tuple-element.184, bf16[32,4096]{1,0:T(8,128)(2,1)} %copy-done, f32[1,128]{1,0:T(1,128)} %bitcast.35, bf16[2,4096,256]{2,1,0:T(8,128)(2,1)} %pair_at.1), custom_call_target="tpu_custom_call" | custom-call | bytes 8388608 | tf_op jit(solution)/shard_map/pair_products/pallas_call | solution.py:330
  51.8 0.0 copy-start.1
  51.8 0.0 copy-start.14
  51.8 0.0 copy-start.3
  51.8 0.0 copy-start.5
  51.9 0.0 copy-start.7
  51.9 0.0 copy-start.8
  51.9 0.0 copy-start.11
  51.9 5.1 %fusion.2.base_query = f32[32,1024]{1,0:T(8,128)S(1)} fusion(bf16[32,4096]{1,0:T(8,128)(2,1)} %copy-done, bf16[4096,1024]{1,0:T(8,128)(2,1)} %param.21), kind=kOutput, calls=%fused_computation.4 | convolution fusion | flops 268435456 | bytes 8781824 | tf_op jit(solution)/shard_map/dot_general | solution.py:603
  57.0 0.0 all-to-all-done.2.sums
  57.0 0.8 %products.1.p0 = f32[40,256]{1,0:T(8,128)S(1)} custom-call(bf16[32,1024]{1,0:T(8,128)(2,1)S(1)} %get-tuple-element.76.own, f32[32,8,512]{2,1,0:T(8,128)S(1)} %all-to-all-done.2.sums, bf16[32,8,2560]{2,1,0:T(8,128)(2,1)S(1)} %all-to-all-done.1.got), custom_call_target="tpu_custom_call" | custom-call | tf_op jit(solution)/shard_map/products/pallas_call | solution.py:425
  57.8 4.3 %collective-permute-start.5 = (f32[40,256]{1,0:T(8,128)S(1)}, f32[40,256]{1,0:T(8,128)S(1)}, u32[]{:S(2)}, u32[]{:S(2)}) collective-permute-start(f32[40,256]{1,0:T(8,128)S(1)} %products.1.p0), channel_id=1, source_target_pairs={{0,3},{1,2},{2,1},{3,0},{4,7},{5,6},{6,5},{7,4},{8,11},{9,10},{10,... | collective-permute-start | bytes 122888 | tf_op jit(solution)/shard_map/ppermute | solution.py:540
  62.1 0.5 collective-permute-start.4
  62.7 0.0 collective-permute-start.3
  62.7 1.2 %copy-done.2 = bf16[8,512,128]{2,1,0:T(8,128)(2,1)S(1)} copy-done((bf16[8,512,128]{2,1,0:T(8,128)(2,1)S(1)}, bf16[8,512,128]{2,1,0:T(8,128)(2,1)}, u32[]{:S(2)}) %copy-start.2) | copy-done | bytes 1048600
  63.9 0.7 %fetch.1 = (bf16[8,128,512]{2,1,0:T(8,128)(2,1)S(1)}, bf16[8,512,128]{2,1,0:T(8,128)(2,1)S(1)}) custom-call(s32[3]{0:T(128)S(1)} %copy-done.14, bf16[8,128,512]{2,1,0:T(8,128)(2,1)S(1)} %copy-done.1, bf16[8,512,128]{2,1,0:T(8,128)(2,1)S(1)} %copy-done.2), custom_call_target="tpu_custom_call" | custom-call | bytes 4194304 | tf_op jit(solution)/shard_map/fetch/pallas_call | solution.py:358
  64.6 0.0 collective-permute-done.5.p3
  64.6 1.9 %collective-permute-done.4.p2 = f32[40,256]{1,0:T(8,128)S(1)} collective-permute-done((f32[40,256]{1,0:T(8,128)S(1)}, f32[40,256]{1,0:T(8,128)S(1)}, u32[]{:S(2)}, u32[]{:S(2)}) %collective-permute-start.4) | collective-permute-done | bytes 40992 | tf_op jit(solution)/shard_map/ppermute | solution.py:540
  66.5 0.0 collective-permute-done.3.p1
  66.5 0.0 copy-done.5
  66.5 2.6 %attend.1 = (bf16[32,1024]{1,0:T(8,128)(2,1)}, f32[2,4096]{1,0:T(2,128)}, f32[2,1024]{1,0:T(2,128)}) custom-call(s32[3]{0:T(128)S(1)} %copy-done.14, f32[32,1024]{1,0:T(8,128)S(1)} %fusion.2.base_query, f32[40,256]{1,0:T(8,128)S(1)} %products.1.p0, f32[40,256]{1,0:T(8,128)S(1)} %collective-permute-done.3.p1, f32[40,256]{1,0:T(8,128)S(1)} %collective-permute-done.4.p2, ...), custom_call_target="tpu_custom_call" | custom-call | tf_op jit(solution)/shard_map/attend/pallas_call | solution.py:520
  (10 shorter events, 0.0 us)
Async XLA Ops:
  0.6 5.6 %copy-start.12 = (s32[4,256]{1,0:T(4,128)S(1)}, s32[4,256]{1,0:T(4,128)}, u32[]{:S(2)}) copy-start(s32[4,256]{1,0:T(4,128)} %tokens_at.1) | copy-start | bytes 12292
  6.9 41.2 %copy-start.13 = (s32[3]{0:T(128)}, s32[3]{0:T(128)S(1)}, u32[]{:S(2)}) copy-start(s32[3]{0:T(128)S(1)} %get-tuple-element.184) | copy-start | bytes 40
  6.9 27.5 %copy-start.4 = (bf16[256,32]{1,0:T(8,128)(2,1)S(1)}, bf16[256,32]{1,0:T(8,128)(2,1)}, u32[]{:S(2)}) copy-start(bf16[256,32]{1,0:T(8,128)(2,1)} %get-tuple-element.68.pick) | copy-start | bytes 49156
  6.9 27.4 %copy-start.9 = (f32[32]{0:T(128)S(1)}, f32[32]{0:T(128)}, u32[]{:S(2)}) copy-start(f32[32]{0:T(128)} %scale.1) | copy-start | bytes 388
  6.9 27.4 %copy-start.10 = (s32[32]{0:T(128)S(1)}, s32[32]{0:T(128)}, u32[]{:S(2)}) copy-start(s32[32]{0:T(128)} %learner.1) | copy-start | bytes 388
  7.0 39.7 %copy-start.6 = (f32[4096]{0:T(1024)S(1)}, f32[4096]{0:T(1024)}, u32[]{:S(2)}) copy-start(f32[4096]{0:T(1024)} %param.18) | copy-start | bytes 49156
  7.0 27.4 %all-to-all-start.1 = ((bf16[32,8,2560]{2,1,0:T(8,128)(2,1)}), bf16[32,8,2560]{2,1,0:T(8,128)(2,1)S(1)}, u32[]{:S(2)}, u32[]{:S(2)}) async-start(bf16[32,8,2560]{2,1,0:T(8,128)(2,1)} %bitcast.34), calls=%async_computation.1 | async-start | bytes 2621440 | tf_op jit(solution)/shard_map/all_to_all | solution.py:573
  35.9 10.5 %collective-permute-start.2 = (bf16[48,1024]{1,0:T(8,128)(2,1)S(1)}, bf16[48,1024]{1,0:T(8,128)(2,1)S(1)}, u32[]{:S(2)}, u32[]{:S(2)}) collective-permute-start(bf16[48,1024]{1,0:T(8,128)(2,1)S(1)} %get-tuple-element.71.e0.s0), channel_id=1, source_target_pairs={{0,3},{1,2},{2,1},{3,0},{4,7},{5,6},{6,5},{7,4},{8,11},{9,10},{10,... | collective-permute-start | bytes 294920 | tf_op jit(solution)/shard_map/ppermute | solution.py:540
  41.2 5.5 %collective-permute-start.1 = (bf16[48,1024]{1,0:T(8,128)(2,1)S(1)}, bf16[48,1024]{1,0:T(8,128)(2,1)S(1)}, u32[]{:S(2)}, u32[]{:S(2)}) collective-permute-start(bf16[48,1024]{1,0:T(8,128)(2,1)S(1)} %get-tuple-element.71.e0.s0), channel_id=1, source_target_pairs={{0,2},{1,3},{2,0},{3,1},{4,6},{5,7},{6,4},{7,5},{8,10},{9,11},{10,... | collective-permute-start | bytes 294920 | tf_op jit(solution)/shard_map/ppermute | solution.py:540
  41.7 4.9 %collective-permute-start = (bf16[48,1024]{1,0:T(8,128)(2,1)S(1)}, bf16[48,1024]{1,0:T(8,128)(2,1)S(1)}, u32[]{:S(2)}, u32[]{:S(2)}) collective-permute-start(bf16[48,1024]{1,0:T(8,128)(2,1)S(1)} %get-tuple-element.71.e0.s0), channel_id=1, source_target_pairs={{0,1},{1,0},{2,3},{3,2},{4,5},{5,4},{6,7},{7,6},{8,9},{9,8},{10,11... | collective-permute-start | bytes 294920 | tf_op jit(solution)/shard_map/ppermute | solution.py:540
  41.7 15.3 %all-to-all-start.2 = ((f32[32,8,512]{2,1,0:T(8,128)}), f32[32,8,512]{2,1,0:T(8,128)S(1)}, u32[]{:S(2)}, u32[]{:S(2)}) async-start(f32[32,8,512]{2,1,0:T(8,128)} %get-tuple-element.77), calls=%async_computation.2 | async-start | bytes 1048576 | tf_op jit(solution)/shard_map/all_to_all | solution.py:597
  47.4 0.7 %copy-start = (bf16[32,4096]{1,0:T(8,128)(2,1)}, bf16[32,4096]{1,0:T(8,128)(2,1)S(1)}, u32[]{:S(2)}) copy-start(bf16[32,4096]{1,0:T(8,128)(2,1)S(1)} %get-tuple-element.73.normed) | copy-start | bytes 786436
  51.8 10.9 %copy-start.1 = (bf16[8,128,512]{2,1,0:T(8,128)(2,1)S(1)}, bf16[8,128,512]{2,1,0:T(8,128)(2,1)}, u32[]{:S(2)}) copy-start(bf16[8,128,512]{2,1,0:T(8,128)(2,1)} %get-tuple-element.82.keys_at) | copy-start | bytes 3145732
  51.8 10.8 %copy-start.14 = (s32[3]{0:T(128)S(1)}, s32[3]{0:T(128)}, u32[]{:S(2)}) copy-start(s32[3]{0:T(128)} %copy-done.13) | copy-start | bytes 40
  51.8 14.7 %copy-start.3 = (f32[2,4096]{1,0:T(2,128)S(1)}, f32[2,4096]{1,0:T(2,128)}, u32[]{:S(2)}) copy-start(f32[2,4096]{1,0:T(2,128)} %old_down.1) | copy-start | bytes 98308
  51.8 14.7 %copy-start.5 = (f32[2,1024]{1,0:T(2,128)S(1)}, f32[2,1024]{1,0:T(2,128)}, u32[]{:S(2)}) copy-start(f32[2,1024]{1,0:T(2,128)} %old_up.1) | copy-start | bytes 24580
  51.9 14.7 %copy-start.7 = (bf16[32,128]{1,0:T(8,128)(2,1)S(1)}, bf16[32,128]{1,0:T(8,128)(2,1)}, u32[]{:S(2)}) copy-start(bf16[32,128]{1,0:T(8,128)(2,1)} %get-tuple-element.78.key_new) | copy-start | bytes 24580
  51.9 14.7 %copy-start.8 = (bf16[32,128]{1,0:T(8,128)(2,1)S(1)}, bf16[32,128]{1,0:T(8,128)(2,1)}, u32[]{:S(2)}) copy-start(bf16[32,128]{1,0:T(8,128)(2,1)} %get-tuple-element.79.value_new) | copy-start | bytes 24580
  51.9 14.7 %copy-start.11 = (f32[128]{0:T(128)S(1)}, f32[128]{0:T(128)}, u32[]{:S(2)}) copy-start(f32[128]{0:T(128)} %param.19) | copy-start | bytes 1540
  57.8 6.8 %collective-permute-start.5 = (f32[40,256]{1,0:T(8,128)S(1)}, f32[40,256]{1,0:T(8,128)S(1)}, u32[]{:S(2)}, u32[]{:S(2)}) collective-permute-start(f32[40,256]{1,0:T(8,128)S(1)} %products.1.p0), channel_id=1, source_target_pairs={{0,3},{1,2},{2,1},{3,0},{4,7},{5,6},{6,5},{7,4},{8,11},{9,10},{10,... | collective-permute-start | bytes 122888 | tf_op jit(solution)/shard_map/ppermute | solution.py:540
  62.1 4.4 %collective-permute-start.4 = (f32[40,256]{1,0:T(8,128)S(1)}, f32[40,256]{1,0:T(8,128)S(1)}, u32[]{:S(2)}, u32[]{:S(2)}) collective-permute-start(f32[40,256]{1,0:T(8,128)S(1)} %products.1.p0), channel_id=1, source_target_pairs={{0,2},{1,3},{2,0},{3,1},{4,6},{5,7},{6,4},{7,5},{8,10},{9,11},{10,... | collective-permute-start | bytes 122888 | tf_op jit(solution)/shard_map/ppermute | solution.py:540
  62.7 3.8 %collective-permute-start.3 = (f32[40,256]{1,0:T(8,128)S(1)}, f32[40,256]{1,0:T(8,128)S(1)}, u32[]{:S(2)}, u32[]{:S(2)}) collective-permute-start(f32[40,256]{1,0:T(8,128)S(1)} %products.1.p0), channel_id=1, source_target_pairs={{0,1},{1,0},{2,3},{3,2},{4,5},{5,4},{6,7},{7,6},{8,9},{9,8},{10,11... | collective-permute-start | bytes 122888 | tf_op jit(solution)/shard_map/ppermute | solution.py:540
  62.7 1.2 %copy-start.2 = (bf16[8,512,128]{2,1,0:T(8,128)(2,1)S(1)}, bf16[8,512,128]{2,1,0:T(8,128)(2,1)}, u32[]{:S(2)}) copy-start(bf16[8,512,128]{2,1,0:T(8,128)(2,1)} %get-tuple-element.83.values_at) | copy-start | bytes 3145732

commit v3 on v2

--- a/solution.py
+++ b/solution.py
@@ -170,9 +170,8 @@
         taken = jnp.where((source == wanted) & (row % 2 == h), 1.0, 0.0).astype(jnp.bfloat16)
         moved += dot_nn(taken, grads[:, h * half : (h + 1) * half])
     sent[:, width : width + half] = moved.astype(jnp.bfloat16)
-    for i, part in enumerate(split(fold(down[:, columns], up[...]))):
-        part = jnp.broadcast_to(part[None], (groups, 8, half)).reshape(groups * 8, half)
-        sent[:, width + (1 + i) * half : width + (2 + i) * half] = part
+    rows = fold(down[:, columns], up[...]).astype(jnp.bfloat16)
+    sent[:, width + half :] = jnp.broadcast_to(rows[None], (groups, 8, half)).reshape(-1, half)
 
     hot = one_hot(chosen, vocab_rows)
     for i, at in enumerate(spans):
@@ -187,7 +186,7 @@
     return pl.pallas_call(
         send_kernel,
         out_shape=(
-            jax.ShapeDtypeStruct((groups * CAP, width * 5 // 2), jnp.bfloat16),
+            jax.ShapeDtypeStruct((groups * CAP, width * 2), jnp.bfloat16),
             jax.ShapeDtypeStruct((groups * CAP, count), jnp.bfloat16),
             jax.ShapeDtypeStruct((1,), jnp.int32),
         ),
@@ -396,10 +395,6 @@
     )(place, *blocks, gain.reshape(1, -1))
 
 
-def old_factors(got, half):
-    return got[:, :, 3 * half : 4 * half], got[:, :, 4 * half :]
-
-
 def products_kernel(own, sums, got, out):
     count = own.shape[0]
     half = sums.shape[2]
@@ -413,8 +408,7 @@
         return jnp.where((lane % 8 == 0) | (lane % 8 == 2), mixed, 0.0)
 
     rows = sums[...].reshape(-1, half)
-    high, low = old_factors(got, half)
-    old = combine([high.reshape(-1, half), low.reshape(-1, half)])
+    old = combine([got[:, :, 3 * half :].reshape(-1, half)])
     new = combine(split(rows))
     out[:count, :] = new + pltpu.roll(old, 1, 1)
     out[count:, :] = jnp.full((8, rows.shape[0]), jnp.sum(rows * rows), jnp.float32)
@@ -453,8 +447,7 @@
     updated = pltpu.roll(product, lanes - 1, 1) - clip * product
     updated = jnp.where((lane == 0) | (lane == 2), updated, 0.0)
     clip = clip[:, :1]
-    high, low = old_factors(got, half)
-    old = high.astype(jnp.float32) + low.astype(jnp.float32)
+    old = got[:, :, 3 * half :].astype(jnp.float32)
     rows = (old - clip[None] * sums[...]).reshape(-1, half)
     row_high, row_low = split(rows)
     for h in (0, 1):
@@ -575,14 +568,18 @@
     def later_round(state):
         r, rows = state
         sent, pick = again(place, (r * CAP).reshape(1), token_ids, embed_table, groups)
-        back = lax.all_to_all(sent.reshape(groups, CAP, -1), "dp", 0, 0, tiled=True)
-        found = lax.dot_general(
-            pick,
-            back.reshape(groups * CAP, width),
-            (((0,), (0,)), ((), ())),
-            preferred_element_type=jnp.float32,
-        )
-        return r + 1, rows + found.astype(jnp.bfloat16)
+        for k in range(groups):
+            there, source = (me + k) % groups * CAP, (me - k) % groups * CAP
+            part = lax.dynamic_slice_in_dim(sent, there, CAP, 0)
+            if k:
+                ring = [(i, (i + k) % groups) for i in range(groups)]
+                part = lax.ppermute(part, "dp", ring)
+            wanted = lax.dynamic_slice_in_dim(pick, source, CAP, 0)
+            found = lax.dot_general(
+                wanted, part, (((0,), (0,)), ((), ())), preferred_element_type=jnp.float32
+            )
+            rows = rows + found.astype(jnp.bfloat16)
+        return r + 1, rows
 
     _, extra = lax.while_loop(
         lambda s: s[0] < rounds[0],

time: 69.6 us -> 65.7 us (0.944)
  waiting for transfers between devices: 15.6 us -> 10.6 us
  between operations: 0.92 us -> 2.28 us
    all_to_all x1, waiting for transfers between devices: 13.5 us -> 8.59 us  [body(): got = lax.all_to_all(sent.reshape(groups, CAP, -1), 'dp', 0, 0, tiled=True)]
    unnamed x30 -> x26, local copies, waits for them, and re-layouts: 1.99 us -> 1.98 us
  transfers between devices with their start and end apart: 8 -> 8, of which waited for: 3 -> 3; matrix products, arithmetic and copies ran while one was open for 7% -> 8% of each run, Pallas kernels for 13% -> 14%
where the time goes in v3:
time: 65.7 us; the launch traced here: 65.2 us
  starting transfers between devices  25.1 us (38%)
  Pallas kernels  19.3 us (29%)
  waiting for transfers between devices  10.6 us (16%)
  matrix products  5.09 us (8%)
  between operations  2.28 us (3%)
  local copies, waits for them, and re-layouts  1.98 us (3%)
  loops' own time  0.87 us (1%)
    ppermute x6, starting transfers between devices, tensor_swap(): return lax.ppermute(values, 'tensor', [(i, i ^ bit) for i in range(size)])  10.5 us
    all_to_all x1, starting transfers between devices, body(): got = lax.all_to_all(sent.reshape(groups, CAP, -1), 'dp', 0, 0, tiled=True)  9.82 us
    all_to_all x1, waiting for transfers between devices, body(): got = lax.all_to_all(sent.reshape(groups, CAP, -1), 'dp', 0, 0, tiled=True)  8.59 us
    pallas_call x1, Pallas kernels, send(): pl.pallas_call(send_kernel, out_shape=(jax.ShapeDtypeStruct((groups * CAP...  5.37 us
    dot_general x1, matrix products, body(): jnp.dot(normed, base_query_weight, preferred_element_type=jnp.float32)  5.09 us
    all_to_all x1, starting transfers between devices, body(): sums = lax.all_to_all(sums, 'dp', 0, 0, tiled=True)  4.81 us
    pallas_call x1, Pallas kernels, stage(): pl.pallas_call(stage_kernel, out_shape=[keys, values], in_specs=[smem(),...  3.92 us
    pallas_call x1, Pallas kernels, pair_products(): pl.pallas_call(pair_kernel, out_shape=(fresh, fresh), in_specs=[smem(), v...  3.72 us
  transfers between devices with their start and end apart: 8, of which 3 were waited for; matrix products, arithmetic and copies ran while one was open for 8% of the time, Pallas kernels for 14%

profile of v3, /device:TPU:1, one launch (start us, length us, event | category | flops | bytes accessed | tf_op | source)
XLA Modules:
  0.0 65.2 jit_solution(10334427499170027146)
XLA Ops:
  0.6 0.0 copy-start.13
  0.7 0.1 pad_add_fusion.place
  0.7 5.4 %send.1 = (bf16[256,2048]{1,0:T(8,128)(2,1)}, bf16[256,32]{1,0:T(8,128)(2,1)}, s32[1]{0:T(128)}) custom-call(s32[3]{0:T(128)S(1)} %pad_add_fusion.place, s32[4,256]{1,0:T(4,128)} %tokens_at.1, bf16[2374,1024]{1,0:T(8,128)(2,1)} %table_at.1, bf16[1,64,4096]{2,1,0:T(8,128)(2,1)} %grad_down_at.1, bf16[1,64,1024]{2,1,0:T(8,128)(2,1)} %grad_up_at.1, ...), custom_call_target="tpu_custom_call" | custom-call | tf_op jit(solution)/shard_map/send/pallas_call | solution.py:186
  6.1 9.8 %all-to-all-start = ((bf16[32,8,2048]{2,1,0:T(8,128)(2,1)}), bf16[32,8,2048]{2,1,0:T(8,128)(2,1)S(1)}, u32[]{:S(2)}, u32[]{:S(2)}) async-start(bf16[32,8,2048]{2,1,0:T(8,128)(2,1)} %bitcast.116), calls=%async_computation | async-start | bytes 2097152 | tf_op jit(solution)/shard_map/all_to_all | solution.py:566
  17.0 3.9 %stage.1 = (bf16[8,128,512]{2,1,0:T(8,128)(2,1)}, bf16[8,512,128]{2,1,0:T(8,128)(2,1)}) custom-call(s32[3]{0:T(128)S(1)} %pad_add_fusion.place, bf16[8,2048,128]{2,1,0:T(8,128)(2,1)} %bitcast.115), custom_call_target="tpu_custom_call" | custom-call | bytes 8388608 | tf_op jit(solution)/shard_map/stage/pallas_call | solution.py:298
  21.3 0.0 copy-done.13
  21.3 0.0 copy-start.5
  21.3 0.0 copy-start.10
  21.3 0.0 copy-start.11
  21.3 0.0 copy-start.7
  21.3 0.9 %while.12 = (s32[]{:T(128)}, bf16[32,1024]{1,0:T(8,128)(2,1)S(1)}, s32[1]{0:T(128)}, s32[3]{0:T(128)S(1)}, s32[4,256]{1,0:T(4,128)S(1)}, /*index=5*/bf16[2374,10...) while((s32[]{:T(128)}, bf16[32,1024]{1,0:T(8,128)(2,1)S(1)}, ...), condition=%wide.region_1.2_spmd, body=%wide.region_0.1_spmd.sunk | while | flops 18874372 | bytes 7915977 | solution.py:584
  22.2 8.6 %all-to-all-done.got = bf16[32,8,2048]{2,1,0:T(8,128)(2,1)S(1)} async-done(((bf16[32,8,2048]{2,1,0:T(8,128)(2,1)}), bf16[32,8,2048]{2,1,0:T(8,128)(2,1)S(1)}, u32[]{:S(2)}, u32[]{:S(2)}) %all-to-all-start) | async-done | bytes 1048608 | tf_op jit(solution)/shard_map/all_to_all | solution.py:566
  30.8 0.0 copy-done.5
  30.8 0.0 copy-done.10
  30.8 0.0 copy-done.11
  30.8 1.5 %gather.1 = (bf16[48,1024]{1,0:T(8,128)(2,1)S(1)}, f32[8,512]{1,0:T(8,128)S(1)}, f32[32,8,512]{2,1,0:T(8,128)}) custom-call(f32[32]{0:T(128)S(1)} %copy-done.10, s32[32]{0:T(128)S(1)} %copy-done.11, bf16[32,8,2048]{2,1,0:T(8,128)(2,1)S(1)} %all-to-all-done.got, bf16[256,32]{1,0:T(8,128)(2,1)S(1)} %copy-done.5, bf16[32,1024]{1,0:T(8,128)(2,1)S(1)} %get-tuple-element.1092.extra), custom_call_target="tpu_custom_call" | custom-call | tf_op jit(solution)/shard_map/gather/pallas_call | solution.py:259
  32.3 5.0 %collective-permute-start.33 = (bf16[48,1024]{1,0:T(8,128)(2,1)S(1)}, bf16[48,1024]{1,0:T(8,128)(2,1)S(1)}, u32[]{:S(2)}, u32[]{:S(2)}) collective-permute-start(bf16[48,1024]{1,0:T(8,128)(2,1)S(1)} %get-tuple-element.1093.e0.s0), channel_id=1, source_target_pairs={{0,3},{1,2},{2,1},{3,0},{4,7},{5,6},{6,5},{7,4},{8,11},{9,10},{10,... | collective-permute-start | bytes 294920 | tf_op jit(solution)/shard_map/ppermute | solution.py:533
  37.3 0.5 collective-permute-start.32
  37.8 0.0 collective-permute-start.31
  37.8 4.8 %all-to-all-start.1 = ((f32[32,8,512]{2,1,0:T(8,128)}), f32[32,8,512]{2,1,0:T(8,128)S(1)}, u32[]{:S(2)}, u32[]{:S(2)}) async-start(f32[32,8,512]{2,1,0:T(8,128)} %get-tuple-element.1099), calls=%async_computation.1 | async-start | bytes 1048576 | tf_op jit(solution)/shard_map/all_to_all | solution.py:594
  42.6 0.0 collective-permute-done.33.e3.s3
  42.7 0.1 collective-permute-done.32.e2.s2
  42.8 0.0 collective-permute-done.31.e1.s1
  42.8 0.0 copy-done.7
  42.8 0.7 %norm.1 = (bf16[32,4096]{1,0:T(8,128)(2,1)S(1)}, bf16[32,1024]{1,0:T(8,128)(2,1)S(1)}) custom-call(s32[3]{0:T(128)S(1)} %get-tuple-element.2053, bf16[48,1024]{1,0:T(8,128)(2,1)S(1)} %get-tuple-element.1093.e0.s0, bf16[48,1024]{1,0:T(8,128)(2,1)S(1)} %collective-permute-done.31.e1.s1, bf16[48,1024]{1,0:T(8,128)(2,1)S(1)} %collective-permute-done.32.e2.s2, ...), custom_call_target="tpu_custom_call" | custom-call | tf_op jit(solution)/shard_map/norm/pallas_call | solution.py:385
  43.5 0.0 copy-start
  43.5 0.7 %copy-done = bf16[32,4096]{1,0:T(8,128)(2,1)} copy-done((bf16[32,4096]{1,0:T(8,128)(2,1)}, bf16[32,4096]{1,0:T(8,128)(2,1)S(1)}, u32[]{:S(2)}) %copy-start) | copy-done | bytes 262168
  44.2 3.7 %pair_products.1 = (bf16[32,128]{1,0:T(8,128)(2,1)}, bf16[32,128]{1,0:T(8,128)(2,1)}) custom-call(s32[3]{0:T(128)S(1)} %get-tuple-element.2053, bf16[32,4096]{1,0:T(8,128)(2,1)} %copy-done, f32[1,128]{1,0:T(1,128)} %bitcast.117, bf16[2,4096,256]{2,1,0:T(8,128)(2,1)} %pair_at.1), custom_call_target="tpu_custom_call" | custom-call | bytes 8388608 | tf_op jit(solution)/shard_map/pair_products/pallas_call | solution.py:329
  47.9 0.0 copy-start.2
  47.9 0.0 copy-start.4
  47.9 0.0 copy-start.6
  48.0 0.0 copy-start.8
  48.0 0.0 copy-start.9
  48.0 0.0 copy-start.12
  48.0 5.1 %fusion.32.base_query = f32[32,1024]{1,0:T(8,128)S(1)} fusion(bf16[32,4096]{1,0:T(8,128)(2,1)} %copy-done, bf16[4096,1024]{1,0:T(8,128)(2,1)} %param.21), kind=kOutput, calls=%fused_computation.129 | convolution fusion | flops 268435456 | bytes 8781824 | tf_op jit(solution)/shard_map/dot_general | solution.py:600
  53.1 0.0 all-to-all-done.1.sums
  53.1 0.7 %products.1.p0 = f32[40,256]{1,0:T(8,128)S(1)} custom-call(bf16[32,1024]{1,0:T(8,128)(2,1)S(1)} %get-tuple-element.1098.own, f32[32,8,512]{2,1,0:T(8,128)S(1)} %all-to-all-done.1.sums, bf16[32,8,2048]{2,1,0:T(8,128)(2,1)S(1)} %all-to-all-done.got), custom_call_target="tpu_custom_call" | custom-call | tf_op jit(solution)/shard_map/products/pallas_call | solution.py:419
  53.8 4.5 %collective-permute-start.36 = (f32[40,256]{1,0:T(8,128)S(1)}, f32[40,256]{1,0:T(8,128)S(1)}, u32[]{:S(2)}, u32[]{:S(2)}) collective-permute-start(f32[40,256]{1,0:T(8,128)S(1)} %products.1.p0), channel_id=1, source_target_pairs={{0,3},{1,2},{2,1},{3,0},{4,7},{5,6},{6,5},{7,4},{8,11},{9,10},{10,... | collective-permute-start | bytes 122888 | tf_op jit(solution)/shard_map/ppermute | solution.py:533
  58.2 0.5 collective-permute-start.35
  58.7 0.0 collective-permute-start.34
  58.7 0.0 copy-done.2
  58.7 1.2 %copy-done.3 = bf16[8,512,128]{2,1,0:T(8,128)(2,1)S(1)} copy-done((bf16[8,512,128]{2,1,0:T(8,128)(2,1)S(1)}, bf16[8,512,128]{2,1,0:T(8,128)(2,1)}, u32[]{:S(2)}) %copy-start.3) | copy-done | bytes 1048600
  60.0 0.7 %fetch.1 = (bf16[8,128,512]{2,1,0:T(8,128)(2,1)S(1)}, bf16[8,512,128]{2,1,0:T(8,128)(2,1)S(1)}) custom-call(s32[3]{0:T(128)S(1)} %get-tuple-element.2053, bf16[8,128,512]{2,1,0:T(8,128)(2,1)S(1)} %copy-done.2, bf16[8,512,128]{2,1,0:T(8,128)(2,1)S(1)} %copy-done.3), custom_call_target="tpu_custom_call" | custom-call | bytes 4194304 | tf_op jit(solution)/shard_map/fetch/pallas_call | solution.py:357
  60.7 0.0 collective-permute-done.36.p3
  60.7 1.9 %collective-permute-done.35.p2 = f32[40,256]{1,0:T(8,128)S(1)} collective-permute-done((f32[40,256]{1,0:T(8,128)S(1)}, f32[40,256]{1,0:T(8,128)S(1)}, u32[]{:S(2)}, u32[]{:S(2)}) %collective-permute-start.35) | collective-permute-done | bytes 40992 | tf_op jit(solution)/shard_map/ppermute | solution.py:533
  62.6 0.0 collective-permute-done.34.p1
  62.6 0.0 copy-done.4
  62.6 2.6 %attend.1 = (bf16[32,1024]{1,0:T(8,128)(2,1)}, f32[2,4096]{1,0:T(2,128)}, f32[2,1024]{1,0:T(2,128)}) custom-call(s32[3]{0:T(128)S(1)} %get-tuple-element.2053, f32[32,1024]{1,0:T(8,128)S(1)} %fusion.32.base_query, f32[40,256]{1,0:T(8,128)S(1)} %products.1.p0, f32[40,256]{1,0:T(8,128)S(1)} %collective-permute-done.34.p1, ...), custom_call_target="tpu_custom_call" | custom-call | tf_op jit(solution)/shard_map/attend/pallas_call | solution.py:513
  (6 shorter events, 0.0 us)
Async XLA Ops:
  0.6 20.7 %copy-start.13 = (s32[4,256]{1,0:T(4,128)S(1)}, s32[4,256]{1,0:T(4,128)}, u32[]{:S(2)}) copy-start(s32[4,256]{1,0:T(4,128)} %tokens_at.1) | copy-start | bytes 12292
  6.1 24.7 %all-to-all-start = ((bf16[32,8,2048]{2,1,0:T(8,128)(2,1)}), bf16[32,8,2048]{2,1,0:T(8,128)(2,1)S(1)}, u32[]{:S(2)}, u32[]{:S(2)}) async-start(bf16[32,8,2048]{2,1,0:T(8,128)(2,1)} %bitcast.116), calls=%async_computation | async-start | bytes 2097152 | tf_op jit(solution)/shard_map/all_to_all | solution.py:566
  21.3 9.5 %copy-start.5 = (bf16[256,32]{1,0:T(8,128)(2,1)S(1)}, bf16[256,32]{1,0:T(8,128)(2,1)}, u32[]{:S(2)}) copy-start(bf16[256,32]{1,0:T(8,128)(2,1)} %get-tuple-element.1090.pick) | copy-start | bytes 49156
  21.3 9.5 %copy-start.10 = (f32[32]{0:T(128)S(1)}, f32[32]{0:T(128)}, u32[]{:S(2)}) copy-start(f32[32]{0:T(128)} %scale.1) | copy-start | bytes 388
  21.3 9.5 %copy-start.11 = (s32[32]{0:T(128)S(1)}, s32[32]{0:T(128)}, u32[]{:S(2)}) copy-start(s32[32]{0:T(128)} %learner.1) | copy-start | bytes 388
  21.3 21.4 %copy-start.7 = (f32[4096]{0:T(1024)S(1)}, f32[4096]{0:T(1024)}, u32[]{:S(2)}) copy-start(f32[4096]{0:T(1024)} %param.18) | copy-start | bytes 49156
  32.3 10.3 %collective-permute-start.33 = (bf16[48,1024]{1,0:T(8,128)(2,1)S(1)}, bf16[48,1024]{1,0:T(8,128)(2,1)S(1)}, u32[]{:S(2)}, u32[]{:S(2)}) collective-permute-start(bf16[48,1024]{1,0:T(8,128)(2,1)S(1)} %get-tuple-element.1093.e0.s0), channel_id=1, source_target_pairs={{0,3},{1,2},{2,1},{3,0},{4,7},{5,6},{6,5},{7,4},{8,11},{9,10},{10,... | collective-permute-start | bytes 294920 | tf_op jit(solution)/shard_map/ppermute | solution.py:533
  37.3 5.5 %collective-permute-start.32 = (bf16[48,1024]{1,0:T(8,128)(2,1)S(1)}, bf16[48,1024]{1,0:T(8,128)(2,1)S(1)}, u32[]{:S(2)}, u32[]{:S(2)}) collective-permute-start(bf16[48,1024]{1,0:T(8,128)(2,1)S(1)} %get-tuple-element.1093.e0.s0), channel_id=1, source_target_pairs={{0,2},{1,3},{2,0},{3,1},{4,6},{5,7},{6,4},{7,5},{8,10},{9,11},{10,... | collective-permute-start | bytes 294920 | tf_op jit(solution)/shard_map/ppermute | solution.py:533
  37.8 4.9 %collective-permute-start.31 = (bf16[48,1024]{1,0:T(8,128)(2,1)S(1)}, bf16[48,1024]{1,0:T(8,128)(2,1)S(1)}, u32[]{:S(2)}, u32[]{:S(2)}) collective-permute-start(bf16[48,1024]{1,0:T(8,128)(2,1)S(1)} %get-tuple-element.1093.e0.s0), channel_id=1, source_target_pairs={{0,1},{1,0},{2,3},{3,2},{4,5},{5,4},{6,7},{7,6},{8,9},{9,8},{10,11... | collective-permute-start | bytes 294920 | tf_op jit(solution)/shard_map/ppermute | solution.py:533
  37.8 15.3 %all-to-all-start.1 = ((f32[32,8,512]{2,1,0:T(8,128)}), f32[32,8,512]{2,1,0:T(8,128)S(1)}, u32[]{:S(2)}, u32[]{:S(2)}) async-start(f32[32,8,512]{2,1,0:T(8,128)} %get-tuple-element.1099), calls=%async_computation.1 | async-start | bytes 1048576 | tf_op jit(solution)/shard_map/all_to_all | solution.py:594
  43.5 0.7 %copy-start = (bf16[32,4096]{1,0:T(8,128)(2,1)}, bf16[32,4096]{1,0:T(8,128)(2,1)S(1)}, u32[]{:S(2)}) copy-start(bf16[32,4096]{1,0:T(8,128)(2,1)S(1)} %get-tuple-element.1095.normed) | copy-start | bytes 786436
  47.9 10.8 %copy-start.2 = (bf16[8,128,512]{2,1,0:T(8,128)(2,1)S(1)}, bf16[8,128,512]{2,1,0:T(8,128)(2,1)}, u32[]{:S(2)}) copy-start(bf16[8,128,512]{2,1,0:T(8,128)(2,1)} %get-tuple-element.1104.keys_at) | copy-start | bytes 3145732
  47.9 14.7 %copy-start.4 = (f32[2,4096]{1,0:T(2,128)S(1)}, f32[2,4096]{1,0:T(2,128)}, u32[]{:S(2)}) copy-start(f32[2,4096]{1,0:T(2,128)} %old_down.1) | copy-start | bytes 98308
  47.9 14.6 %copy-start.6 = (f32[2,1024]{1,0:T(2,128)S(1)}, f32[2,1024]{1,0:T(2,128)}, u32[]{:S(2)}) copy-start(f32[2,1024]{1,0:T(2,128)} %old_up.1) | copy-start | bytes 24580
  48.0 14.6 %copy-start.8 = (bf16[32,128]{1,0:T(8,128)(2,1)S(1)}, bf16[32,128]{1,0:T(8,128)(2,1)}, u32[]{:S(2)}) copy-start(bf16[32,128]{1,0:T(8,128)(2,1)} %get-tuple-element.1100.key_new) | copy-start | bytes 24580
  48.0 14.6 %copy-start.9 = (bf16[32,128]{1,0:T(8,128)(2,1)S(1)}, bf16[32,128]{1,0:T(8,128)(2,1)}, u32[]{:S(2)}) copy-start(bf16[32,128]{1,0:T(8,128)(2,1)} %get-tuple-element.1101.value_new) | copy-start | bytes 24580
  48.0 14.6 %copy-start.12 = (f32[128]{0:T(128)S(1)}, f32[128]{0:T(128)}, u32[]{:S(2)}) copy-start(f32[128]{0:T(128)} %param.19) | copy-start | bytes 1540
  53.8 6.9 %collective-permute-start.36 = (f32[40,256]{1,0:T(8,128)S(1)}, f32[40,256]{1,0:T(8,128)S(1)}, u32[]{:S(2)}, u32[]{:S(2)}) collective-permute-start(f32[40,256]{1,0:T(8,128)S(1)} %products.1.p0), channel_id=1, source_target_pairs={{0,3},{1,2},{2,1},{3,0},{4,7},{5,6},{6,5},{7,4},{8,11},{9,10},{10,... | collective-permute-start | bytes 122888 | tf_op jit(solution)/shard_map/ppermute | solution.py:533
  58.2 4.4 %collective-permute-start.35 = (f32[40,256]{1,0:T(8,128)S(1)}, f32[40,256]{1,0:T(8,128)S(1)}, u32[]{:S(2)}, u32[]{:S(2)}) collective-permute-start(f32[40,256]{1,0:T(8,128)S(1)} %products.1.p0), channel_id=1, source_target_pairs={{0,2},{1,3},{2,0},{3,1},{4,6},{5,7},{6,4},{7,5},{8,10},{9,11},{10,... | collective-permute-start | bytes 122888 | tf_op jit(solution)/shard_map/ppermute | solution.py:533
  58.7 3.8 %collective-permute-start.34 = (f32[40,256]{1,0:T(8,128)S(1)}, f32[40,256]{1,0:T(8,128)S(1)}, u32[]{:S(2)}, u32[]{:S(2)}) collective-permute-start(f32[40,256]{1,0:T(8,128)S(1)} %products.1.p0), channel_id=1, source_target_pairs={{0,1},{1,0},{2,3},{3,2},{4,5},{5,4},{6,7},{7,6},{8,9},{9,8},{10,11... | collective-permute-start | bytes 122888 | tf_op jit(solution)/shard_map/ppermute | solution.py:533
  58.7 1.2 %copy-start.3 = (bf16[8,512,128]{2,1,0:T(8,128)(2,1)S(1)}, bf16[8,512,128]{2,1,0:T(8,128)(2,1)}, u32[]{:S(2)}) copy-start(bf16[8,512,128]{2,1,0:T(8,128)(2,1)} %get-tuple-element.1105.values_at) | copy-start | bytes 3145732

commit v4 on v3

--- a/solution.py
+++ b/solution.py
@@ -28,6 +28,12 @@
 def split(values):
     high = values.astype(jnp.bfloat16)
     return high, (values - high.astype(jnp.float32)).astype(jnp.bfloat16)
+
+
+def thirds(values):
+    first, _ = split(values)
+    second, third = split(values - first.astype(jnp.float32))
+    return first, second, third
 
 
 def dot_nt(a, b):
@@ -126,8 +132,8 @@
 
 
 def send_kernel(
-    place, tokens_at, table_at, grad_down_at, grad_up_at, down_at, up_at, sent, pick, rounds,
-    tokens, table, grad_down, grad_up, down, up, places, sems,
+    place, tokens_at, table_at, grad_down_at, grad_up_at, sent, pick, rounds,
+    tokens, table, grad_down, grad_up, places, sems,
 ):
     groups = sent.shape[0] // CAP
     vocab_rows, width = table.shape
@@ -141,15 +147,13 @@
                 (tokens_at, tokens),
                 (grad_down_at.at[:, :, columns], grad_down),
                 (grad_up_at, grad_up),
-                (down_at, down),
-                (up_at, up),
             )
         )
     ]
     span = width // TABLE_PARTS
     spans = [slice(i * span, (i + 1) * span) for i in range(TABLE_PARTS)]
     copies += [
-        pltpu.make_async_copy(table_at.at[:, at], table.at[:, at], sems.at[5 + i])
+        pltpu.make_async_copy(table_at.at[:, at], table.at[:, at], sems.at[3 + i])
         for i, at in enumerate(spans)
     ]
     for copy in copies:
@@ -158,7 +162,7 @@
     ids = arrange_ids(tokens[...], groups)
     chosen, count = find_rows(place, 0, ids, table, pick.shape[1], pick, places)
     rounds[0] = count
-    for copy in copies[1:5]:
+    for copy in copies[1:3]:
         copy.wait()
 
     grads = jnp.concatenate([grad_down[0], grad_up[0]], axis=0)
@@ -169,42 +173,38 @@
     for h in (0, 1):
         taken = jnp.where((source == wanted) & (row % 2 == h), 1.0, 0.0).astype(jnp.bfloat16)
         moved += dot_nn(taken, grads[:, h * half : (h + 1) * half])
-    sent[:, width : width + half] = moved.astype(jnp.bfloat16)
-    rows = fold(down[:, columns], up[...]).astype(jnp.bfloat16)
-    sent[:, width + half :] = jnp.broadcast_to(rows[None], (groups, 8, half)).reshape(-1, half)
+    sent[:, width:] = moved.astype(jnp.bfloat16)
 
     hot = one_hot(chosen, vocab_rows)
     for i, at in enumerate(spans):
-        copies[5 + i].wait()
+        copies[3 + i].wait()
         sent[:, at] = read_rows(hot, table.at[:, at])
 
 
-def send(place, tokens, table, grad_down, grad_up, down, up, groups):
+def send(place, tokens, table, grad_down, grad_up, groups):
     width = table.shape[1]
     count = tokens.size // groups
     anywhere = pl.BlockSpec(memory_space=pl.ANY)
     return pl.pallas_call(
         send_kernel,
         out_shape=(
-            jax.ShapeDtypeStruct((groups * CAP, width * 2), jnp.bfloat16),
+            jax.ShapeDtypeStruct((groups * CAP, width * 3 // 2), jnp.bfloat16),
             jax.ShapeDtypeStruct((groups * CAP, count), jnp.bfloat16),
             jax.ShapeDtypeStruct((1,), jnp.int32),
         ),
-        in_specs=[smem()] + [anywhere] * 6,
+        in_specs=[smem()] + [anywhere] * 4,
         out_specs=(vmem(), vmem(), smem()),
         scratch_shapes=[
             pltpu.VMEM(tokens.shape, jnp.int32),
             pltpu.VMEM(table.shape, jnp.bfloat16),
             pltpu.VMEM(grad_up.shape, jnp.bfloat16),
             pltpu.VMEM(grad_up.shape, jnp.bfloat16),
-            pltpu.VMEM(down.shape, jnp.float32),
-            pltpu.VMEM(up.shape, jnp.float32),
             pltpu.VMEM((groups, 128), jnp.int32),
-            pltpu.SemaphoreType.DMA((5 + TABLE_PARTS,)),
+            pltpu.SemaphoreType.DMA((3 + TABLE_PARTS,)),
         ],
         compiler_params=params(56),
         name="send",
-    )(place, tokens, table, grad_down, grad_up, down, up)
+    )(place, tokens, table, grad_down, grad_up)
 
 
 def again_kernel(place, first, tokens, table, sent, pick, places):
@@ -229,7 +229,7 @@
     )(place, first, tokens, table)
 
 
-def gather_kernel(scale, learner, got, pick, extra, block, own_sum, sent):
+def gather_kernel(place, scale, learner, got, pick, extra, down, up, block, own_sum, sent):
     groups = got.shape[0]
     count, width = extra.shape
     half = width // 2
@@ -238,22 +238,29 @@
         weight = scale[learner[learn]]
         total += got[learn, :, width : width + half].astype(jnp.float32) * weight
     own_sum[...] = total
-    sent[...] = jnp.broadcast_to(total[None], sent.shape)
+    columns = pl.ds(pl.multiple_of(place[0] * width, width), width)
+    old = fold(down[:, columns], up[...])
+    square = jnp.broadcast_to(jnp.sum(total * total, keepdims=True), (8, 128))
+    terms = thirds(square)
+    row = lax.broadcasted_iota(jnp.int32, square.shape, 0)
+    for i in range(3):
+        square = jnp.where(row == i, terms[i].astype(jnp.float32), square)
+    square = jnp.where(row < 3, square, 0.0)
+    message = jnp.concatenate([total, old, square], axis=1).astype(jnp.bfloat16)
+    sent[...] = jnp.broadcast_to(message[None], sent.shape)
     rows = got[:, :, :width].reshape(groups * CAP, width)
     found = lax.dot_general(
         pick[...], rows, (((0,), (0,)), ((), ())), preferred_element_type=jnp.float32
     )
     block[:count, :] = found.astype(jnp.bfloat16) + extra[...]
-    down = jnp.concatenate(
+    own_down = jnp.concatenate(
         [jnp.concatenate([total[2 * i : 2 * i + 1], total[2 * i + 1 : 2 * i + 2]], 1) for i in (0, 1)], 0
     )
-    first, _ = split(down)
-    second, third = split(down - first.astype(jnp.float32))
-    rows = [first, second, third, jnp.zeros((10, width), jnp.bfloat16)]
+    rows = [*thirds(own_down), jnp.zeros((10, width), jnp.bfloat16)]
     block[count:, :] = jnp.concatenate([r.astype(jnp.float32) for r in rows], 0).astype(jnp.bfloat16)
 
 
-def gather(scale, learner, got, pick, extra):
+def gather(place, scale, learner, got, pick, extra, down, up):
     groups = got.shape[0]
     count, width = extra.shape
     return pl.pallas_call(
@@ -261,13 +268,13 @@
         out_shape=(
             jax.ShapeDtypeStruct((count + 16, width), jnp.bfloat16),
             jax.ShapeDtypeStruct((8, width // 2), jnp.float32),
-            jax.ShapeDtypeStruct((groups, 8, width // 2), jnp.float32),
+            jax.ShapeDtypeStruct((groups, 8, width + 128), jnp.bfloat16),
         ),
-        in_specs=[smem(), smem(), vmem(), vmem(), vmem()],
+        in_specs=[smem(), smem(), smem()] + [vmem()] * 5,
         out_specs=(vmem(), vmem(), vmem()),
         compiler_params=params(8),
         name="gather",
-    )(scale, learner, got, pick, extra)
+    )(place, scale, learner, got, pick, extra, down, up)
 
 
 def stage_kernel(place, cache_at, keys_at, values_at, cache, keys, values, wide, sems):
@@ -395,39 +402,39 @@
     )(place, *blocks, gain.reshape(1, -1))
 
 
-def products_kernel(own, sums, got, out):
-    count = own.shape[0]
-    half = sums.shape[2]
-
-    def combine(parts):
-        left = sum(dot_nt(own[:, :half], p) for p in parts)
-        right = sum(dot_nt(own[:, half:], p) for p in parts)
+def products_kernel(own, rows, out):
+    count, width = own.shape
+    half = width // 2
+    groups = rows.shape[0]
+
+    def combine(part):
+        left, right = dot_nt(own[:, :half], part), dot_nt(own[:, half:], part)
         lane = lax.broadcasted_iota(jnp.int32, left.shape, 1)
         mixed = jnp.where(lane % 2 == 0, left, right)
         mixed = mixed + pltpu.roll(mixed, mixed.shape[1] - 1, 1)
         return jnp.where((lane % 8 == 0) | (lane % 8 == 2), mixed, 0.0)
 
-    rows = sums[...].reshape(-1, half)
-    old = combine([got[:, :, 3 * half :].reshape(-1, half)])
-    new = combine(split(rows))
+    new = combine(rows[:, :, :half].reshape(groups * 8, half))
+    old = combine(rows[:, :, half:width].reshape(groups * 8, half))
     out[:count, :] = new + pltpu.roll(old, 1, 1)
-    out[count:, :] = jnp.full((8, rows.shape[0]), jnp.sum(rows * rows), jnp.float32)
-
-
-def products(own, sums, got):
-    count = own.shape[0]
+    squares = rows[:, :, width:].astype(jnp.float32).reshape(groups * 8, 128)
+    square = jnp.sum(squares, axis=0, keepdims=True)
+    out[count:, :] = jnp.broadcast_to(square[:, :1], (8, groups * 8))
+
+
+def products(own, rows):
     return pl.pallas_call(
         products_kernel,
-        out_shape=jax.ShapeDtypeStruct((count + 8, sums.shape[0] * 8), jnp.float32),
-        in_specs=[vmem()] * 3,
+        out_shape=jax.ShapeDtypeStruct((own.shape[0] + 8, rows.shape[0] * 8), jnp.float32),
+        in_specs=[vmem()] * 2,
         out_specs=vmem(),
         compiler_params=params(8),
         name="products",
-    )(own, sums, got)
+    )(own, rows)
 
 
 def attend_kernel(
-    place, base_query, p0, p1, p2, p3, sums, got, gain, key_new, value_new, s0, s1, s2,
+    place, base_query, p0, p1, p2, p3, factors, gain, key_new, value_new, s0, s1, s2,
     s3, own_sum, old_down, old_up, keys, values, out, new_down, new_up, queries, results,
 ):
     t = place[0]
@@ -447,8 +454,8 @@
     updated = pltpu.roll(product, lanes - 1, 1) - clip * product
     updated = jnp.where((lane == 0) | (lane == 2), updated, 0.0)
     clip = clip[:, :1]
-    old = got[:, :, 3 * half :].astype(jnp.float32)
-    rows = (old - clip[None] * sums[...]).reshape(-1, half)
+    old = factors[:, :, half:width].astype(jnp.float32)
+    rows = (old - clip[None] * factors[:, :, :half].astype(jnp.float32)).reshape(-1, half)
     row_high, row_low = split(rows)
     for h in (0, 1):
         left_high, left_low = split(pltpu.roll(updated, 4 + h, 1))
@@ -560,9 +567,7 @@
     steps = token_ids.shape[0]
     count = steps * rows_here
 
-    sent, pick, rounds = send(
-        place, token_ids, embed_table, grad_down, grad_up, down_factor, up_factor, groups
-    )
+    sent, pick, rounds = send(place, token_ids, embed_table, grad_down, grad_up, groups)
     got = lax.all_to_all(sent.reshape(groups, CAP, -1), "dp", 0, 0, tiled=True)
 
     def later_round(state):
@@ -590,8 +595,10 @@
     cache = cache.reshape(rows_here, context * KVH * 2, HEAD)
     keys, values = stage(place, cache, pick)
     pick, keys, values = lax.optimization_barrier((pick, keys, values))
-    block, own_sum, sums = gather(group_scale, learner_group, got, pick, extra)
-    sums = lax.all_to_all(sums, "dp", 0, 0, tiled=True)
+    block, own_sum, sums = gather(
+        place, group_scale, learner_group, got, pick, extra, down_factor, up_factor
+    )
+    rows = lax.all_to_all(sums, "dp", 0, 0, tiled=True)
 
     blocks = [block] + [tensor_swap(block, bit) for bit in (1, 2, 3)]
     normed, own = norm(place, blocks, norm_gain, count)
@@ -600,11 +607,11 @@
     query = jnp.dot(normed, base_query_weight, preferred_element_type=jnp.float32)
     own, query, key_new = lax.optimization_barrier((own, query, key_new))
 
-    part = products(own, sums, got)
+    part = products(own, rows)
     keys, values = fetch(place, keys, values, part)
     parts = [part] + [tensor_swap(part, bit) for bit in (1, 2, 3)]
     attended, new_down, new_up = attend(
-        place, query, *parts, sums, got, query_gain.reshape(1, -1), key_new, value_new,
+        place, query, *parts, rows, query_gain.reshape(1, -1), key_new, value_new,
         *blocks, own_sum, down_factor, up_factor, keys, values,
     )
     return attended.reshape(steps, rows_here, width), new_down, new_up

time: 65.7 us -> 62.9 us (0.957)
  local copies, waits for them, and re-layouts: 1.98 us -> 0.76 us
  starting transfers between devices: 25.1 us -> 24.3 us
  waiting for transfers between devices: 10.6 us -> 9.91 us
    all_to_all x1, waiting for transfers between devices: 8.59 us -> 5.8 us  [body(): got = lax.all_to_all(sent.reshape(groups, CAP, -1), 'dp', 0, 0, tiled=True)]
    ppermute x6, waiting for transfers between devices: 2.01 us -> 4.11 us  [tensor_swap(): return lax.ppermute(values, 'tensor', [(i, i ^ bit) for i in range(size)])]
    unnamed x26, local copies, waits for them, and re-layouts: 1.98 us -> 0.75 us
    all_to_all x1, starting transfers between devices: 4.81 us -> 3.94 us  [body(): rows = lax.all_to_all(sums, 'dp', 0, 0, tiled=True)]
  transfers between devices with their start and end apart: 8 -> 8, of which waited for: 3 -> 4; matrix products, arithmetic and copies ran while one was open for 8% -> 8% of each run, Pallas kernels for 14% -> 15%
where the time goes in v4:
time: 62.9 us; the launch traced here: 62.5 us
  starting transfers between devices  24.3 us (39%)
  Pallas kernels  19.1 us (30%)
  waiting for transfers between devices  9.91 us (16%)
  matrix products  5.14 us (8%)
  between operations  2.28 us (4%)
  loops' own time  0.95 us (2%)
  local copies, waits for them, and re-layouts  0.76 us (1%)
    ppermute x6, starting transfers between devices, tensor_swap(): return lax.ppermute(values, 'tensor', [(i, i ^ bit) for i in range(size)])  10.5 us
    all_to_all x1, starting transfers between devices, body(): got = lax.all_to_all(sent.reshape(groups, CAP, -1), 'dp', 0, 0, tiled=True)  9.82 us
    all_to_all x1, waiting for transfers between devices, body(): got = lax.all_to_all(sent.reshape(groups, CAP, -1), 'dp', 0, 0, tiled=True)  5.8 us
    pallas_call x1, Pallas kernels, send(): pl.pallas_call(send_kernel, out_shape=(jax.ShapeDtypeStruct((groups * CAP...  5.23 us
    dot_general x1, matrix products, body(): jnp.dot(normed, base_query_weight, preferred_element_type=jnp.float32)  5.14 us
    ppermute x6, waiting for transfers between devices, tensor_swap(): return lax.ppermute(values, 'tensor', [(i, i ^ bit) for i in range(size)])  4.11 us
    all_to_all x1, starting transfers between devices, body(): rows = lax.all_to_all(sums, 'dp', 0, 0, tiled=True)  3.94 us
    pallas_call x1, Pallas kernels, stage(): pl.pallas_call(stage_kernel, out_shape=[keys, values], in_specs=[smem(),...  3.92 us
  transfers between devices with their start and end apart: 8, of which 4 were waited for; matrix products, arithmetic and copies ran while one was open for 8% of the time, Pallas kernels for 15%

profile of v4, /device:TPU:1, one launch (start us, length us, event | category | flops | bytes accessed | tf_op | source)
XLA Modules:
  0.0 62.5 jit_solution(4688525379696320415)
XLA Ops:
  0.6 0.0 copy-start.13
  0.7 0.1 pad_add_fusion.place
  0.7 5.2 %send.1 = (bf16[256,1536]{1,0:T(8,128)(2,1)}, bf16[256,32]{1,0:T(8,128)(2,1)}, s32[1]{0:T(128)}) custom-call(s32[3]{0:T(128)S(1)} %pad_add_fusion.place, s32[4,256]{1,0:T(4,128)} %tokens_at.1, bf16[2374,1024]{1,0:T(8,128)(2,1)} %table_at.1, bf16[1,64,4096]{2,1,0:T(8,128)(2,1)} %grad_down_at.1, bf16[1,64,1024]{2,1,0:T(8,128)(2,1)} %grad_up_at.1), custom_call_target="tpu_custom_call" | custom-call | tf_op jit(solution)/shard_map/send/pallas_call | solution.py:188
  6.0 9.8 %all-to-all-start = ((bf16[32,8,1536]{2,1,0:T(8,128)(2,1)}), bf16[32,8,1536]{2,1,0:T(8,128)(2,1)S(1)}, u32[]{:S(2)}, u32[]{:S(2)}) async-start(bf16[32,8,1536]{2,1,0:T(8,128)(2,1)} %bitcast.116), calls=%async_computation | async-start | bytes 1572864 | tf_op jit(solution)/shard_map/all_to_all | solution.py:571
  16.8 3.9 %stage.1 = (bf16[8,128,512]{2,1,0:T(8,128)(2,1)}, bf16[8,512,128]{2,1,0:T(8,128)(2,1)}) custom-call(s32[3]{0:T(128)S(1)} %pad_add_fusion.place, bf16[8,2048,128]{2,1,0:T(8,128)(2,1)} %bitcast.115), custom_call_target="tpu_custom_call" | custom-call | bytes 8388608 | tf_op jit(solution)/shard_map/stage/pallas_call | solution.py:305
  21.1 0.0 copy-done.13
  21.1 0.0 copy-start.4
  21.2 0.0 copy-start.5
  21.2 0.0 copy-start.6
  21.2 0.0 copy-start.10
  21.2 0.0 copy-start.11
  21.2 0.0 copy-start.7
  21.2 0.9 %while.12 = (s32[]{:T(128)}, bf16[32,1024]{1,0:T(8,128)(2,1)S(1)}, s32[1]{0:T(128)}, s32[3]{0:T(128)S(1)}, s32[4,256]{1,0:T(4,128)S(1)}, /*index=5*/bf16[2374,10...) while((s32[]{:T(128)}, bf16[32,1024]{1,0:T(8,128)(2,1)S(1)}, ...), condition=%wide.region_1.2_spmd, body=%wide.region_0.1_spmd.sunk | while | flops 18874372 | bytes 7915977 | solution.py:589
  22.2 5.8 %all-to-all-done.got = bf16[32,8,1536]{2,1,0:T(8,128)(2,1)S(1)} async-done(((bf16[32,8,1536]{2,1,0:T(8,128)(2,1)}), bf16[32,8,1536]{2,1,0:T(8,128)(2,1)S(1)}, u32[]{:S(2)}, u32[]{:S(2)}) %all-to-all-start) | async-done | bytes 786464 | tf_op jit(solution)/shard_map/all_to_all | solution.py:571
  28.0 0.0 copy-done.4
  28.0 0.0 copy-done.5
  28.0 0.0 copy-done.6
  28.0 0.0 copy-done.10
  28.0 0.0 copy-done.11
  28.0 1.6 %gather.1 = (bf16[48,1024]{1,0:T(8,128)(2,1)S(1)}, f32[8,512]{1,0:T(8,128)S(1)}, bf16[32,8,1152]{2,1,0:T(8,128)(2,1)}) custom-call(s32[3]{0:T(128)S(1)} %get-tuple-element.2053, f32[32]{0:T(128)S(1)} %copy-done.10, s32[32]{0:T(128)S(1)} %copy-done.11, bf16[32,8,1536]{2,1,0:T(8,128)(2,1)S(1)} %all-to-all-done.got, bf16[256,32]{1,0:T(8,128)(2,1)S(1)} %copy-done.5, ...), custom_call_target="tpu_custom_call" | custom-call | tf_op jit(solution)/shard_map/gather/pallas_call | solution.py:266
  29.6 5.3 %collective-permute-start.33 = (bf16[48,1024]{1,0:T(8,128)(2,1)S(1)}, bf16[48,1024]{1,0:T(8,128)(2,1)S(1)}, u32[]{:S(2)}, u32[]{:S(2)}) collective-permute-start(bf16[48,1024]{1,0:T(8,128)(2,1)S(1)} %get-tuple-element.1093.e0.s0), channel_id=1, source_target_pairs={{0,3},{1,2},{2,1},{3,0},{4,7},{5,6},{6,5},{7,4},{8,11},{9,10},{10,... | collective-permute-start | bytes 294920 | tf_op jit(solution)/shard_map/ppermute | solution.py:540
  35.0 0.5 collective-permute-start.32
  35.5 0.0 collective-permute-start.31
  35.5 3.9 %all-to-all-start.1 = ((bf16[32,8,1152]{2,1,0:T(8,128)(2,1)}), bf16[32,8,1152]{2,1,0:T(8,128)(2,1)S(1)}, u32[]{:S(2)}, u32[]{:S(2)}) async-start(bf16[32,8,1152]{2,1,0:T(8,128)(2,1)} %get-tuple-element.1099), calls=%async_computation.1 | async-start | bytes 1179648 | tf_op jit(solution)/shard_map/all_to_all | solution.py:601
  39.5 0.0 collective-permute-done.33.e3.s3
  39.5 1.0 %collective-permute-done.32.e2.s2 = bf16[48,1024]{1,0:T(8,128)(2,1)S(1)} collective-permute-done((bf16[48,1024]{1,0:T(8,128)(2,1)S(1)}, bf16[48,1024]{1,0:T(8,128)(2,1)S(1)}, u32[]{:S(2)}, u32[]{:S(2)}) %collective-permute-start.32) | collective-permute-done | bytes 98336 | tf_op jit(solution)/shard_map/ppermute | solution.py:540
  40.4 0.0 collective-permute-done.31.e1.s1
  40.4 0.0 copy-done.7
  40.4 0.7 %norm.1 = (bf16[32,4096]{1,0:T(8,128)(2,1)S(1)}, bf16[32,1024]{1,0:T(8,128)(2,1)S(1)}) custom-call(s32[3]{0:T(128)S(1)} %get-tuple-element.2053, bf16[48,1024]{1,0:T(8,128)(2,1)S(1)} %get-tuple-element.1093.e0.s0, bf16[48,1024]{1,0:T(8,128)(2,1)S(1)} %collective-permute-done.31.e1.s1, bf16[48,1024]{1,0:T(8,128)(2,1)S(1)} %collective-permute-done.32.e2.s2, ...), custom_call_target="tpu_custom_call" | custom-call | tf_op jit(solution)/shard_map/norm/pallas_call | solution.py:392
  41.2 0.0 copy-start
  41.2 0.7 %copy-done = bf16[32,4096]{1,0:T(8,128)(2,1)} copy-done((bf16[32,4096]{1,0:T(8,128)(2,1)}, bf16[32,4096]{1,0:T(8,128)(2,1)S(1)}, u32[]{:S(2)}) %copy-start) | copy-done | bytes 262168
  41.9 3.7 %pair_products.1 = (bf16[32,128]{1,0:T(8,128)(2,1)}, bf16[32,128]{1,0:T(8,128)(2,1)}) custom-call(s32[3]{0:T(128)S(1)} %get-tuple-element.2053, bf16[32,4096]{1,0:T(8,128)(2,1)} %copy-done, f32[1,128]{1,0:T(1,128)} %bitcast.117, bf16[2,4096,256]{2,1,0:T(8,128)(2,1)} %pair_at.1), custom_call_target="tpu_custom_call" | custom-call | bytes 8388608 | tf_op jit(solution)/shard_map/pair_products/pallas_call | solution.py:336
  45.6 0.0 copy-start.2
  45.6 0.0 copy-start.8
  45.6 0.0 copy-start.9
  45.6 0.0 copy-start.12
  45.6 5.1 %fusion.32.base_query = f32[32,1024]{1,0:T(8,128)S(1)} fusion(bf16[32,4096]{1,0:T(8,128)(2,1)} %copy-done, bf16[4096,1024]{1,0:T(8,128)(2,1)} %param.21), kind=kOutput, calls=%fused_computation.129 | convolution fusion | flops 268435456 | bytes 8781824 | tf_op jit(solution)/shard_map/dot_general | solution.py:607
  50.8 0.0 all-to-all-done.1.rows.factors
  50.8 0.5 products.1.p0
  51.3 4.2 %collective-permute-start.36 = (f32[40,256]{1,0:T(8,128)S(1)}, f32[40,256]{1,0:T(8,128)S(1)}, u32[]{:S(2)}, u32[]{:S(2)}) collective-permute-start(f32[40,256]{1,0:T(8,128)S(1)} %products.1.p0), channel_id=1, source_target_pairs={{0,3},{1,2},{2,1},{3,0},{4,7},{5,6},{6,5},{7,4},{8,11},{9,10},{10,... | collective-permute-start | bytes 122888 | tf_op jit(solution)/shard_map/ppermute | solution.py:540
  55.5 0.5 collective-permute-start.35
  56.0 0.0 collective-permute-start.34
  56.0 0.0 copy-done.3
  56.0 0.7 %fetch.1 = (bf16[8,128,512]{2,1,0:T(8,128)(2,1)S(1)}, bf16[8,512,128]{2,1,0:T(8,128)(2,1)S(1)}) custom-call(s32[3]{0:T(128)S(1)} %get-tuple-element.2053, bf16[8,128,512]{2,1,0:T(8,128)(2,1)S(1)} %copy-done.2, bf16[8,512,128]{2,1,0:T(8,128)(2,1)S(1)} %copy-done.3), custom_call_target="tpu_custom_call" | custom-call | bytes 4194304 | tf_op jit(solution)/shard_map/fetch/pallas_call | solution.py:364
  56.7 1.0 %collective-permute-done.36.p3 = f32[40,256]{1,0:T(8,128)S(1)} collective-permute-done((f32[40,256]{1,0:T(8,128)S(1)}, f32[40,256]{1,0:T(8,128)S(1)}, u32[]{:S(2)}, u32[]{:S(2)}) %collective-permute-start.36) | collective-permute-done | bytes 40992 | tf_op jit(solution)/shard_map/ppermute | solution.py:540
  57.7 2.1 %collective-permute-done.35.p2 = f32[40,256]{1,0:T(8,128)S(1)} collective-permute-done((f32[40,256]{1,0:T(8,128)S(1)}, f32[40,256]{1,0:T(8,128)S(1)}, u32[]{:S(2)}, u32[]{:S(2)}) %collective-permute-start.35) | collective-permute-done | bytes 40992 | tf_op jit(solution)/shard_map/ppermute | solution.py:540
  59.9 0.0 collective-permute-done.34.p1
  59.9 2.6 %attend.1 = (bf16[32,1024]{1,0:T(8,128)(2,1)}, f32[2,4096]{1,0:T(2,128)}, f32[2,1024]{1,0:T(2,128)}) custom-call(s32[3]{0:T(128)S(1)} %get-tuple-element.2053, f32[32,1024]{1,0:T(8,128)S(1)} %fusion.32.base_query, f32[40,256]{1,0:T(8,128)S(1)} %products.1.p0, f32[40,256]{1,0:T(8,128)S(1)} %collective-permute-done.34.p1, ...), custom_call_target="tpu_custom_call" | custom-call | tf_op jit(solution)/shard_map/attend/pallas_call | solution.py:520
  (6 shorter events, 0.0 us)
Async XLA Ops:
  0.6 20.5 %copy-start.13 = (s32[4,256]{1,0:T(4,128)S(1)}, s32[4,256]{1,0:T(4,128)}, u32[]{:S(2)}) copy-start(s32[4,256]{1,0:T(4,128)} %tokens_at.1) | copy-start | bytes 12292
  6.0 22.0 %all-to-all-start = ((bf16[32,8,1536]{2,1,0:T(8,128)(2,1)}), bf16[32,8,1536]{2,1,0:T(8,128)(2,1)S(1)}, u32[]{:S(2)}, u32[]{:S(2)}) async-start(bf16[32,8,1536]{2,1,0:T(8,128)(2,1)} %bitcast.116), calls=%async_computation | async-start | bytes 1572864 | tf_op jit(solution)/shard_map/all_to_all | solution.py:571
  21.1 6.8 %copy-start.4 = (f32[2,4096]{1,0:T(2,128)S(1)}, f32[2,4096]{1,0:T(2,128)}, u32[]{:S(2)}) copy-start(f32[2,4096]{1,0:T(2,128)} %old_down.1) | copy-start | bytes 98308
  21.2 6.8 %copy-start.5 = (bf16[256,32]{1,0:T(8,128)(2,1)S(1)}, bf16[256,32]{1,0:T(8,128)(2,1)}, u32[]{:S(2)}) copy-start(bf16[256,32]{1,0:T(8,128)(2,1)} %get-tuple-element.1090.pick) | copy-start | bytes 49156
  21.2 6.8 %copy-start.6 = (f32[2,1024]{1,0:T(2,128)S(1)}, f32[2,1024]{1,0:T(2,128)}, u32[]{:S(2)}) copy-start(f32[2,1024]{1,0:T(2,128)} %old_up.1) | copy-start | bytes 24580
  21.2 6.8 %copy-start.10 = (f32[32]{0:T(128)S(1)}, f32[32]{0:T(128)}, u32[]{:S(2)}) copy-start(f32[32]{0:T(128)} %scale.1) | copy-start | bytes 388
  21.2 6.8 %copy-start.11 = (s32[32]{0:T(128)S(1)}, s32[32]{0:T(128)}, u32[]{:S(2)}) copy-start(s32[32]{0:T(128)} %learner.1) | copy-start | bytes 388
  21.2 19.2 %copy-start.7 = (f32[4096]{0:T(1024)S(1)}, f32[4096]{0:T(1024)}, u32[]{:S(2)}) copy-start(f32[4096]{0:T(1024)} %param.18) | copy-start | bytes 49156
  29.6 9.8 %collective-permute-start.33 = (bf16[48,1024]{1,0:T(8,128)(2,1)S(1)}, bf16[48,1024]{1,0:T(8,128)(2,1)S(1)}, u32[]{:S(2)}, u32[]{:S(2)}) collective-permute-start(bf16[48,1024]{1,0:T(8,128)(2,1)S(1)} %get-tuple-element.1093.e0.s0), channel_id=1, source_target_pairs={{0,3},{1,2},{2,1},{3,0},{4,7},{5,6},{6,5},{7,4},{8,11},{9,10},{10,... | collective-permute-start | bytes 294920 | tf_op jit(solution)/shard_map/ppermute | solution.py:540
  35.0 5.5 %collective-permute-start.32 = (bf16[48,1024]{1,0:T(8,128)(2,1)S(1)}, bf16[48,1024]{1,0:T(8,128)(2,1)S(1)}, u32[]{:S(2)}, u32[]{:S(2)}) collective-permute-start(bf16[48,1024]{1,0:T(8,128)(2,1)S(1)} %get-tuple-element.1093.e0.s0), channel_id=1, source_target_pairs={{0,2},{1,3},{2,0},{3,1},{4,6},{5,7},{6,4},{7,5},{8,10},{9,11},{10,... | collective-permute-start | bytes 294920 | tf_op jit(solution)/shard_map/ppermute | solution.py:540
  35.5 4.9 %collective-permute-start.31 = (bf16[48,1024]{1,0:T(8,128)(2,1)S(1)}, bf16[48,1024]{1,0:T(8,128)(2,1)S(1)}, u32[]{:S(2)}, u32[]{:S(2)}) collective-permute-start(bf16[48,1024]{1,0:T(8,128)(2,1)S(1)} %get-tuple-element.1093.e0.s0), channel_id=1, source_target_pairs={{0,1},{1,0},{2,3},{3,2},{4,5},{5,4},{6,7},{7,6},{8,9},{9,8},{10,11... | collective-permute-start | bytes 294920 | tf_op jit(solution)/shard_map/ppermute | solution.py:540
  35.5 15.3 %all-to-all-start.1 = ((bf16[32,8,1152]{2,1,0:T(8,128)(2,1)}), bf16[32,8,1152]{2,1,0:T(8,128)(2,1)S(1)}, u32[]{:S(2)}, u32[]{:S(2)}) async-start(bf16[32,8,1152]{2,1,0:T(8,128)(2,1)} %get-tuple-element.1099), calls=%async_computation.1 | async-start | bytes 1179648 | tf_op jit(solution)/shard_map/all_to_all | solution.py:601
  41.2 0.7 %copy-start = (bf16[32,4096]{1,0:T(8,128)(2,1)}, bf16[32,4096]{1,0:T(8,128)(2,1)S(1)}, u32[]{:S(2)}) copy-start(bf16[32,4096]{1,0:T(8,128)(2,1)S(1)} %get-tuple-element.1095.normed) | copy-start | bytes 786436
  45.6 10.4 %copy-start.2 = (bf16[8,128,512]{2,1,0:T(8,128)(2,1)S(1)}, bf16[8,128,512]{2,1,0:T(8,128)(2,1)}, u32[]{:S(2)}) copy-start(bf16[8,128,512]{2,1,0:T(8,128)(2,1)} %get-tuple-element.1104.keys_at) | copy-start | bytes 3145732
  45.6 10.4 %copy-start.3 = (bf16[8,512,128]{2,1,0:T(8,128)(2,1)S(1)}, bf16[8,512,128]{2,1,0:T(8,128)(2,1)}, u32[]{:S(2)}) copy-start(bf16[8,512,128]{2,1,0:T(8,128)(2,1)} %get-tuple-element.1105.values_at) | copy-start | bytes 3145732
  45.6 14.3 %copy-start.8 = (bf16[32,128]{1,0:T(8,128)(2,1)S(1)}, bf16[32,128]{1,0:T(8,128)(2,1)}, u32[]{:S(2)}) copy-start(bf16[32,128]{1,0:T(8,128)(2,1)} %get-tuple-element.1100.key_new) | copy-start | bytes 24580
  45.6 14.2 %copy-start.9 = (bf16[32,128]{1,0:T(8,128)(2,1)S(1)}, bf16[32,128]{1,0:T(8,128)(2,1)}, u32[]{:S(2)}) copy-start(bf16[32,128]{1,0:T(8,128)(2,1)} %get-tuple-element.1101.value_new) | copy-start | bytes 24580
  45.6 14.2 %copy-start.12 = (f32[128]{0:T(128)S(1)}, f32[128]{0:T(128)}, u32[]{:S(2)}) copy-start(f32[128]{0:T(128)} %param.19) | copy-start | bytes 1540
  51.3 6.4 %collective-permute-start.36 = (f32[40,256]{1,0:T(8,128)S(1)}, f32[40,256]{1,0:T(8,128)S(1)}, u32[]{:S(2)}, u32[]{:S(2)}) collective-permute-start(f32[40,256]{1,0:T(8,128)S(1)} %products.1.p0), channel_id=1, source_target_pairs={{0,3},{1,2},{2,1},{3,0},{4,7},{5,6},{6,5},{7,4},{8,11},{9,10},{10,... | collective-permute-start | bytes 122888 | tf_op jit(solution)/shard_map/ppermute | solution.py:540
  55.5 4.4 %collective-permute-start.35 = (f32[40,256]{1,0:T(8,128)S(1)}, f32[40,256]{1,0:T(8,128)S(1)}, u32[]{:S(2)}, u32[]{:S(2)}) collective-permute-start(f32[40,256]{1,0:T(8,128)S(1)} %products.1.p0), channel_id=1, source_target_pairs={{0,2},{1,3},{2,0},{3,1},{4,6},{5,7},{6,4},{7,5},{8,10},{9,11},{10,... | collective-permute-start | bytes 122888 | tf_op jit(solution)/shard_map/ppermute | solution.py:540
  56.0 3.8 %collective-permute-start.34 = (f32[40,256]{1,0:T(8,128)S(1)}, f32[40,256]{1,0:T(8,128)S(1)}, u32[]{:S(2)}, u32[]{:S(2)}) collective-permute-start(f32[40,256]{1,0:T(8,128)S(1)} %products.1.p0), channel_id=1, source_target_pairs={{0,1},{1,0},{2,3},{3,2},{4,5},{5,4},{6,7},{7,6},{8,9},{9,8},{10,11... | collective-permute-start | bytes 122888 | tf_op jit(solution)/shard_map/ppermute | solution.py:540

commit v5 on v4

--- a/solution.py
+++ b/solution.py
@@ -106,8 +106,11 @@
     me = place[2]
     own = places[pl.ds(me, 1), :]
     rows = groups * CAP
-    at = lax.broadcasted_iota(jnp.int32, (rows, lanes), 0)
-    pick[...] = jnp.where(at == own, 1.0, 0.0).astype(jnp.bfloat16)[:, :period]
+    at = lax.broadcasted_iota(jnp.int32, (period, lanes), 0)
+    same = at == lax.broadcasted_iota(jnp.int32, (period, lanes), 1)
+    own = jnp.max(jnp.where(same, jnp.broadcast_to(own, same.shape), -1), axis=1, keepdims=True)
+    at = lax.broadcasted_iota(jnp.int32, (period, rows), 1)
+    pick[...] = jnp.where(at == own, 1.0, 0.0).astype(jnp.bfloat16)
 
     local = jnp.where(owner == me, ids - lowest, -1)
     spread = (groups, CAP, lanes)
@@ -160,7 +163,7 @@
         copy.start()
     copies[0].wait()
     ids = arrange_ids(tokens[...], groups)
-    chosen, count = find_rows(place, 0, ids, table, pick.shape[1], pick, places)
+    chosen, count = find_rows(place, 0, ids, table, pick.shape[0], pick, places)
     rounds[0] = count
     for copy in copies[1:3]:
         copy.wait()
@@ -189,7 +192,7 @@
         send_kernel,
         out_shape=(
             jax.ShapeDtypeStruct((groups * CAP, width * 3 // 2), jnp.bfloat16),
-            jax.ShapeDtypeStruct((groups * CAP, count), jnp.bfloat16),
+            jax.ShapeDtypeStruct((count, groups * CAP), jnp.bfloat16),
             jax.ShapeDtypeStruct((1,), jnp.int32),
         ),
         in_specs=[smem()] + [anywhere] * 4,
@@ -210,7 +213,7 @@
 def again_kernel(place, first, tokens, table, sent, pick, places):
     groups = sent.shape[0] // CAP
     ids = arrange_ids(tokens[...], groups)
-    chosen, _ = find_rows(place, first[0], ids, table, pick.shape[1], pick, places)
+    chosen, _ = find_rows(place, first[0], ids, table, pick.shape[0], pick, places)
     sent[...] = read_rows(one_hot(chosen, table.shape[0]), table)
 
 
@@ -219,7 +222,7 @@
         again_kernel,
         out_shape=(
             jax.ShapeDtypeStruct((groups * CAP, table.shape[1]), jnp.bfloat16),
-            jax.ShapeDtypeStruct((groups * CAP, tokens.size // groups), jnp.bfloat16),
+            jax.ShapeDtypeStruct((tokens.size // groups, groups * CAP), jnp.bfloat16),
         ),
         in_specs=[smem(), smem(), vmem(), vmem()],
         out_specs=(vmem(), vmem()),
@@ -240,18 +243,10 @@
     own_sum[...] = total
     columns = pl.ds(pl.multiple_of(place[0] * width, width), width)
     old = fold(down[:, columns], up[...])
-    square = jnp.broadcast_to(jnp.sum(total * total, keepdims=True), (8, 128))
-    terms = thirds(square)
-    row = lax.broadcasted_iota(jnp.int32, square.shape, 0)
-    for i in range(3):
-        square = jnp.where(row == i, terms[i].astype(jnp.float32), square)
-    square = jnp.where(row < 3, square, 0.0)
-    message = jnp.concatenate([total, old, square], axis=1).astype(jnp.bfloat16)
+    message = jnp.concatenate([total, old], axis=1).astype(jnp.bfloat16)
     sent[...] = jnp.broadcast_to(message[None], sent.shape)
     rows = got[:, :, :width].reshape(groups * CAP, width)
-    found = lax.dot_general(
-        pick[...], rows, (((0,), (0,)), ((), ())), preferred_element_type=jnp.float32
-    )
+    found = dot_nn(pick[...], rows)
     block[:count, :] = found.astype(jnp.bfloat16) + extra[...]
     own_down = jnp.concatenate(
         [jnp.concatenate([total[2 * i : 2 * i + 1], total[2 * i + 1 : 2 * i + 2]], 1) for i in (0, 1)], 0
@@ -268,7 +263,7 @@
         out_shape=(
             jax.ShapeDtypeStruct((count + 16, width), jnp.bfloat16),
             jax.ShapeDtypeStruct((8, width // 2), jnp.float32),
-            jax.ShapeDtypeStruct((groups, 8, width + 128), jnp.bfloat16),
+            jax.ShapeDtypeStruct((groups, 8, width), jnp.bfloat16),
         ),
         in_specs=[smem(), smem(), smem()] + [vmem()] * 5,
         out_specs=(vmem(), vmem(), vmem()),
@@ -414,18 +409,21 @@
         mixed = mixed + pltpu.roll(mixed, mixed.shape[1] - 1, 1)
         return jnp.where((lane % 8 == 0) | (lane % 8 == 2), mixed, 0.0)
 
-    new = combine(rows[:, :, :half].reshape(groups * 8, half))
+    summed = rows[:, :, :half].reshape(groups * 8, half)
+    new = combine(summed)
     old = combine(rows[:, :, half:width].reshape(groups * 8, half))
-    out[:count, :] = new + pltpu.roll(old, 1, 1)
-    squares = rows[:, :, width:].astype(jnp.float32).reshape(groups * 8, 128)
-    square = jnp.sum(squares, axis=0, keepdims=True)
-    out[count:, :] = jnp.broadcast_to(square[:, :1], (8, groups * 8))
+    both = new + pltpu.roll(old, 1, 1)
+    lanes = out.shape[1]
+    out[:count, :] = both[:, :lanes] + pltpu.roll(both[:, lanes:], 4, 1)
+    summed = summed.astype(jnp.float32)
+    square = jnp.sum(summed * summed, keepdims=True)
+    out[count:, :] = jnp.broadcast_to(square, (8, lanes))
 
 
 def products(own, rows):
     return pl.pallas_call(
         products_kernel,
-        out_shape=jax.ShapeDtypeStruct((own.shape[0] + 8, rows.shape[0] * 8), jnp.float32),
+        out_shape=jax.ShapeDtypeStruct((own.shape[0] + 8, rows.shape[0] * 4), jnp.float32),
         in_specs=[vmem()] * 2,
         out_specs=vmem(),
         compiler_params=params(8),
@@ -447,20 +445,22 @@
 
     both = (p0[...] + p1[...]) + (p2[...] + p3[...])
     product = both[:count, :]
-    overall = both[count : count + 1, :]
+    overall = both[count : count + 1, :1]
     clip = RATE * (1.0 / jnp.maximum(jnp.sqrt(overall), 1.0))
     lanes = product.shape[1]
+    product = jnp.concatenate([product, pltpu.roll(product, lanes - 4, 1)], axis=1)
+    lanes = 2 * lanes
     lane = lax.broadcasted_iota(jnp.int32, product.shape, 1) % 8
     updated = pltpu.roll(product, lanes - 1, 1) - clip * product
     updated = jnp.where((lane == 0) | (lane == 2), updated, 0.0)
-    clip = clip[:, :1]
-    old = factors[:, :, half:width].astype(jnp.float32)
-    rows = (old - clip[None] * factors[:, :, :half].astype(jnp.float32)).reshape(-1, half)
-    row_high, row_low = split(rows)
+    dropped = clip * updated
+    old = factors[:, :, half:width].reshape(-1, half)
+    summed = factors[:, :, :half].reshape(-1, half)
     for h in (0, 1):
-        left_high, left_low = split(pltpu.roll(updated, 4 + h, 1))
-        change = dot_nn(left_high, row_high) + dot_nn(left_low, row_high)
-        change += dot_nn(left_high, row_low)
+        left = jnp.concatenate(split(pltpu.roll(updated, 4 + h, 1)), axis=0)
+        less = jnp.concatenate(split(pltpu.roll(dropped, 4 + h, 1)), axis=0)
+        change = dot_nn(left, old) - dot_nn(less, summed)
+        change = change[:count] + change[count:]
         query = base_query[:, h * half : (h + 1) * half] + ADAPTER_SCALING * change
         for j in range(heads // 2):
             part = query[:, j * HEAD : (j + 1) * HEAD]
@@ -579,10 +579,7 @@
             if k:
                 ring = [(i, (i + k) % groups) for i in range(groups)]
                 part = lax.ppermute(part, "dp", ring)
-            wanted = lax.dynamic_slice_in_dim(pick, source, CAP, 0)
-            found = lax.dot_general(
-                wanted, part, (((0,), (0,)), ((), ())), preferred_element_type=jnp.float32
-            )
+            found = dot_nn(lax.dynamic_slice_in_dim(pick, source, CAP, 1), part)
             rows = rows + found.astype(jnp.bfloat16)
         return r + 1, rows
 

time: 62.9 us -> 62 us (0.986)
  no operation moved by 1% of the time
where the time goes in v5:
time: 62 us; the launch traced here: 61.6 us
  starting transfers between devices  23.7 us (38%)
  Pallas kernels  19 us (31%)
  waiting for transfers between devices  9.74 us (16%)
  matrix products  5.14 us (8%)
  between operations  2.28 us (4%)
  loops' own time  0.88 us (1%)
  local copies, waits for them, and re-layouts  0.76 us (1%)
    ppermute x6, starting transfers between devices, tensor_swap(): return lax.ppermute(values, 'tensor', [(i, i ^ bit) for i in range(size)])  9.96 us
    all_to_all x1, starting transfers between devices, body(): got = lax.all_to_all(sent.reshape(groups, CAP, -1), 'dp', 0, 0, tiled=True)  9.82 us
    all_to_all x1, waiting for transfers between devices, body(): got = lax.all_to_all(sent.reshape(groups, CAP, -1), 'dp', 0, 0, tiled=True)  5.85 us
    pallas_call x1, Pallas kernels, send(): pl.pallas_call(send_kernel, out_shape=(jax.ShapeDtypeStruct((groups * CAP...  5.23 us
    dot_general x1, matrix products, body(): jnp.dot(normed, base_query_weight, preferred_element_type=jnp.float32)  5.14 us
    all_to_all x1, starting transfers between devices, body(): rows = lax.all_to_all(sums, 'dp', 0, 0, tiled=True)  3.94 us
    pallas_call x1, Pallas kernels, stage(): pl.pallas_call(stage_kernel, out_shape=[keys, values], in_specs=[smem(),...  3.92 us
    ppermute x6, waiting for transfers between devices, tensor_swap(): return lax.ppermute(values, 'tensor', [(i, i ^ bit) for i in range(size)])  3.88 us
  transfers between devices with their start and end apart: 8, of which 4 were waited for; matrix products, arithmetic and copies ran while one was open for 8% of the time, Pallas kernels for 15%

profile of v5, /device:TPU:1, one launch (start us, length us, event | category | flops | bytes accessed | tf_op | source)
XLA Modules:
  0.0 61.6 jit_solution(8618597563704703785)
XLA Ops:
  0.6 0.0 copy-start.13
  0.7 0.1 pad_add_fusion.place
  0.7 5.2 %send.1 = (bf16[256,1536]{1,0:T(8,128)(2,1)}, bf16[32,256]{1,0:T(8,128)(2,1)}, s32[1]{0:T(128)}) custom-call(s32[3]{0:T(128)S(1)} %pad_add_fusion.place, s32[4,256]{1,0:T(4,128)} %tokens_at.1, bf16[2374,1024]{1,0:T(8,128)(2,1)} %table_at.1, bf16[1,64,4096]{2,1,0:T(8,128)(2,1)} %grad_down_at.1, bf16[1,64,1024]{2,1,0:T(8,128)(2,1)} %grad_up_at.1), custom_call_target="tpu_custom_call" | custom-call | tf_op jit(solution)/shard_map/send/pallas_call | solution.py:191
  6.0 9.8 %all-to-all-start = ((bf16[32,8,1536]{2,1,0:T(8,128)(2,1)}), bf16[32,8,1536]{2,1,0:T(8,128)(2,1)S(1)}, u32[]{:S(2)}, u32[]{:S(2)}) async-start(bf16[32,8,1536]{2,1,0:T(8,128)(2,1)} %bitcast.116), calls=%async_computation | async-start | bytes 1572864 | tf_op jit(solution)/shard_map/all_to_all | solution.py:571
  16.8 3.9 %stage.1 = (bf16[8,128,512]{2,1,0:T(8,128)(2,1)}, bf16[8,512,128]{2,1,0:T(8,128)(2,1)}) custom-call(s32[3]{0:T(128)S(1)} %pad_add_fusion.place, bf16[8,2048,128]{2,1,0:T(8,128)(2,1)} %bitcast.115), custom_call_target="tpu_custom_call" | custom-call | bytes 8388608 | tf_op jit(solution)/shard_map/stage/pallas_call | solution.py:300
  21.1 0.0 copy-done.13
  21.1 0.0 copy-start.4
  21.2 0.0 copy-start.5
  21.2 0.0 copy-start.6
  21.2 0.0 copy-start.10
  21.2 0.0 copy-start.11
  21.2 0.0 copy-start.7
  21.2 0.9 %while.12 = (s32[]{:T(128)}, bf16[32,1024]{1,0:T(8,128)(2,1)S(1)}, s32[1]{0:T(128)}, s32[3]{0:T(128)S(1)}, s32[4,256]{1,0:T(4,128)S(1)}, /*index=5*/bf16[2374,10...) while((s32[]{:T(128)}, bf16[32,1024]{1,0:T(8,128)(2,1)S(1)}, ...), condition=%wide.region_1.2_spmd, body=%wide.region_0.1_spmd.sunk | while | flops 18874372 | bytes 8112585 | solution.py:586
  22.1 5.9 %all-to-all-done.got = bf16[32,8,1536]{2,1,0:T(8,128)(2,1)S(1)} async-done(((bf16[32,8,1536]{2,1,0:T(8,128)(2,1)}), bf16[32,8,1536]{2,1,0:T(8,128)(2,1)S(1)}, u32[]{:S(2)}, u32[]{:S(2)}) %all-to-all-start) | async-done | bytes 786464 | tf_op jit(solution)/shard_map/all_to_all | solution.py:571
  28.0 0.0 copy-done.4
  28.0 0.0 copy-done.5
  28.0 0.0 copy-done.6
  28.0 0.0 copy-done.10
  28.0 0.0 copy-done.11
  28.0 1.5 %gather.1 = (bf16[48,1024]{1,0:T(8,128)(2,1)S(1)}, f32[8,512]{1,0:T(8,128)S(1)}, bf16[32,8,1024]{2,1,0:T(8,128)(2,1)}) custom-call(s32[3]{0:T(128)S(1)} %get-tuple-element.2053, f32[32]{0:T(128)S(1)} %copy-done.10, s32[32]{0:T(128)S(1)} %copy-done.11, bf16[32,8,1536]{2,1,0:T(8,128)(2,1)S(1)} %all-to-all-done.got, bf16[32,256]{1,0:T(8,128)(2,1)S(1)} %copy-done.6, ...), custom_call_target="tpu_custom_call" | custom-call | tf_op jit(solution)/shard_map/gather/pallas_call | solution.py:261
  29.5 5.4 %collective-permute-start.33 = (bf16[48,1024]{1,0:T(8,128)(2,1)S(1)}, bf16[48,1024]{1,0:T(8,128)(2,1)S(1)}, u32[]{:S(2)}, u32[]{:S(2)}) collective-permute-start(bf16[48,1024]{1,0:T(8,128)(2,1)S(1)} %get-tuple-element.1093.e0.s0), channel_id=1, source_target_pairs={{0,3},{1,2},{2,1},{3,0},{4,7},{5,6},{6,5},{7,4},{8,11},{9,10},{10,... | collective-permute-start | bytes 294920 | tf_op jit(solution)/shard_map/ppermute | solution.py:540
  34.9 0.5 collective-permute-start.32
  35.4 0.0 collective-permute-start.31
  35.4 3.9 %all-to-all-start.1 = ((bf16[32,8,1024]{2,1,0:T(8,128)(2,1)}), bf16[32,8,1024]{2,1,0:T(8,128)(2,1)S(1)}, u32[]{:S(2)}, u32[]{:S(2)}) async-start(bf16[32,8,1024]{2,1,0:T(8,128)(2,1)} %get-tuple-element.1099), calls=%async_computation.1 | async-start | bytes 1048576 | tf_op jit(solution)/shard_map/all_to_all | solution.py:598
  39.4 0.0 collective-permute-done.33.e3.s3
  39.4 1.0 %collective-permute-done.32.e2.s2 = bf16[48,1024]{1,0:T(8,128)(2,1)S(1)} collective-permute-done((bf16[48,1024]{1,0:T(8,128)(2,1)S(1)}, bf16[48,1024]{1,0:T(8,128)(2,1)S(1)}, u32[]{:S(2)}, u32[]{:S(2)}) %collective-permute-start.32) | collective-permute-done | bytes 98336 | tf_op jit(solution)/shard_map/ppermute | solution.py:540
  40.3 0.0 collective-permute-done.31.e1.s1
  40.3 0.0 copy-done.7
  40.3 0.7 %norm.1 = (bf16[32,4096]{1,0:T(8,128)(2,1)S(1)}, bf16[32,1024]{1,0:T(8,128)(2,1)S(1)}) custom-call(s32[3]{0:T(128)S(1)} %get-tuple-element.2053, bf16[48,1024]{1,0:T(8,128)(2,1)S(1)} %get-tuple-element.1093.e0.s0, bf16[48,1024]{1,0:T(8,128)(2,1)S(1)} %collective-permute-done.31.e1.s1, bf16[48,1024]{1,0:T(8,128)(2,1)S(1)} %collective-permute-done.32.e2.s2, ...), custom_call_target="tpu_custom_call" | custom-call | tf_op jit(solution)/shard_map/norm/pallas_call | solution.py:387
  41.1 0.7 %copy-done.1 = bf16[32,4096]{1,0:T(8,128)(2,1)} copy-done((bf16[32,4096]{1,0:T(8,128)(2,1)}, bf16[32,4096]{1,0:T(8,128)(2,1)S(1)}, u32[]{:S(2)}) %copy-start.1) | copy-done | bytes 262168
  41.8 3.7 %pair_products.1 = (bf16[32,128]{1,0:T(8,128)(2,1)}, bf16[32,128]{1,0:T(8,128)(2,1)}) custom-call(s32[3]{0:T(128)S(1)} %get-tuple-element.2053, bf16[32,4096]{1,0:T(8,128)(2,1)} %copy-done.1, f32[1,128]{1,0:T(1,128)} %bitcast.117, bf16[2,4096,256]{2,1,0:T(8,128)(2,1)} %pair_at.1), custom_call_target="tpu_custom_call" | custom-call | bytes 8388608 | tf_op jit(solution)/shard_map/pair_products/pallas_call | solution.py:331
  45.5 0.0 copy-start.2
  45.5 0.0 copy-start.3
  45.5 0.0 copy-start.8
  45.5 0.0 copy-start.9
  45.5 0.0 copy-start.12
  45.5 5.1 %fusion.32.base_query = f32[32,1024]{1,0:T(8,128)S(1)} fusion(bf16[32,4096]{1,0:T(8,128)(2,1)} %copy-done.1, bf16[4096,1024]{1,0:T(8,128)(2,1)} %param.21), kind=kOutput, calls=%fused_computation.129 | convolution fusion | flops 268435456 | bytes 8781824 | tf_op jit(solution)/shard_map/dot_general | solution.py:604
  50.7 0.0 all-to-all-done.1.rows.factors
  50.7 0.6 %products.1.p0 = f32[40,128]{1,0:T(8,128)S(1)} custom-call(bf16[32,1024]{1,0:T(8,128)(2,1)S(1)} %get-tuple-element.1098.own, bf16[32,8,1024]{2,1,0:T(8,128)(2,1)S(1)} %all-to-all-done.1.rows.factors), custom_call_target="tpu_custom_call" | custom-call | tf_op jit(solution)/shard_map/products/pallas_call | solution.py:424
  51.3 3.6 %collective-permute-start.36 = (f32[40,128]{1,0:T(8,128)S(1)}, f32[40,128]{1,0:T(8,128)S(1)}, u32[]{:S(2)}, u32[]{:S(2)}) collective-permute-start(f32[40,128]{1,0:T(8,128)S(1)} %products.1.p0), channel_id=1, source_target_pairs={{0,3},{1,2},{2,1},{3,0},{4,7},{5,6},{6,5},{7,4},{8,11},{9,10},{10,... | collective-permute-start | bytes 61448 | tf_op jit(solution)/shard_map/ppermute | solution.py:540
  54.9 0.5 collective-permute-start.35
  55.4 0.0 collective-permute-start.34
  55.4 0.0 copy-done.3
  55.4 0.7 %fetch.1 = (bf16[8,128,512]{2,1,0:T(8,128)(2,1)S(1)}, bf16[8,512,128]{2,1,0:T(8,128)(2,1)S(1)}) custom-call(s32[3]{0:T(128)S(1)} %get-tuple-element.2053, bf16[8,128,512]{2,1,0:T(8,128)(2,1)S(1)} %copy-done.2, bf16[8,512,128]{2,1,0:T(8,128)(2,1)S(1)} %copy-done.3), custom_call_target="tpu_custom_call" | custom-call | bytes 4194304 | tf_op jit(solution)/shard_map/fetch/pallas_call | solution.py:359
  56.1 0.2 collective-permute-done.36.p3
  56.4 2.7 %collective-permute-done.35.p2 = f32[40,128]{1,0:T(8,128)S(1)} collective-permute-done((f32[40,128]{1,0:T(8,128)S(1)}, f32[40,128]{1,0:T(8,128)S(1)}, u32[]{:S(2)}, u32[]{:S(2)}) %collective-permute-start.35) | collective-permute-done | bytes 20512 | tf_op jit(solution)/shard_map/ppermute | solution.py:540
  59.0 0.0 collective-permute-done.34.p1
  59.1 2.5 %attend.1 = (bf16[32,1024]{1,0:T(8,128)(2,1)}, f32[2,4096]{1,0:T(2,128)}, f32[2,1024]{1,0:T(2,128)}) custom-call(s32[3]{0:T(128)S(1)} %get-tuple-element.2053, f32[32,1024]{1,0:T(8,128)S(1)} %fusion.32.base_query, f32[40,128]{1,0:T(8,128)S(1)} %products.1.p0, f32[40,128]{1,0:T(8,128)S(1)} %collective-permute-done.34.p1, ...), custom_call_target="tpu_custom_call" | custom-call | tf_op jit(solution)/shard_map/attend/pallas_call | solution.py:520
  (6 shorter events, 0.0 us)
Async XLA Ops:
  0.6 20.5 %copy-start.13 = (s32[4,256]{1,0:T(4,128)S(1)}, s32[4,256]{1,0:T(4,128)}, u32[]{:S(2)}) copy-start(s32[4,256]{1,0:T(4,128)} %tokens_at.1) | copy-start | bytes 12292
  6.0 22.0 %all-to-all-start = ((bf16[32,8,1536]{2,1,0:T(8,128)(2,1)}), bf16[32,8,1536]{2,1,0:T(8,128)(2,1)S(1)}, u32[]{:S(2)}, u32[]{:S(2)}) async-start(bf16[32,8,1536]{2,1,0:T(8,128)(2,1)} %bitcast.116), calls=%async_computation | async-start | bytes 1572864 | tf_op jit(solution)/shard_map/all_to_all | solution.py:571
  21.1 6.8 %copy-start.4 = (f32[2,4096]{1,0:T(2,128)S(1)}, f32[2,4096]{1,0:T(2,128)}, u32[]{:S(2)}) copy-start(f32[2,4096]{1,0:T(2,128)} %old_down.1) | copy-start | bytes 98308
  21.2 6.8 %copy-start.5 = (f32[2,1024]{1,0:T(2,128)S(1)}, f32[2,1024]{1,0:T(2,128)}, u32[]{:S(2)}) copy-start(f32[2,1024]{1,0:T(2,128)} %old_up.1) | copy-start | bytes 24580
  21.2 6.8 %copy-start.6 = (bf16[32,256]{1,0:T(8,128)(2,1)S(1)}, bf16[32,256]{1,0:T(8,128)(2,1)}, u32[]{:S(2)}) copy-start(bf16[32,256]{1,0:T(8,128)(2,1)} %get-tuple-element.1090.pick) | copy-start | bytes 49156
  21.2 6.8 %copy-start.10 = (f32[32]{0:T(128)S(1)}, f32[32]{0:T(128)}, u32[]{:S(2)}) copy-start(f32[32]{0:T(128)} %scale.1) | copy-start | bytes 388
  21.2 6.8 %copy-start.11 = (s32[32]{0:T(128)S(1)}, s32[32]{0:T(128)}, u32[]{:S(2)}) copy-start(s32[32]{0:T(128)} %learner.1) | copy-start | bytes 388
  21.2 19.1 %copy-start.7 = (f32[4096]{0:T(1024)S(1)}, f32[4096]{0:T(1024)}, u32[]{:S(2)}) copy-start(f32[4096]{0:T(1024)} %param.18) | copy-start | bytes 49156
  29.5 9.8 %collective-permute-start.33 = (bf16[48,1024]{1,0:T(8,128)(2,1)S(1)}, bf16[48,1024]{1,0:T(8,128)(2,1)S(1)}, u32[]{:S(2)}, u32[]{:S(2)}) collective-permute-start(bf16[48,1024]{1,0:T(8,128)(2,1)S(1)} %get-tuple-element.1093.e0.s0), channel_id=1, source_target_pairs={{0,3},{1,2},{2,1},{3,0},{4,7},{5,6},{6,5},{7,4},{8,11},{9,10},{10,... | collective-permute-start | bytes 294920 | tf_op jit(solution)/shard_map/ppermute | solution.py:540
  34.9 5.5 %collective-permute-start.32 = (bf16[48,1024]{1,0:T(8,128)(2,1)S(1)}, bf16[48,1024]{1,0:T(8,128)(2,1)S(1)}, u32[]{:S(2)}, u32[]{:S(2)}) collective-permute-start(bf16[48,1024]{1,0:T(8,128)(2,1)S(1)} %get-tuple-element.1093.e0.s0), channel_id=1, source_target_pairs={{0,2},{1,3},{2,0},{3,1},{4,6},{5,7},{6,4},{7,5},{8,10},{9,11},{10,... | collective-permute-start | bytes 294920 | tf_op jit(solution)/shard_map/ppermute | solution.py:540
  35.4 4.9 %collective-permute-start.31 = (bf16[48,1024]{1,0:T(8,128)(2,1)S(1)}, bf16[48,1024]{1,0:T(8,128)(2,1)S(1)}, u32[]{:S(2)}, u32[]{:S(2)}) collective-permute-start(bf16[48,1024]{1,0:T(8,128)(2,1)S(1)} %get-tuple-element.1093.e0.s0), channel_id=1, source_target_pairs={{0,1},{1,0},{2,3},{3,2},{4,5},{5,4},{6,7},{7,6},{8,9},{9,8},{10,11... | collective-permute-start | bytes 294920 | tf_op jit(solution)/shard_map/ppermute | solution.py:540
  35.4 15.3 %all-to-all-start.1 = ((bf16[32,8,1024]{2,1,0:T(8,128)(2,1)}), bf16[32,8,1024]{2,1,0:T(8,128)(2,1)S(1)}, u32[]{:S(2)}, u32[]{:S(2)}) async-start(bf16[32,8,1024]{2,1,0:T(8,128)(2,1)} %get-tuple-element.1099), calls=%async_computation.1 | async-start | bytes 1048576 | tf_op jit(solution)/shard_map/all_to_all | solution.py:598
  41.1 0.7 %copy-start.1 = (bf16[32,4096]{1,0:T(8,128)(2,1)}, bf16[32,4096]{1,0:T(8,128)(2,1)S(1)}, u32[]{:S(2)}) copy-start(bf16[32,4096]{1,0:T(8,128)(2,1)S(1)} %get-tuple-element.1095.normed) | copy-start | bytes 786436
  45.5 9.9 %copy-start.2 = (bf16[8,128,512]{2,1,0:T(8,128)(2,1)S(1)}, bf16[8,128,512]{2,1,0:T(8,128)(2,1)}, u32[]{:S(2)}) copy-start(bf16[8,128,512]{2,1,0:T(8,128)(2,1)} %get-tuple-element.1104.keys_at) | copy-start | bytes 3145732
  45.5 9.9 %copy-start.3 = (bf16[8,512,128]{2,1,0:T(8,128)(2,1)S(1)}, bf16[8,512,128]{2,1,0:T(8,128)(2,1)}, u32[]{:S(2)}) copy-start(bf16[8,512,128]{2,1,0:T(8,128)(2,1)} %get-tuple-element.1105.values_at) | copy-start | bytes 3145732
  45.5 13.5 %copy-start.8 = (bf16[32,128]{1,0:T(8,128)(2,1)S(1)}, bf16[32,128]{1,0:T(8,128)(2,1)}, u32[]{:S(2)}) copy-start(bf16[32,128]{1,0:T(8,128)(2,1)} %get-tuple-element.1100.key_new) | copy-start | bytes 24580
  45.5 13.5 %copy-start.9 = (bf16[32,128]{1,0:T(8,128)(2,1)S(1)}, bf16[32,128]{1,0:T(8,128)(2,1)}, u32[]{:S(2)}) copy-start(bf16[32,128]{1,0:T(8,128)(2,1)} %get-tuple-element.1101.value_new) | copy-start | bytes 24580
  45.5 13.5 %copy-start.12 = (f32[128]{0:T(128)S(1)}, f32[128]{0:T(128)}, u32[]{:S(2)}) copy-start(f32[128]{0:T(128)} %param.19) | copy-start | bytes 1540
  51.3 5.0 %collective-permute-start.36 = (f32[40,128]{1,0:T(8,128)S(1)}, f32[40,128]{1,0:T(8,128)S(1)}, u32[]{:S(2)}, u32[]{:S(2)}) collective-permute-start(f32[40,128]{1,0:T(8,128)S(1)} %products.1.p0), channel_id=1, source_target_pairs={{0,3},{1,2},{2,1},{3,0},{4,7},{5,6},{6,5},{7,4},{8,11},{9,10},{10,... | collective-permute-start | bytes 61448 | tf_op jit(solution)/shard_map/ppermute | solution.py:540
  54.9 4.1 %collective-permute-start.35 = (f32[40,128]{1,0:T(8,128)S(1)}, f32[40,128]{1,0:T(8,128)S(1)}, u32[]{:S(2)}, u32[]{:S(2)}) collective-permute-start(f32[40,128]{1,0:T(8,128)S(1)} %products.1.p0), channel_id=1, source_target_pairs={{0,2},{1,3},{2,0},{3,1},{4,6},{5,7},{6,4},{7,5},{8,10},{9,11},{10,... | collective-permute-start | bytes 61448 | tf_op jit(solution)/shard_map/ppermute | solution.py:540
  55.4 3.6 %collective-permute-start.34 = (f32[40,128]{1,0:T(8,128)S(1)}, f32[40,128]{1,0:T(8,128)S(1)}, u32[]{:S(2)}, u32[]{:S(2)}) collective-permute-start(f32[40,128]{1,0:T(8,128)S(1)} %products.1.p0), channel_id=1, source_target_pairs={{0,1},{1,0},{2,3},{3,2},{4,5},{5,4},{6,7},{7,6},{8,9},{9,8},{10,11... | collective-permute-start | bytes 61448 | tf_op jit(solution)/shard_map/ppermute | solution.py:540

commit v6 on v5

--- a/solution.py
+++ b/solution.py
@@ -281,8 +281,9 @@
     for i in range(rows):
         copies[i].wait()
         wide[...] = cache[i].astype(jnp.float32)
-        keys[i] = wide[pl.ds(place[1], count, stride=4), :].T.astype(jnp.bfloat16)
-        values[i] = wide[pl.ds(place[1] + 2, count, stride=4), :].astype(jnp.bfloat16)
+        parts = [wide[pl.ds(j, count, stride=4), :] for j in range(4)]
+        keys[i] = jnp.where(place[1] == 0, parts[0], parts[1]).T.astype(jnp.bfloat16)
+        values[i] = jnp.where(place[1] == 0, parts[2], parts[3]).astype(jnp.bfloat16)
         back.append(pltpu.make_async_copy(keys.at[i], keys_at.at[i], sems.at[rows + 2 * i]))
         back.append(pltpu.make_async_copy(values.at[i], values_at.at[i], sems.at[rows + 2 * i + 1]))
         back[-2].start()
@@ -362,7 +363,7 @@
         in_specs=[smem()] + [pl.BlockSpec(memory_space=pl.ANY)] * 2,
         out_specs=[vmem(), vmem()],
         scratch_shapes=[pltpu.SemaphoreType.DMA((2,))],
-        compiler_params=params(1),
+        compiler_params=params(8),
         cost_estimate=pl.CostEstimate(flops=0, bytes_accessed=2**22, transcendentals=0),
         name="fetch",
     )(place, keys, values)

time: 62 us -> 62 us (level)
  no operation moved by 1% of the time
where the time goes in v6:
time: 62 us; the launch traced here: 61.6 us
  starting transfers between devices  23.7 us (38%)
  Pallas kernels  19.1 us (31%)
  waiting for transfers between devices  9.63 us (16%)
  matrix products  5.14 us (8%)
  between operations  2.28 us (4%)
  loops' own time  0.88 us (1%)
  local copies, waits for them, and re-layouts  0.76 us (1%)
    ppermute x6, starting transfers between devices, tensor_swap(): return lax.ppermute(values, 'tensor', [(i, i ^ bit) for i in range(size)])  9.96 us
    all_to_all x1, starting transfers between devices, body(): got = lax.all_to_all(sent.reshape(groups, CAP, -1), 'dp', 0, 0, tiled=True)  9.82 us
    all_to_all x1, waiting for transfers between devices, body(): got = lax.all_to_all(sent.reshape(groups, CAP, -1), 'dp', 0, 0, tiled=True)  5.75 us
    pallas_call x1, Pallas kernels, send(): pl.pallas_call(send_kernel, out_shape=(jax.ShapeDtypeStruct((groups * CAP...  5.23 us
    dot_general x1, matrix products, body(): jnp.dot(normed, base_query_weight, preferred_element_type=jnp.float32)  5.14 us
    pallas_call x1, Pallas kernels, stage(): pl.pallas_call(stage_kernel, out_shape=[keys, values], in_specs=[smem(),...  4.03 us
    all_to_all x1, starting transfers between devices, body(): rows = lax.all_to_all(sums, 'dp', 0, 0, tiled=True)  3.94 us
    ppermute x6, waiting for transfers between devices, tensor_swap(): return lax.ppermute(values, 'tensor', [(i, i ^ bit) for i in range(size)])  3.88 us
  transfers between devices with their start and end apart: 8, of which 4 were waited for; matrix products, arithmetic and copies ran while one was open for 8% of the time, Pallas kernels for 15%

profile of v6, /device:TPU:1, one launch (start us, length us, event | category | flops | bytes accessed | tf_op | source)
XLA Modules:
  0.0 61.6 jit_solution(13756390961300713881)
XLA Ops:
  0.6 0.0 copy-start.13
  0.7 0.1 pad_add_fusion.place
  0.7 5.2 %send.1 = (bf16[256,1536]{1,0:T(8,128)(2,1)}, bf16[32,256]{1,0:T(8,128)(2,1)}, s32[1]{0:T(128)}) custom-call(s32[3]{0:T(128)S(1)} %pad_add_fusion.place, s32[4,256]{1,0:T(4,128)} %tokens_at.1, bf16[2374,1024]{1,0:T(8,128)(2,1)} %table_at.1, bf16[1,64,4096]{2,1,0:T(8,128)(2,1)} %grad_down_at.1, bf16[1,64,1024]{2,1,0:T(8,128)(2,1)} %grad_up_at.1), custom_call_target="tpu_custom_call" | custom-call | tf_op jit(solution)/shard_map/send/pallas_call | solution.py:191
  6.0 9.8 %all-to-all-start = ((bf16[32,8,1536]{2,1,0:T(8,128)(2,1)}), bf16[32,8,1536]{2,1,0:T(8,128)(2,1)S(1)}, u32[]{:S(2)}, u32[]{:S(2)}) async-start(bf16[32,8,1536]{2,1,0:T(8,128)(2,1)} %bitcast.116), calls=%async_computation | async-start | bytes 1572864 | tf_op jit(solution)/shard_map/all_to_all | solution.py:572
  16.8 4.0 %stage.1 = (bf16[8,128,512]{2,1,0:T(8,128)(2,1)}, bf16[8,512,128]{2,1,0:T(8,128)(2,1)}) custom-call(s32[3]{0:T(128)S(1)} %pad_add_fusion.place, bf16[8,2048,128]{2,1,0:T(8,128)(2,1)} %bitcast.115), custom_call_target="tpu_custom_call" | custom-call | bytes 8388608 | tf_op jit(solution)/shard_map/stage/pallas_call | solution.py:301
  21.2 0.0 copy-done.13
  21.3 0.0 copy-start.4
  21.3 0.0 copy-start.5
  21.3 0.0 copy-start.6
  21.3 0.0 copy-start.10
  21.3 0.0 copy-start.11
  21.3 0.0 copy-start.7
  21.3 0.9 %while.12 = (s32[]{:T(128)}, bf16[32,1024]{1,0:T(8,128)(2,1)S(1)}, s32[1]{0:T(128)}, s32[3]{0:T(128)S(1)}, s32[4,256]{1,0:T(4,128)S(1)}, /*index=5*/bf16[2374,10...) while((s32[]{:T(128)}, bf16[32,1024]{1,0:T(8,128)(2,1)S(1)}, ...), condition=%wide.region_1.2_spmd, body=%wide.region_0.1_spmd.sunk | while | flops 18874372 | bytes 8112585 | solution.py:587
  22.2 5.7 %all-to-all-done.got = bf16[32,8,1536]{2,1,0:T(8,128)(2,1)S(1)} async-done(((bf16[32,8,1536]{2,1,0:T(8,128)(2,1)}), bf16[32,8,1536]{2,1,0:T(8,128)(2,1)S(1)}, u32[]{:S(2)}, u32[]{:S(2)}) %all-to-all-start) | async-done | bytes 786464 | tf_op jit(solution)/shard_map/all_to_all | solution.py:572
  28.0 0.0 copy-done.4
  28.0 0.0 copy-done.5
  28.0 0.0 copy-done.6
  28.0 0.0 copy-done.10
  28.0 0.0 copy-done.11
  28.0 1.5 %gather.1 = (bf16[48,1024]{1,0:T(8,128)(2,1)S(1)}, f32[8,512]{1,0:T(8,128)S(1)}, bf16[32,8,1024]{2,1,0:T(8,128)(2,1)}) custom-call(s32[3]{0:T(128)S(1)} %get-tuple-element.2053, f32[32]{0:T(128)S(1)} %copy-done.10, s32[32]{0:T(128)S(1)} %copy-done.11, bf16[32,8,1536]{2,1,0:T(8,128)(2,1)S(1)} %all-to-all-done.got, bf16[32,256]{1,0:T(8,128)(2,1)S(1)} %copy-done.6, ...), custom_call_target="tpu_custom_call" | custom-call | tf_op jit(solution)/shard_map/gather/pallas_call | solution.py:261
  29.5 5.4 %collective-permute-start.33 = (bf16[48,1024]{1,0:T(8,128)(2,1)S(1)}, bf16[48,1024]{1,0:T(8,128)(2,1)S(1)}, u32[]{:S(2)}, u32[]{:S(2)}) collective-permute-start(bf16[48,1024]{1,0:T(8,128)(2,1)S(1)} %get-tuple-element.1093.e0.s0), channel_id=1, source_target_pairs={{0,3},{1,2},{2,1},{3,0},{4,7},{5,6},{6,5},{7,4},{8,11},{9,10},{10,... | collective-permute-start | bytes 294920 | tf_op jit(solution)/shard_map/ppermute | solution.py:541
  34.9 0.5 collective-permute-start.32
  35.4 0.0 collective-permute-start.31
  35.4 3.9 %all-to-all-start.1 = ((bf16[32,8,1024]{2,1,0:T(8,128)(2,1)}), bf16[32,8,1024]{2,1,0:T(8,128)(2,1)S(1)}, u32[]{:S(2)}, u32[]{:S(2)}) async-start(bf16[32,8,1024]{2,1,0:T(8,128)(2,1)} %get-tuple-element.1099), calls=%async_computation.1 | async-start | bytes 1048576 | tf_op jit(solution)/shard_map/all_to_all | solution.py:599
  39.4 0.0 collective-permute-done.33.e3.s3
  39.4 1.0 %collective-permute-done.32.e2.s2 = bf16[48,1024]{1,0:T(8,128)(2,1)S(1)} collective-permute-done((bf16[48,1024]{1,0:T(8,128)(2,1)S(1)}, bf16[48,1024]{1,0:T(8,128)(2,1)S(1)}, u32[]{:S(2)}, u32[]{:S(2)}) %collective-permute-start.32) | collective-permute-done | bytes 98336 | tf_op jit(solution)/shard_map/ppermute | solution.py:541
  40.3 0.0 collective-permute-done.31.e1.s1
  40.3 0.0 copy-done.7
  40.3 0.7 %norm.1 = (bf16[32,4096]{1,0:T(8,128)(2,1)S(1)}, bf16[32,1024]{1,0:T(8,128)(2,1)S(1)}) custom-call(s32[3]{0:T(128)S(1)} %get-tuple-element.2053, bf16[48,1024]{1,0:T(8,128)(2,1)S(1)} %get-tuple-element.1093.e0.s0, bf16[48,1024]{1,0:T(8,128)(2,1)S(1)} %collective-permute-done.31.e1.s1, bf16[48,1024]{1,0:T(8,128)(2,1)S(1)} %collective-permute-done.32.e2.s2, ...), custom_call_target="tpu_custom_call" | custom-call | tf_op jit(solution)/shard_map/norm/pallas_call | solution.py:388
  41.1 0.7 %copy-done.1 = bf16[32,4096]{1,0:T(8,128)(2,1)} copy-done((bf16[32,4096]{1,0:T(8,128)(2,1)}, bf16[32,4096]{1,0:T(8,128)(2,1)S(1)}, u32[]{:S(2)}) %copy-start.1) | copy-done | bytes 262168
  41.8 3.7 %pair_products.1 = (bf16[32,128]{1,0:T(8,128)(2,1)}, bf16[32,128]{1,0:T(8,128)(2,1)}) custom-call(s32[3]{0:T(128)S(1)} %get-tuple-element.2053, bf16[32,4096]{1,0:T(8,128)(2,1)} %copy-done.1, f32[1,128]{1,0:T(1,128)} %bitcast.117, bf16[2,4096,256]{2,1,0:T(8,128)(2,1)} %pair_at.1), custom_call_target="tpu_custom_call" | custom-call | bytes 8388608 | tf_op jit(solution)/shard_map/pair_products/pallas_call | solution.py:332
  45.5 0.0 copy-start.2
  45.5 0.0 copy-start.3
  45.5 0.0 copy-start.8
  45.5 0.0 copy-start.9
  45.5 0.0 copy-start.12
  45.5 5.1 %fusion.32.base_query = f32[32,1024]{1,0:T(8,128)S(1)} fusion(bf16[32,4096]{1,0:T(8,128)(2,1)} %copy-done.1, bf16[4096,1024]{1,0:T(8,128)(2,1)} %param.21), kind=kOutput, calls=%fused_computation.129 | convolution fusion | flops 268435456 | bytes 8781824 | tf_op jit(solution)/shard_map/dot_general | solution.py:605
  50.7 0.0 all-to-all-done.1.rows.factors
  50.7 0.6 %products.1.p0 = f32[40,128]{1,0:T(8,128)S(1)} custom-call(bf16[32,1024]{1,0:T(8,128)(2,1)S(1)} %get-tuple-element.1098.own, bf16[32,8,1024]{2,1,0:T(8,128)(2,1)S(1)} %all-to-all-done.1.rows.factors), custom_call_target="tpu_custom_call" | custom-call | tf_op jit(solution)/shard_map/products/pallas_call | solution.py:425
  51.3 3.6 %collective-permute-start.36 = (f32[40,128]{1,0:T(8,128)S(1)}, f32[40,128]{1,0:T(8,128)S(1)}, u32[]{:S(2)}, u32[]{:S(2)}) collective-permute-start(f32[40,128]{1,0:T(8,128)S(1)} %products.1.p0), channel_id=1, source_target_pairs={{0,3},{1,2},{2,1},{3,0},{4,7},{5,6},{6,5},{7,4},{8,11},{9,10},{10,... | collective-permute-start | bytes 61448 | tf_op jit(solution)/shard_map/ppermute | solution.py:541
  54.9 0.5 collective-permute-start.35
  55.4 0.0 collective-permute-start.34
  55.4 0.0 copy-done.3
  55.4 0.7 %fetch.1 = (bf16[8,128,512]{2,1,0:T(8,128)(2,1)S(1)}, bf16[8,512,128]{2,1,0:T(8,128)(2,1)S(1)}) custom-call(s32[3]{0:T(128)S(1)} %get-tuple-element.2053, bf16[8,128,512]{2,1,0:T(8,128)(2,1)S(1)} %copy-done.2, bf16[8,512,128]{2,1,0:T(8,128)(2,1)S(1)} %copy-done.3), custom_call_target="tpu_custom_call" | custom-call | bytes 4194304 | tf_op jit(solution)/shard_map/fetch/pallas_call | solution.py:360
  56.1 0.2 collective-permute-done.36.p3
  56.4 2.7 %collective-permute-done.35.p2 = f32[40,128]{1,0:T(8,128)S(1)} collective-permute-done((f32[40,128]{1,0:T(8,128)S(1)}, f32[40,128]{1,0:T(8,128)S(1)}, u32[]{:S(2)}, u32[]{:S(2)}) %collective-permute-start.35) | collective-permute-done | bytes 20512 | tf_op jit(solution)/shard_map/ppermute | solution.py:541
  59.0 0.0 collective-permute-done.34.p1
  59.1 2.5 %attend.1 = (bf16[32,1024]{1,0:T(8,128)(2,1)}, f32[2,4096]{1,0:T(2,128)}, f32[2,1024]{1,0:T(2,128)}) custom-call(s32[3]{0:T(128)S(1)} %get-tuple-element.2053, f32[32,1024]{1,0:T(8,128)S(1)} %fusion.32.base_query, f32[40,128]{1,0:T(8,128)S(1)} %products.1.p0, f32[40,128]{1,0:T(8,128)S(1)} %collective-permute-done.34.p1, ...), custom_call_target="tpu_custom_call" | custom-call | tf_op jit(solution)/shard_map/attend/pallas_call | solution.py:521
  (6 shorter events, 0.0 us)
Async XLA Ops:
  0.6 20.6 %copy-start.13 = (s32[4,256]{1,0:T(4,128)S(1)}, s32[4,256]{1,0:T(4,128)}, u32[]{:S(2)}) copy-start(s32[4,256]{1,0:T(4,128)} %tokens_at.1) | copy-start | bytes 12292
  6.0 22.0 %all-to-all-start = ((bf16[32,8,1536]{2,1,0:T(8,128)(2,1)}), bf16[32,8,1536]{2,1,0:T(8,128)(2,1)S(1)}, u32[]{:S(2)}, u32[]{:S(2)}) async-start(bf16[32,8,1536]{2,1,0:T(8,128)(2,1)} %bitcast.116), calls=%async_computation | async-start | bytes 1572864 | tf_op jit(solution)/shard_map/all_to_all | solution.py:572
  21.3 6.7 %copy-start.4 = (f32[2,4096]{1,0:T(2,128)S(1)}, f32[2,4096]{1,0:T(2,128)}, u32[]{:S(2)}) copy-start(f32[2,4096]{1,0:T(2,128)} %old_down.1) | copy-start | bytes 98308
  21.3 6.7 %copy-start.5 = (f32[2,1024]{1,0:T(2,128)S(1)}, f32[2,1024]{1,0:T(2,128)}, u32[]{:S(2)}) copy-start(f32[2,1024]{1,0:T(2,128)} %old_up.1) | copy-start | bytes 24580
  21.3 6.7 %copy-start.6 = (bf16[32,256]{1,0:T(8,128)(2,1)S(1)}, bf16[32,256]{1,0:T(8,128)(2,1)}, u32[]{:S(2)}) copy-start(bf16[32,256]{1,0:T(8,128)(2,1)} %get-tuple-element.1090.pick) | copy-start | bytes 49156
  21.3 6.7 %copy-start.10 = (f32[32]{0:T(128)S(1)}, f32[32]{0:T(128)}, u32[]{:S(2)}) copy-start(f32[32]{0:T(128)} %scale.1) | copy-start | bytes 388
  21.3 6.7 %copy-start.11 = (s32[32]{0:T(128)S(1)}, s32[32]{0:T(128)}, u32[]{:S(2)}) copy-start(s32[32]{0:T(128)} %learner.1) | copy-start | bytes 388
  21.3 19.0 %copy-start.7 = (f32[4096]{0:T(1024)S(1)}, f32[4096]{0:T(1024)}, u32[]{:S(2)}) copy-start(f32[4096]{0:T(1024)} %param.18) | copy-start | bytes 49156
  29.5 9.8 %collective-permute-start.33 = (bf16[48,1024]{1,0:T(8,128)(2,1)S(1)}, bf16[48,1024]{1,0:T(8,128)(2,1)S(1)}, u32[]{:S(2)}, u32[]{:S(2)}) collective-permute-start(bf16[48,1024]{1,0:T(8,128)(2,1)S(1)} %get-tuple-element.1093.e0.s0), channel_id=1, source_target_pairs={{0,3},{1,2},{2,1},{3,0},{4,7},{5,6},{6,5},{7,4},{8,11},{9,10},{10,... | collective-permute-start | bytes 294920 | tf_op jit(solution)/shard_map/ppermute | solution.py:541
  34.9 5.5 %collective-permute-start.32 = (bf16[48,1024]{1,0:T(8,128)(2,1)S(1)}, bf16[48,1024]{1,0:T(8,128)(2,1)S(1)}, u32[]{:S(2)}, u32[]{:S(2)}) collective-permute-start(bf16[48,1024]{1,0:T(8,128)(2,1)S(1)} %get-tuple-element.1093.e0.s0), channel_id=1, source_target_pairs={{0,2},{1,3},{2,0},{3,1},{4,6},{5,7},{6,4},{7,5},{8,10},{9,11},{10,... | collective-permute-start | bytes 294920 | tf_op jit(solution)/shard_map/ppermute | solution.py:541
  35.4 4.9 %collective-permute-start.31 = (bf16[48,1024]{1,0:T(8,128)(2,1)S(1)}, bf16[48,1024]{1,0:T(8,128)(2,1)S(1)}, u32[]{:S(2)}, u32[]{:S(2)}) collective-permute-start(bf16[48,1024]{1,0:T(8,128)(2,1)S(1)} %get-tuple-element.1093.e0.s0), channel_id=1, source_target_pairs={{0,1},{1,0},{2,3},{3,2},{4,5},{5,4},{6,7},{7,6},{8,9},{9,8},{10,11... | collective-permute-start | bytes 294920 | tf_op jit(solution)/shard_map/ppermute | solution.py:541
  35.4 15.3 %all-to-all-start.1 = ((bf16[32,8,1024]{2,1,0:T(8,128)(2,1)}), bf16[32,8,1024]{2,1,0:T(8,128)(2,1)S(1)}, u32[]{:S(2)}, u32[]{:S(2)}) async-start(bf16[32,8,1024]{2,1,0:T(8,128)(2,1)} %get-tuple-element.1099), calls=%async_computation.1 | async-start | bytes 1048576 | tf_op jit(solution)/shard_map/all_to_all | solution.py:599
  41.1 0.7 %copy-start.1 = (bf16[32,4096]{1,0:T(8,128)(2,1)}, bf16[32,4096]{1,0:T(8,128)(2,1)S(1)}, u32[]{:S(2)}) copy-start(bf16[32,4096]{1,0:T(8,128)(2,1)S(1)} %get-tuple-element.1095.normed) | copy-start | bytes 786436
  45.5 9.9 %copy-start.2 = (bf16[8,128,512]{2,1,0:T(8,128)(2,1)S(1)}, bf16[8,128,512]{2,1,0:T(8,128)(2,1)}, u32[]{:S(2)}) copy-start(bf16[8,128,512]{2,1,0:T(8,128)(2,1)} %get-tuple-element.1104.keys_at) | copy-start | bytes 3145732
  45.5 9.9 %copy-start.3 = (bf16[8,512,128]{2,1,0:T(8,128)(2,1)S(1)}, bf16[8,512,128]{2,1,0:T(8,128)(2,1)}, u32[]{:S(2)}) copy-start(bf16[8,512,128]{2,1,0:T(8,128)(2,1)} %get-tuple-element.1105.values_at) | copy-start | bytes 3145732
  45.5 13.5 %copy-start.8 = (bf16[32,128]{1,0:T(8,128)(2,1)S(1)}, bf16[32,128]{1,0:T(8,128)(2,1)}, u32[]{:S(2)}) copy-start(bf16[32,128]{1,0:T(8,128)(2,1)} %get-tuple-element.1100.key_new) | copy-start | bytes 24580
  45.5 13.5 %copy-start.9 = (bf16[32,128]{1,0:T(8,128)(2,1)S(1)}, bf16[32,128]{1,0:T(8,128)(2,1)}, u32[]{:S(2)}) copy-start(bf16[32,128]{1,0:T(8,128)(2,1)} %get-tuple-element.1101.value_new) | copy-start | bytes 24580
  45.5 13.5 %copy-start.12 = (f32[128]{0:T(128)S(1)}, f32[128]{0:T(128)}, u32[]{:S(2)}) copy-start(f32[128]{0:T(128)} %param.19) | copy-start | bytes 1540
  51.3 5.0 %collective-permute-start.36 = (f32[40,128]{1,0:T(8,128)S(1)}, f32[40,128]{1,0:T(8,128)S(1)}, u32[]{:S(2)}, u32[]{:S(2)}) collective-permute-start(f32[40,128]{1,0:T(8,128)S(1)} %products.1.p0), channel_id=1, source_target_pairs={{0,3},{1,2},{2,1},{3,0},{4,7},{5,6},{6,5},{7,4},{8,11},{9,10},{10,... | collective-permute-start | bytes 61448 | tf_op jit(solution)/shard_map/ppermute | solution.py:541
  54.9 4.1 %collective-permute-start.35 = (f32[40,128]{1,0:T(8,128)S(1)}, f32[40,128]{1,0:T(8,128)S(1)}, u32[]{:S(2)}, u32[]{:S(2)}) collective-permute-start(f32[40,128]{1,0:T(8,128)S(1)} %products.1.p0), channel_id=1, source_target_pairs={{0,2},{1,3},{2,0},{3,1},{4,6},{5,7},{6,4},{7,5},{8,10},{9,11},{10,... | collective-permute-start | bytes 61448 | tf_op jit(solution)/shard_map/ppermute | solution.py:541
  55.4 3.6 %collective-permute-start.34 = (f32[40,128]{1,0:T(8,128)S(1)}, f32[40,128]{1,0:T(8,128)S(1)}, u32[]{:S(2)}, u32[]{:S(2)}) collective-permute-start(f32[40,128]{1,0:T(8,128)S(1)} %products.1.p0), channel_id=1, source_target_pairs={{0,1},{1,0},{2,3},{3,2},{4,5},{5,4},{6,7},{7,6},{8,9},{9,8},{10,11... | collective-permute-start | bytes 61448 | tf_op jit(solution)/shard_map/ppermute | solution.py:541
